TPU v7x, 32 devices: a whole 2x2x4 slice. The times are simulated.
32 devices in a mesh: cpi: 2 (over x), elem: 16 (over z, y, core).
Axes of the slice: x: 2, y: 2, z: 4, core: 2. Of those that a mesh axis runs over, the one named last changes fastest.
Arguments:
- raw_echo: bfloat16 [256, 2, 128, 3072], P(('cpi', 'elem')), parts along dimension 0, may hold values from -6 to 6
- beam_weights: bfloat16 [8, 2, 128], replicated, may hold values from -0.375 to 0.375
- steer: float32 [2, 24], replicated, may hold values from -4 to 4
- train_mask: int32 [256, 3072], P(('cpi', 'elem')), parts along dimension 0, may hold values 0 or 1
Outputs:
- filtered: float32 [256, 2, 3072], P(('cpi', 'elem')), parts along dimension 0
There are 2 independent parts, one for each index of `cpi`. A program takes and returns all parts, laid end to end along the dimension named above; an argument that names none is the same for every part. Nothing has to cross between parts.
All inputs are finite; a program needn't handle non-finite values. No bound on the sum of `train_mask` on one device may be relied on, other than what follows from the above.
Results may differ from a plain program's by a relative error of at most 0.0044.
Values may be sent and summed in bfloat16 or wider, within the bound.
No kernel may reach another device: no remote copies, remote signals or barrier semaphores. Data moves between devices by JAX's collectives and lax.ppermute only.
A program may use at most 128 MiB of HBM per device.

v0:
```python
import math

import jax
import jax.numpy as jnp
from jax import lax
from jax.sharding import PartitionSpec as P

LOADING = 1.0


def padded_2(cells, sides, width):
    for axis, dim in sides:
        count = lax.axis_size(axis)
        head = lax.slice_in_dim(cells, 0, width, axis=dim)
        tail = lax.slice_in_dim(cells, cells.shape[dim] - width, cells.shape[dim], axis=dim)
        cells = jnp.concatenate(
            [
                lax.ppermute(tail, axis, [(i, (i + 1) % count) for i in range(count)]),
                cells,
                lax.ppermute(head, axis, [((i + 1) % count, i) for i in range(count)]),
            ],
            axis=dim,
        )
    return cells


def doppler_table(pulses):
    doppler_index = jnp.arange(pulses, dtype=jnp.int32)
    phase = doppler_index[:, None] * doppler_index[None, :] % pulses
    angles = -2.0 * math.pi / pulses * phase.astype(jnp.float32)
    cosine = jnp.cos(angles) / math.sqrt(pulses)
    sine_part = jnp.sin(angles) / math.sqrt(pulses)
    real_row = jnp.concatenate([cosine, -sine_part], axis=1)
    imag_row = jnp.concatenate([sine_part, cosine], axis=1)
    return jnp.stack([real_row, imag_row], axis=1).astype(jnp.bfloat16)


def beam_matrix(beam_weights):
    beam_count = beam_weights.shape[0]
    elem_count = beam_weights.shape[2]
    weight_re = beam_weights[:, 0, :]
    weight_im = beam_weights[:, 1, :]
    real_row = jnp.stack([weight_re, -weight_im], axis=2).reshape(beam_count, 2 * elem_count)
    imag_row = jnp.stack([weight_im, weight_re], axis=2).reshape(beam_count, 2 * elem_count)
    return jnp.concatenate([real_row, imag_row], axis=0)


def adapt(window, train_mask, steer):
    bins_here = window.shape[0]
    gate_count = window.shape[-1]
    beam_count = window.shape[2] // 2
    stacked = window.reshape(bins_here, 3, 2, beam_count, gate_count).transpose(0, 2, 1, 3, 4)
    stacked = stacked.reshape(bins_here, 6 * beam_count, gate_count)
    picked = stacked * train_mask[:, None, :].astype(jnp.float32)
    gram_sums = jnp.einsum("nig,njg->nij", picked, stacked, precision=lax.Precision.HIGHEST)
    half_dim = 3 * beam_count
    upper_left = gram_sums[:, :half_dim, :half_dim]
    upper_right = gram_sums[:, :half_dim, half_dim:]
    lower_left = gram_sums[:, half_dim:, :half_dim]
    lower_right = gram_sums[:, half_dim:, half_dim:]
    identity = jnp.eye(half_dim, dtype=jnp.float32)
    real_part = upper_left + lower_right + LOADING * identity[None]
    imag_part = lower_left - upper_right
    system = jnp.concatenate(
        [
            jnp.concatenate([real_part, -imag_part], axis=2),
            jnp.concatenate([imag_part, real_part], axis=2),
        ],
        axis=1,
    )
    target = steer.reshape(-1)
    factor = jnp.linalg.cholesky(system)
    solved = jax.vmap(lambda factor_one: jax.scipy.linalg.cho_solve((factor_one, True), target))(
        factor
    )
    response = jnp.sum(solved * target[None, :], axis=1)
    weight = solved / response[:, None]
    weight_re = weight[:, :half_dim]
    weight_im = weight[:, half_dim:]
    snap_re = stacked[:, :half_dim]
    snap_im = stacked[:, half_dim:]
    highest = lax.Precision.HIGHEST
    output_re = jnp.einsum("ni,nig->ng", weight_re, snap_re, precision=highest) + jnp.einsum(
        "ni,nig->ng", weight_im, snap_im, precision=highest
    )
    output_im = jnp.einsum("ni,nig->ng", weight_re, snap_im, precision=highest) - jnp.einsum(
        "ni,nig->ng", weight_im, snap_re, precision=highest
    )
    return jnp.stack([output_re, output_im], axis=1)


def local(raw_echo, beam_weights, steer, train_mask):
    elem_dev = raw_echo.shape[0]
    pulses = raw_echo.shape[2]
    gate_count = raw_echo.shape[3]
    dft_table = doppler_table(pulses)
    matrix = beam_matrix(beam_weights)
    echo_rows = raw_echo.reshape(elem_dev, 2 * pulses, gate_count)
    dop_dev = pulses // lax.axis_size("elem")
    columns = lax.dynamic_slice_in_dim(
        matrix, lax.axis_index("elem") * (2 * elem_dev), 2 * elem_dev, 1
    )
    spectra_rows = jnp.einsum(
        "dcr,erg->decg", dft_table, echo_rows, preferred_element_type=jnp.float32
    ).astype(jnp.bfloat16)
    spectra_rows = spectra_rows.reshape(dop_dev * lax.axis_size("elem"), 2 * elem_dev, gate_count)
    beam_rows = lax.psum_scatter(
        jnp.einsum("ok,dkg->dog", columns, spectra_rows, preferred_element_type=jnp.float32),
        "elem",
        scatter_dimension=0,
        tiled=True,
    )
    padded = padded_2(beam_rows, (("elem", 0),), 1)
    window = jnp.stack([padded[:-2], padded[1:-1], padded[2:]], axis=1)
    return adapt(window, train_mask, steer)


def solution(mesh):
    return jax.shard_map(
        local,
        mesh=mesh,
        in_specs=(P(("cpi", "elem"), None, None, None), P(), P(), P(("cpi", "elem"), None)),
        out_specs=P(("cpi", "elem"), None, None),
        check_vma=False,
    )
```

profile of v0, /device:TPU:0, one launch (start us, length us, event | category | flops | bytes accessed | tf_op | source)
XLA Modules:
  0.0 403.8 jit_solution(5125254393638696238)
XLA Ops:
  6.5 0.0 reduce-scatter.2.cloned.1.call-start
  6.5 0.3 negate_convert_fusion
  6.8 0.3 fusion.33
  7.1 10.9 %convert_bitcast_fusion = bf16[128,8,2,3072]{3,0,1,2:T(8,128)(2,1)} fusion(bf16[8,256,3072,1]{2,1,0,3:T(8,128)(2,1)} %bitcast.92, bf16[128,1,256]{2,0,1:T(8,128)(2,1)S(1)} %get-tuple-element.15, bf16[128,1,256]{2,0,1:T(8,128)(2,1)S(1)} %get-tuple-element.14), kind=kOutput, calls=%fused_computation.2 | convolution fusion | flops 3227779072 | bytes 25296896 | tf_op jit(solution)/shard_map/dcr,erg->decg/dot_general | solution.py:103
  18.0 0.0 copy-start.4
  18.0 10.6 %copy.29 = bf16[128,8,2,3072]{3,0,2,1:T(8,128)(2,1)} copy(bf16[128,8,2,3072]{3,0,1,2:T(8,128)(2,1)} %convert_bitcast_fusion) | data formatting | bytes 25165824 | tf_op jit(solution)/shard_map/convert_element_type | solution.py:105
  28.7 0.0 copy-done.4
  28.7 0.1 copy.32
  28.9 0.1 copy.34
  28.9 0.1 copy.33
  29.1 0.1 copy.35
  29.1 27.2 %fusion.2 = f32[128,16,3072]{2,1,0:T(8,128)} fusion(bf16[128,16,3072]{2,0,1:T(8,128)(2,1)} %bitcast.91, s32[]{:T(128)S(6)} %select_n.21, bf16[8,256]{1,0:T(8,128)(2,1)S(1)} %copy.34, bf16[8,256]{1,0:T(8,128)(2,1)S(1)} %copy.35), kind=kOutput, calls=%fused_computation.3 | convolution fusion | flops 201327616 | bytes 37756932 | tf_op jit(solution)/shard_map/ok,dkg->dog/dot_general | solution.py:108
  56.3 0.0 copy-start.3
  56.3 0.0 copy-start.5
  56.3 0.0 reduce-scatter.2.cloned.1.call-update
  56.3 0.9 copy-done.3
  57.2 0.0 copy-done.5
  57.2 0.1 broadcast_in_dim.8
  57.3 245.7 %reduce-scatter.2.cloned.1.call-done = f32[8,16,3072]{2,1,0:T(8,128)} async-done(((f32[128,16,3072]{2,1,0:T(8,128)}), f32[8,16,3072]{2,1,0:T(8,128)}) %reduce-scatter.2.cloned.1.call-update) | async-done | bytes 1572880 | tf_op jit(solution)/shard_map/reduce_scatter | solution.py:107
  303.0 0.0 copy-start.2
  303.0 1.2 fusion.43
  304.1 0.1 collective-permute-start
  304.2 4.4 %collective-permute-start.1 = (f32[1,16,3072]{2,1,0:T(8,128)S(1)}, f32[1,16,3072]{2,1,0:T(8,128)S(1)}, u32[]{:S(2)}, u32[]{:S(2)}) collective-permute-start(f32[1,16,3072]{2,1,0:T(8,128)S(1)} %get-tuple-element.12), channel_id=1, source_target_pairs={{1,0},{2,1},{3,2},{4,3},{5,4},{6,5},{7,6},{8,7},{9,8},{10,9},{11,1... | collective-permute-start | bytes 589832 | tf_op jit(solution)/shard_map/ppermute | solution.py:20
  308.7 3.4 collective-permute-done
  312.1 0.0 collective-permute-done.1
  312.1 2.2 fusion.17
  314.3 0.0 copy-done.2
  314.3 0.5 maximum_bitcast_fusion
  314.8 0.3 copy.37
  315.2 0.0 copy-start
  315.2 5.0 %fusion.5 = f32[8,48,48]{1,2,0:T(8,128)S(1)} fusion(f32[8,48,3072]{2,1,0:T(8,128)S(1)} %bitcast.86, f32[8,3072]{1,0:T(8,128)S(1)} %convert_element_type.30), kind=kOutput, calls=%fused_computation.4 | convolution fusion | flops 680656896 | bytes 4890624 | tf_op jit(solution)/shard_map/nig,njg->nij/dot_general | solution.py:55
  320.2 0.0 copy-done
  320.2 0.1 fusion.41
  320.3 0.1 maximum_maximum_fusion
  320.4 0.1 copy.42
  320.5 0.1 fusion.21
  320.7 35.4 %custom-call.11 = f32[8,48,48]{2,1,0:T(8,128)S(1)} custom-call(f32[8,48,48]{2,1,0:T(8,128)S(1)} %fusion.21), custom_call_target="Cholesky" | custom-call | tf_op jit(solution)/shard_map/jit(cholesky)/cholesky | solution.py:72
  356.2 0.1 compare_reduce_fusion
  356.3 0.1 select_bitcast_fusion
  356.4 29.5 %custom-call.12 = f32[8,1,48,48]{2,3,1,0:T(8,128)S(1)} custom-call(f32[8,1,48,48]{3,2,1,0:T(8,128)S(1)} %select_bitcast_fusion), custom_call_target="InvertDiagBlocksLowerTriangular" | custom-call | tf_op jit(solution)/shard_map/vmap(jit(_cho_solve))/triangular_solve | solution.py:73
  385.9 0.0 copy-start.1
  385.9 0.3 convolution_bitcast_fusion
  386.2 0.4 fusion.18
  386.6 0.1 multiply_reduce_fusion
  386.7 0.1 broadcast_divide_fusion
  386.8 0.1 fusion.44
  386.9 3.4 fusion.14
  390.3 3.0 fusion.8
  393.3 0.0 copy-done.1
  393.4 1.3 fusion.10
  394.7 1.3 fusion.12
  396.1 0.8 copy.43
  (14 shorter events, 0.2 us)
Async XLA Ops:
  6.5 296.4 %reduce-scatter.2.cloned.1.call-start = ((), (), s32[]{:S(2)}) async-start(), calls=%async_computation.1 | async-start | bytes 26738688 | tf_op jit(solution)/shard_map/reduce_scatter | solution.py:107
  18.0 10.6 %copy-start.4 = (bf16[8,2,128]{2,1,0:T(2,128)(2,1)S(1)}, bf16[8,2,128]{2,1,0:T(2,128)(2,1)}, u32[]{:S(2)}) copy-start(bf16[8,2,128]{2,1,0:T(2,128)(2,1)} %param.5) | copy-start | bytes 12292
  56.3 0.9 copy-start.3
  56.3 0.9 copy-start.5
  303.0 11.3 %copy-start.2 = (f32[8,16,3072]{2,1,0:T(8,128)S(1)}, f32[8,16,3072]{2,1,0:T(8,128)}, u32[]{:S(2)}) copy-start(f32[8,16,3072]{2,1,0:T(8,128)} %reduce-scatter.2.cloned.1.call-done) | copy-start | bytes 4718596
  304.1 8.0 %collective-permute-start = (f32[1,16,3072]{2,1,0:T(8,128)S(1)}, f32[1,16,3072]{2,1,0:T(8,128)S(1)}, u32[]{:S(2)}, u32[]{:S(2)}) collective-permute-start(f32[1,16,3072]{2,1,0:T(8,128)S(1)} %get-tuple-element.11), channel_id=1, source_target_pairs={{0,1},{1,2},{2,3},{3,4},{4,5},{5,6},{6,7},{7,8},{8,9},{9,10},{10,1... | collective-permute-start | bytes 589832 | tf_op jit(solution)/shard_map/ppermute | solution.py:18
  304.2 7.9 %collective-permute-start.1 = (f32[1,16,3072]{2,1,0:T(8,128)S(1)}, f32[1,16,3072]{2,1,0:T(8,128)S(1)}, u32[]{:S(2)}, u32[]{:S(2)}) collective-permute-start(f32[1,16,3072]{2,1,0:T(8,128)S(1)} %get-tuple-element.12), channel_id=1, source_target_pairs={{1,0},{2,1},{3,2},{4,3},{5,4},{6,5},{7,6},{8,7},{9,8},{10,9},{11,1... | collective-permute-start | bytes 589832 | tf_op jit(solution)/shard_map/ppermute | solution.py:20
  315.2 5.0 %copy-start = (f32[8,2,3,8,3072]{4,3,2,1,0:T(8,128)}, f32[8,2,3,8,3072]{4,3,2,1,0:T(8,128)S(1)}, u32[]{:S(2)}) copy-start(f32[8,2,3,8,3072]{4,3,2,1,0:T(8,128)S(1)} %copy.37) | copy-start | bytes 14155780
  385.9 7.5 %copy-start.1 = (f32[8,2,3,8,3072]{4,3,2,1,0:T(8,128)S(1)}, f32[8,2,3,8,3072]{4,3,2,1,0:T(8,128)}, u32[]{:S(2)}) copy-start(f32[8,2,3,8,3072]{4,3,2,1,0:T(8,128)} %copy-done) | copy-start | bytes 14155780
Sparse Core Ops, SparseCore 0:
  56.4 246.4 reduce-scatter.1
where the time goes:
time: 405 us; the launch traced here: 404 us
  waiting for transfers between devices  249 us (61%)
  other arithmetic  69.2 us (17%)
  matrix products  52.9 us (13%)
  local copies, waits for them, and re-layouts  14.5 us (4%)
  between operations  13.7 us (3%)
  starting transfers between devices  4.49 us (1%)
    reduce_scatter x1, waiting for transfers between devices, local(): lax.psum_scatter(jnp.einsum('ok,dkg->dog', columns, spectra_rows, preferr...  246 us
    another operation x4, other arithmetic, adapt(): factor = jnp.linalg.cholesky(system)  35.6 us
    another operation x3, other arithmetic, adapt(): jax.scipy.linalg.cho_solve((factor_one, True), target)  29.6 us
    dot_general x1, matrix products, local(): jnp.einsum('ok,dkg->dog', columns, spectra_rows, preferred_element_type=j...  27.2 us
    dot_general x1, matrix products, local(): jnp.einsum('dcr,erg->decg', dft_table, echo_rows, preferred_element_type=...  10.9 us
    convert_element_type x1, local copies, waits for them, and re-layouts, local(): spectra_rows = jnp.einsum('dcr,erg->decg', dft_table, echo_rows, preferre...  10.6 us
  transfers between devices with their start and end apart: 3, of which 2 were waited for; matrix products, arithmetic and copies ran while one was open for 0% of the time, Pallas kernels for 0%

commit v1 on v0

v1 whole, which is shorter than its diff:
```python
import functools
import math

import jax
import jax.numpy as jnp
import numpy as np
from jax import lax
from jax.experimental import pallas as pl
from jax.experimental.pallas import tpu as pltpu
from jax.sharding import PartitionSpec as P

LOADING = 1.0
F32 = jnp.float32
BF16 = jnp.bfloat16
GROUP = 16
CHUNKS = ((3, 0), (6, 0), (6, 0), (6, 0), (3, 0))


def bin_order(strides):
    count = len(strides)
    blocks = []
    for position in range(1 << count):
        blocks.append(sum(s for i, s in enumerate(strides) if position >> (count - 1 - i) & 1))
    return np.array(blocks, np.int32)


def doppler_table(me, strides, bins_here, pulses):
    owners = jnp.bitwise_xor(me, jnp.asarray(bin_order(strides)))
    bins = (owners[:, None] * bins_here + jnp.arange(bins_here, dtype=jnp.int32)).reshape(-1)
    phase = bins[:, None] * jnp.arange(pulses, dtype=jnp.int32)[None, :] % pulses
    angles = -2.0 * math.pi / pulses * phase.astype(F32)
    cosine = jnp.cos(angles) / math.sqrt(pulses)
    sine_part = jnp.sin(angles) / math.sqrt(pulses)
    real_row = jnp.concatenate([cosine, -sine_part], axis=1)
    imag_row = jnp.concatenate([sine_part, cosine], axis=1)
    return jnp.stack([real_row, imag_row], axis=1).astype(BF16).reshape(2 * pulses, 2 * pulses)


def block_weights(beam_weights, me, elem_dev):
    mine = lax.dynamic_slice_in_dim(beam_weights, me * elem_dev, elem_dev, 2)
    weight_re, weight_im = mine[:, 0, :], mine[:, 1, :]
    real_row = jnp.stack([weight_re, -weight_im], axis=2)
    imag_row = jnp.stack([weight_im, weight_re], axis=2)
    matrix = jnp.concatenate([real_row, imag_row], axis=0)
    same = jnp.eye(GROUP, dtype=BF16)
    full = same[:, None, None, :, None] * matrix[None, :, :, None, :]
    return full.reshape(GROUP * matrix.shape[0], elem_dev * GROUP * 2)


def front_kernel(table_ref, weights_ref, echo_ref, send_ref, keep_ref, spectra_ref):
    elem_dev = echo_ref.shape[0]
    groups = spectra_ref.shape[0]
    width = echo_ref.shape[-1]
    table = table_ref[...]
    for e in range(elem_dev):
        spectra = jnp.dot(table, echo_ref[e], preferred_element_type=F32)
        spectra_ref[:, e] = spectra.astype(BF16).reshape(groups, 2 * GROUP, width)
    weights = weights_ref[...]
    rows = weights.shape[0]
    for g in range(groups):
        beams = jnp.dot(weights, spectra_ref[g].reshape(-1, width), preferred_element_type=F32)
        at = g % (groups // 2) * rows
        if g < groups // 2:
            keep_ref[at : at + rows] = beams
        else:
            send_ref[at : at + rows] = beams.astype(BF16)


def front(table, weights, echo, start, size, width):
    elem_dev, rows_in, _ = echo.shape
    groups = rows_in // 2 // GROUP
    half = rows_in // 4 * (weights.shape[0] // GROUP)
    steps = size // width
    first = start // width
    return pl.pallas_call(
        front_kernel,
        grid=(steps,),
        in_specs=[
            pl.BlockSpec(table.shape, lambda i: (0, 0)),
            pl.BlockSpec(weights.shape, lambda i: (0, 0)),
            pl.BlockSpec((elem_dev, rows_in, width), lambda i: (0, 0, first + i)),
        ],
        out_specs=[
            pl.BlockSpec((half, width), lambda i: (0, i)),
            pl.BlockSpec((half, width), lambda i: (0, i)),
        ],
        out_shape=[
            jax.ShapeDtypeStruct((half, size), BF16),
            jax.ShapeDtypeStruct((half, size), F32),
        ],
        scratch_shapes=[pltpu.VMEM((groups, elem_dev, 2 * GROUP, width), BF16)],
        compiler_params=pltpu.CompilerParams(vmem_limit_bytes=48 << 20),
        cost_estimate=pl.CostEstimate(
            flops=4 * elem_dev * rows_in * rows_in * size,
            bytes_accessed=elem_dev * rows_in * size * 2 + half * size * 6,
            transcendentals=0,
        ),
        name="front",
    )(table, weights, echo)


def gram_kernel(own_ref, low_ref, high_ref, mask_ref, gram_ref):
    bins_here = mask_ref.shape[0]
    rows = low_ref.shape[0]
    window = jnp.concatenate([low_ref[...], own_ref[...], high_ref[...]], axis=0)
    top = window.astype(BF16)
    rest = (window - top.astype(F32)).astype(BF16)
    mask = mask_ref[...].astype(F32)
    picked_top, picked_rest = [], []
    for d in range(bins_here):
        keep = mask[d : d + 1].astype(BF16)
        picked_top.append(top[rows * d : rows * (d + 3)] * keep)
        picked_rest.append(rest[rows * d : rows * (d + 3)] * keep)
    left = jnp.concatenate(picked_top, axis=0)
    left_rest = jnp.concatenate(picked_rest, axis=0)
    dims = (((1,), (1,)), ((), ()))
    gram = lax.dot_general(left, top, dims, preferred_element_type=F32)
    gram += lax.dot_general(left, rest, dims, preferred_element_type=F32)
    gram += lax.dot_general(left_rest, top, dims, preferred_element_type=F32)
    gram_ref[...] = gram


def gram_of(own, low, high, mask):
    bins_here, size = mask.shape
    rows = low.shape[0]
    return pl.pallas_call(
        gram_kernel,
        out_shape=jax.ShapeDtypeStruct((bins_here * 3 * rows, (bins_here + 2) * rows), F32),
        compiler_params=pltpu.CompilerParams(vmem_limit_bytes=48 << 20),
        cost_estimate=pl.CostEstimate(
            flops=6 * bins_here * 3 * rows * (bins_here + 2) * rows * size,
            bytes_accessed=(bins_here + 2) * rows * size * 4,
            transcendentals=0,
        ),
        name="gram",
    )(own, low, high, mask)


def tail_kernel(count, *refs):
    steer_ref, refs = refs[0], refs[1:]
    grams, refs = refs[:count], refs[count:]
    owns, lows, highs = refs[:count], refs[count : 2 * count], refs[2 * count : 3 * count]
    out_ref = refs[3 * count]
    window_ref = refs[3 * count + 1]
    rows = lows[0].shape[0]
    beams = rows // 2
    bins_here = owns[0].shape[0] // rows
    order = 3 * beams
    at = 0
    spans = []
    for own, low, high in zip(owns, lows, highs):
        size = own.shape[1]
        spans.append((at, size))
        at += size
    gram = grams[0][...]
    for other in grams[1:]:
        gram += other[...]

    lane = lax.broadcasted_iota(jnp.int32, (1, 1, 128), 2)
    real_lane = lane // beams % 2 == 0
    row_at = lax.broadcasted_iota(jnp.int32, (1, order, 128), 1)
    lane_at = lax.broadcasted_iota(jnp.int32, (1, order, 128), 2)
    column_of = lane_at // rows * beams + lane_at % beams
    diagonal = (column_of == row_at) & (lane_at // beams % 2 == 0) & (lane_at < 3 * rows)
    systems = []
    pad = jnp.zeros((3 * rows, 128 - 3 * rows), F32)
    for d in range(bins_here):
        block = gram[3 * rows * d : 3 * rows * (d + 1), rows * d : rows * (d + 3)]
        block = jnp.concatenate([block, pad], axis=1)
        from_re = jnp.concatenate([block[rows * w : rows * w + beams] for w in range(3)], axis=0)
        from_im = jnp.concatenate(
            [block[rows * w + beams : rows * (w + 1)] for w in range(3)], axis=0
        )
        real = from_re + pltpu.roll(from_im, 128 - beams, 1)
        imag = pltpu.roll(from_im, beams, 1) - from_re
        systems.append(jnp.where(real_lane[0], real, imag))
    steer = steer_ref[...]
    system = jnp.stack(systems, axis=0)
    system = jnp.where(lane < 3 * rows, system, 0.0) + jnp.where(diagonal, LOADING, 0.0)
    system = system + steer[None]

    def swapped(row):
        return jnp.where(
            real_lane, -pltpu.roll(row, 128 - beams, 2), pltpu.roll(row, beams, 2)
        )

    for k in range(order):
        spot = k // beams * rows + k % beams
        pivot_row = system[:, k : k + 1, :]
        pivot_row = pivot_row / pivot_row[:, :, spot : spot + 1]
        factor_re = system[:, :, spot : spot + 1]
        factor_im = system[:, :, spot + beams : spot + beams + 1]
        changed = system - factor_re * pivot_row - factor_im * swapped(pivot_row)
        system = jnp.where(row_at == k, pivot_row, changed)

    solved_re = system[:, :, 3 * rows : 3 * rows + 1]
    solved_im = system[:, :, 3 * rows + beams : 3 * rows + beams + 1]
    target_re = steer[None, :, 3 * rows : 3 * rows + 1]
    target_im = steer[None, :, 3 * rows + beams : 3 * rows + beams + 1]
    response = jnp.sum(solved_re * target_re + solved_im * target_im, axis=1, keepdims=True)
    weight_re = jnp.broadcast_to(solved_re / response, (bins_here, order, 128))
    weight_im = jnp.broadcast_to(solved_im / response, (bins_here, order, 128))

    for index, (start, size) in enumerate(spans):
        for low_lane in range(0, size, 128):
            lanes = slice(low_lane, low_lane + 128)
            blocks = []
            for ref in (lows[index], owns[index], highs[index]):
                part = ref[:, lanes]
                blocks += [part[i : i + beams] for i in range(0, part.shape[0], beams)]
            for d in range(bins_here):
                total_re = jnp.zeros((beams, 128), F32)
                total_im = jnp.zeros((beams, 128), F32)
                for w in range(3):
                    coeff_re = weight_re[d, w * beams : (w + 1) * beams]
                    coeff_im = weight_im[d, w * beams : (w + 1) * beams]
                    snap_re, snap_im = blocks[2 * (d + w)], blocks[2 * (d + w) + 1]
                    total_re += coeff_re * snap_re + coeff_im * snap_im
                    total_im += coeff_re * snap_im - coeff_im * snap_re
                both = jnp.concatenate(
                    [
                        jnp.sum(total_re, axis=0, keepdims=True),
                        jnp.sum(total_im, axis=0, keepdims=True),
                    ],
                    axis=0,
                )
                out_ref[d, :, start + low_lane : start + low_lane + 128] = both


def tail(steer, grams, owns, lows, highs, bins_here):
    gate_count = sum(own.shape[1] for own in owns)
    count = len(owns)
    rows = lows[0].shape[0]
    return pl.pallas_call(
        functools.partial(tail_kernel, count),
        out_shape=jax.ShapeDtypeStruct((bins_here, 2, gate_count), F32),
        scratch_shapes=[pltpu.VMEM((8, 128), F32)],
        compiler_params=pltpu.CompilerParams(vmem_limit_bytes=48 << 20),
        name="tail",
    )(steer, *grams, *owns, *lows, *highs)


def steer_lanes(steer, beams):
    order = steer.shape[1]
    rows = 2 * beams
    return jnp.concatenate(
        [
            jnp.zeros((order, 3 * rows), F32),
            steer[0][:, None],
            jnp.zeros((order, beams - 1), F32),
            steer[1][:, None],
            jnp.zeros((order, 128 - 3 * rows - beams - 1), F32),
        ],
        axis=1,
    )


def swap(x, stride, count):
    return lax.ppermute(x, "elem", [(i, i ^ stride) for i in range(count)])


def reduce_chunk(send, keep, strides, count):
    received = [swap(send, strides[0], count)]
    size = keep.shape[0]
    for stride in strides[1:]:
        size //= 2
        total = keep[size : 2 * size]
        for got in received:
            total = total + got[size : 2 * size].astype(F32)
        received.append(swap(total.astype(BF16), stride, count))
    total = keep[:size]
    for got in received:
        total = total + got[:size].astype(F32)
    return total


def local(raw_echo, beam_weights, steer, train_mask):
    elem_dev, _, pulses, gate_count = raw_echo.shape
    count = lax.axis_size("elem")
    me = lax.axis_index("elem")
    bins_here = pulses // count
    beams = beam_weights.shape[0]
    rows = 2 * beams
    echo = raw_echo.reshape(elem_dev, 2 * pulses, gate_count)
    weights = block_weights(beam_weights, me, elem_dev)
    levels = count.bit_length() - 1
    plain = [1 << i for i in range(levels)]
    other = [plain[0], plain[2], plain[1]] + plain[3:]
    orders = [plain, other]
    tables = {
        kind: doppler_table(me, orders[kind], bins_here, pulses)
        for kind in sorted({kind for _, kind in CHUNKS})
    }
    unit = gate_count // sum(width for width, _ in CHUNKS)
    start = 0
    owns, lows, highs, grams = [], [], [], []
    up = [(i, (i + 1) % count) for i in range(count)]
    down = [((i + 1) % count, i) for i in range(count)]
    for width, kind in CHUNKS:
        size = width * unit
        send, keep = front(tables[kind], weights, echo, start, size, 3 * unit)
        own = reduce_chunk(send, keep, orders[kind], count)
        low = lax.ppermute(own[-rows:], "elem", up)
        high = lax.ppermute(own[:rows], "elem", down)
        grams.append(gram_of(own, low, high, train_mask[:, start : start + size]))
        owns.append(own)
        lows.append(low)
        highs.append(high)
        start += size
    return tail(steer_lanes(steer, beams), grams, owns, lows, highs, bins_here)


def solution(mesh):
    return jax.shard_map(
        local,
        mesh=mesh,
        in_specs=(P(("cpi", "elem"), None, None, None), P(), P(), P(("cpi", "elem"), None)),
        out_specs=P(("cpi", "elem"), None, None),
        check_vma=False,
    )
```

time: 405 us -> 177 us (0.44)
  waiting for transfers between devices: 249 us -> 67.3 us
  matrix products: 52.9 us -> 0 us
  other arithmetic: 69.2 us -> 24.6 us
  Pallas kernels: 0 us -> 34.1 us
  starting transfers between devices: 4.49 us -> 36.8 us
  between operations: 13.7 us -> 0.44 us
    reduce_scatter x1 -> x0, waiting for transfers between devices: 246 us -> none  [local(): lax.psum_scatter(jnp.einsum('ok,dkg->dog', columns, spectra_rows, preferr...]
    another operation x15 -> x3, other arithmetic: 68.1 us -> 0.39 us  [the longest x4 35.6 us: adapt(): factor = jnp.linalg.cholesky(system)]
    ppermute x2 -> x30, waiting for transfers between devices: 3.43 us -> 67.3 us  [the longest x20 66.8 us: swap(): return lax.ppermute(x, 'elem', [(i, i ^ stride) for i in range(count)])]
    dot_general x7 -> x0, matrix products: 52.2 us -> none  [the longest x1 27.2 us: local(): jnp.einsum('ok,dkg->dog', columns, spectra_rows, preferred_element_type=j...]
    pallas_call x0 -> x11, Pallas kernels: none -> 34.1 us  [the longest x5 23.5 us: front(): pl.pallas_call(front_kernel, grid=(steps,), in_specs=[pl.BlockSpec(table....]
    ppermute x2 -> x30, starting transfers between devices: 4.49 us -> 36.8 us  [the longest x20 18.7 us: swap(): return lax.ppermute(x, 'elem', [(i, i ^ stride) for i in range(count)])]
    convert_element_type x2 -> x16, other arithmetic: 0.01 us -> 18.6 us  [the longest x15 18.6 us: reduce_chunk(): received.append(swap(total.astype(BF16), stride, count))]
    convert_element_type x1, local copies, waits for them, and re-layouts: 10.6 us -> 0.06 us  [doppler_table(): jnp.stack([real_row, imag_row], axis=1).astype(BF16)]
  transfers between devices with their start and end apart: 3 -> 30, of which waited for: 2 -> 10; matrix products, arithmetic and copies ran while one was open for 0% -> 17% of each run, Pallas kernels for 0% -> 13%
where the time goes in v1:
time: 177 us; the launch traced here: 176 us
  waiting for transfers between devices  67.3 us (38%)
  starting transfers between devices  36.8 us (21%)
  Pallas kernels  34.1 us (19%)
  other arithmetic  24.6 us (14%)
  local copies, waits for them, and re-layouts  12.6 us (7%)
    ppermute x20, waiting for transfers between devices, swap(): return lax.ppermute(x, 'elem', [(i, i ^ stride) for i in range(count)])  66.8 us
    pallas_call x5, Pallas kernels, front(): pl.pallas_call(front_kernel, grid=(steps,), in_specs=[pl.BlockSpec(table....  23.5 us
    ppermute x20, starting transfers between devices, swap(): return lax.ppermute(x, 'elem', [(i, i ^ stride) for i in range(count)])  18.7 us
    convert_element_type x15, other arithmetic, reduce_chunk(): received.append(swap(total.astype(BF16), stride, count))  18.6 us
    ppermute x5, starting transfers between devices, local(): high = lax.ppermute(own[:rows], 'elem', down)  17.9 us
    pallas_call x1, Pallas kernels, tail(): pl.pallas_call(functools.partial(tail_kernel, count), out_shape=jax.Shape...  6.92 us
    add x5, other arithmetic, reduce_chunk(): total = total + got[:size].astype(F32)  5.34 us
    unnamed x39, local copies, waits for them, and re-layouts  4.38 us
  transfers between devices with their start and end apart: 30, of which 10 were waited for; matrix products, arithmetic and copies ran while one was open for 17% of the time, Pallas kernels for 13%

profile of v1, /device:TPU:0, one launch (start us, length us, event | category | flops | bytes accessed | tf_op | source)
XLA Modules:
  0.0 175.8 jit_solution(6339891976577345150)
XLA Ops:
  0.0 0.8 constant_dynamic-slice_fusion.1
  1.1 1.0 mul.53
  3.0 3.6 %front.9 = (bf16[1024,384]{1,0:T(8,128)(2,1)}, f32[1024,384]{1,0:T(8,128)S(1)}) custom-call(bf16[256,256]{1,0:T(8,128)(2,1)S(1)} %convert_element_type.211.table_ref, bf16[256,256]{1,0:T(8,128)(2,1)S(1)} %copy.16.weights_ref, bf16[8,256,3072]{2,1,0:T(8,128)(2,1)} %bitcast.19), custom_call_target="tpu_custom_call" | custom-call | flops 805306368 | bytes 3932160 | tf_op jit(solution)/shard_map/front/pallas_call | solution.py:75
  7.1 4.4 %front.8 = (bf16[1024,768]{1,0:T(8,128)(2,1)S(1)}, f32[1024,768]{1,0:T(8,128)S(1)}) custom-call(bf16[256,256]{1,0:T(8,128)(2,1)S(1)} %convert_element_type.211.table_ref, bf16[256,256]{1,0:T(8,128)(2,1)S(1)} %copy.16.weights_ref, bf16[8,256,3072]{2,1,0:T(8,128)(2,1)} %bitcast.20), custom_call_target="tpu_custom_call" | custom-call | flops 1610612736 | bytes 7864320 | tf_op jit(solution)/shard_map/front/pallas_call | solution.py:75
  11.7 4.7 %front.5 = (bf16[1024,384]{1,0:T(8,128)(2,1)}, f32[1024,384]{1,0:T(8,128)S(1)}) custom-call(bf16[256,256]{1,0:T(8,128)(2,1)S(1)} %convert_element_type.211.table_ref, bf16[256,256]{1,0:T(8,128)(2,1)S(1)} %copy.16.weights_ref, bf16[8,256,3072]{2,1,0:T(8,128)(2,1)} %bitcast.21), custom_call_target="tpu_custom_call" | custom-call | flops 805306368 | bytes 3932160 | tf_op jit(solution)/shard_map/front/pallas_call | solution.py:75
  16.3 5.1 %front.7 = (bf16[1024,768]{1,0:T(8,128)(2,1)}, f32[1024,768]{1,0:T(8,128)S(1)}) custom-call(bf16[256,256]{1,0:T(8,128)(2,1)S(1)} %convert_element_type.211.table_ref, bf16[256,256]{1,0:T(8,128)(2,1)S(1)} %copy.16.weights_ref, bf16[8,256,3072]{2,1,0:T(8,128)(2,1)} %bitcast.22), custom_call_target="tpu_custom_call" | custom-call | flops 1610612736 | bytes 7864320 | tf_op jit(solution)/shard_map/front/pallas_call | solution.py:75
  21.9 5.7 %front.6 = (bf16[1024,768]{1,0:T(8,128)(2,1)}, f32[1024,768]{1,0:T(8,128)S(1)}) custom-call(bf16[256,256]{1,0:T(8,128)(2,1)S(1)} %convert_element_type.211.table_ref, bf16[256,256]{1,0:T(8,128)(2,1)S(1)} %copy.16.weights_ref, bf16[8,256,3072]{2,1,0:T(8,128)(2,1)} %bitcast.23), custom_call_target="tpu_custom_call" | custom-call | flops 1610612736 | bytes 7864320 | tf_op jit(solution)/shard_map/front/pallas_call | solution.py:75
  28.2 0.6 fusion.15
  28.8 1.1 add_convert_fusion.3
  29.9 2.6 %collective-permute-start.25 = (bf16[512,384]{1,0:T(8,128)(2,1)S(1)}, bf16[512,384]{1,0:T(8,128)(2,1)S(1)}, u32[]{:S(2)}, u32[]{:S(2)}) collective-permute-start(bf16[512,384]{1,0:T(8,128)(2,1)S(1)} %add_convert_fusion.3), channel_id=1, source_target_pairs={{0,2},{1,3},{2,0},{3,1},{4,6},{5,7},{6,4},{7,5},{8,10},{9,11},{10,... | collective-permute-start | bytes 1179656 | tf_op jit(solution)/shard_map/ppermute | solution.py:259
  32.5 1.1 add_convert_fusion.7
  34.3 8.2 %collective-permute-done.25 = bf16[512,384]{1,0:T(8,128)(2,1)S(1)} collective-permute-done((bf16[512,384]{1,0:T(8,128)(2,1)S(1)}, bf16[512,384]{1,0:T(8,128)(2,1)S(1)}, u32[]{:S(2)}, u32[]{:S(2)}) %collective-permute-start.25) | collective-permute-done | bytes 393248 | tf_op jit(solution)/shard_map/ppermute | solution.py:259
  42.5 1.0 add_convert_fusion.8
  43.5 2.1 %collective-permute-start.26 = (bf16[256,384]{1,0:T(8,128)(2,1)S(1)}, bf16[256,384]{1,0:T(8,128)(2,1)S(1)}, u32[]{:S(2)}, u32[]{:S(2)}) collective-permute-start(bf16[256,384]{1,0:T(8,128)(2,1)S(1)} %add_convert_fusion.8), channel_id=1, source_target_pairs={{0,4},{1,5},{2,6},{3,7},{4,0},{5,1},{6,2},{7,3},{8,12},{9,13},{10,... | collective-permute-start | bytes 589832 | tf_op jit(solution)/shard_map/ppermute | solution.py:259
  45.5 5.2 %collective-permute-done.1 = bf16[512,384]{1,0:T(8,128)(2,1)S(1)} collective-permute-done((bf16[512,384]{1,0:T(8,128)(2,1)S(1)}, bf16[512,384]{1,0:T(8,128)(2,1)S(1)}, u32[]{:S(2)}, u32[]{:S(2)}) %collective-permute-start.1) | collective-permute-done | bytes 393248 | tf_op jit(solution)/shard_map/ppermute | solution.py:259
  50.7 1.0 add_convert_fusion.12
  51.7 1.9 %collective-permute-start.2 = (bf16[256,384]{1,0:T(8,128)(2,1)S(1)}, bf16[256,384]{1,0:T(8,128)(2,1)S(1)}, u32[]{:S(2)}, u32[]{:S(2)}) collective-permute-start(bf16[256,384]{1,0:T(8,128)(2,1)S(1)} %add_convert_fusion.12), channel_id=1, source_target_pairs={{0,4},{1,5},{2,6},{3,7},{4,0},{5,1},{6,2},{7,3},{8,12},{9,13},{10,... | collective-permute-start | bytes 589832 | tf_op jit(solution)/shard_map/ppermute | solution.py:259
  53.6 0.9 add_convert_fusion.13
  54.5 2.7 %collective-permute-start.27 = (bf16[128,384]{1,0:T(8,128)(2,1)S(1)}, bf16[128,384]{1,0:T(8,128)(2,1)S(1)}, u32[]{:S(2)}, u32[]{:S(2)}) collective-permute-start(bf16[128,384]{1,0:T(8,128)(2,1)S(1)} %add_convert_fusion.13), channel_id=1, source_target_pairs={{0,8},{1,9},{2,10},{3,11},{4,12},{5,13},{6,14},{7,15},{8,0},{9,1},... | collective-permute-start | bytes 294920 | tf_op jit(solution)/shard_map/ppermute | solution.py:259
  57.2 3.1 %collective-permute-done.2 = bf16[256,384]{1,0:T(8,128)(2,1)S(1)} collective-permute-done((bf16[256,384]{1,0:T(8,128)(2,1)S(1)}, bf16[256,384]{1,0:T(8,128)(2,1)S(1)}, u32[]{:S(2)}, u32[]{:S(2)}) %collective-permute-start.2) | collective-permute-done | bytes 196640 | tf_op jit(solution)/shard_map/ppermute | solution.py:259
  60.3 0.9 add_convert_fusion.14
  61.2 1.9 %collective-permute-start.3 = (bf16[128,384]{1,0:T(8,128)(2,1)S(1)}, bf16[128,384]{1,0:T(8,128)(2,1)S(1)}, u32[]{:S(2)}, u32[]{:S(2)}) collective-permute-start(bf16[128,384]{1,0:T(8,128)(2,1)S(1)} %add_convert_fusion.14), channel_id=1, source_target_pairs={{0,8},{1,9},{2,10},{3,11},{4,12},{5,13},{6,14},{7,15},{8,0},{9,1},... | collective-permute-start | bytes 294920 | tf_op jit(solution)/shard_map/ppermute | solution.py:259
  63.2 1.0 convert_add_fusion.3.own_ref.refs_10_
  64.2 3.7 %collective-permute-done.3 = bf16[128,384]{1,0:T(8,128)(2,1)S(1)} collective-permute-done((bf16[128,384]{1,0:T(8,128)(2,1)S(1)}, bf16[128,384]{1,0:T(8,128)(2,1)S(1)}, u32[]{:S(2)}, u32[]{:S(2)}) %collective-permute-start.3) | collective-permute-done | bytes 98336 | tf_op jit(solution)/shard_map/ppermute | solution.py:259
  67.9 0.8 collective-permute-start.29
  68.6 1.0 convert_add_fusion.4.own_ref.refs_6_
  69.6 0.6 fusion.13
  70.2 2.2 %add_convert_fusion = bf16[512,768]{1,0:T(8,128)(2,1)} fusion(f32[1024,768]{1,0:T(8,128)S(1)} %get-tuple-element.21, bf16[1024,768]{1,0:T(8,128)(2,1)} %collective-permute-done.18), kind=kLoop, calls=%fused_computation | loop fusion | flops 1179648 | bytes 3145728 | tf_op jit(solution)/shard_map/convert_element_type | solution.py:270
  72.4 1.3 collective-permute-start.19
  73.7 2.2 %add_convert_fusion.1 = bf16[512,768]{1,0:T(8,128)(2,1)} fusion(f32[1024,768]{1,0:T(8,128)S(1)} %get-tuple-element.19, bf16[1024,768]{1,0:T(8,128)(2,1)} %collective-permute-done.12), kind=kLoop, calls=%fused_computation.1 | loop fusion | flops 1179648 | bytes 3145728 | tf_op jit(solution)/shard_map/convert_element_type | solution.py:270
  75.9 0.7 collective-permute-start.13
  76.7 1.1 add_convert_fusion.2
  78.3 3.9 %collective-permute-start.5 = (f32[16,384]{1,0:T(8,128)}, f32[16,384]{1,0:T(8,128)}, u32[]{:S(2)}, u32[]{:S(2)}) collective-permute-start(f32[16,384]{1,0:T(8,128)} %get-tuple-element.35), channel_id=1, source_target_pairs={{1,0},{2,1},{3,2},{4,3},{5,4},{6,5},{7,6},{8,7},{9,8},{10,9},{11,1... | collective-permute-start | bytes 73736 | tf_op jit(solution)/shard_map/ppermute | solution.py:304
  82.2 0.6 copy-done.6
  82.8 0.7 copy.11
  83.5 0.7 copy.12
  86.0 0.9 concatenate.14.refs_0_
  86.8 0.7 copy-done.4
  87.6 0.7 copy-done.7
  88.3 0.7 copy-done.10
  89.5 0.9 copy-done.9
  90.5 1.2 gram.5.refs_1_
  91.7 1.7 collective-permute-done.19
  93.4 1.5 add_convert_fusion.4
  95.2 15.1 %collective-permute-done.13 = bf16[512,768]{1,0:T(8,128)(2,1)} collective-permute-done((bf16[512,768]{1,0:T(8,128)(2,1)}, bf16[512,768]{1,0:T(8,128)(2,1)}, u32[]{:S(2)}, u32[]{:S(2)}) %collective-permute-start.13) | collective-permute-done | bytes 786464 | tf_op jit(solution)/shard_map/ppermute | solution.py:259
  110.3 1.2 add_convert_fusion.5
  111.8 15.5 %collective-permute-done.7 = bf16[512,768]{1,0:T(8,128)(2,1)} collective-permute-done((bf16[512,768]{1,0:T(8,128)(2,1)}, bf16[512,768]{1,0:T(8,128)(2,1)}, u32[]{:S(2)}, u32[]{:S(2)}) %collective-permute-start.7) | collective-permute-done | bytes 786464 | tf_op jit(solution)/shard_map/ppermute | solution.py:259
  127.3 1.1 add_convert_fusion.6
  128.5 1.2 add_convert_fusion.9
  129.8 2.8 %collective-permute-start.21 = (bf16[128,768]{1,0:T(8,128)(2,1)S(1)}, bf16[128,768]{1,0:T(8,128)(2,1)S(1)}, u32[]{:S(2)}, u32[]{:S(2)}) collective-permute-start(bf16[128,768]{1,0:T(8,128)(2,1)S(1)} %add_convert_fusion.9), channel_id=1, source_target_pairs={{0,8},{1,9},{2,10},{3,11},{4,12},{5,13},{6,14},{7,15},{8,0},{9,1},... | collective-permute-start | bytes 589832 | tf_op jit(solution)/shard_map/ppermute | solution.py:259
  132.6 1.1 add_convert_fusion.10
  133.9 12.2 %collective-permute-done.8 = bf16[256,768]{1,0:T(8,128)(2,1)S(1)} collective-permute-done((bf16[256,768]{1,0:T(8,128)(2,1)S(1)}, bf16[256,768]{1,0:T(8,128)(2,1)S(1)}, u32[]{:S(2)}, u32[]{:S(2)}) %collective-permute-start.8) | collective-permute-done | bytes 393248 | tf_op jit(solution)/shard_map/ppermute | solution.py:259
  146.2 1.0 add_convert_fusion.11
  147.3 1.3 convert_add_fusion.own_ref.refs_9_
  148.6 4.4 %collective-permute-start.23 = (f32[16,768]{1,0:T(8,128)S(1)}, f32[16,768]{1,0:T(8,128)S(1)}, u32[]{:S(2)}, u32[]{:S(2)}) collective-permute-start(f32[16,768]{1,0:T(8,128)S(1)} %get-tuple-element.27), channel_id=1, source_target_pairs={{1,0},{2,1},{3,2},{4,3},{5,4},{6,5},{7,6},{8,7},{9,8},{10,9},{11,1... | collective-permute-start | bytes 147464 | tf_op jit(solution)/shard_map/ppermute | solution.py:304
  153.1 2.1 %collective-permute-done.15 = bf16[128,768]{1,0:T(8,128)(2,1)S(1)} collective-permute-done((bf16[128,768]{1,0:T(8,128)(2,1)S(1)}, bf16[128,768]{1,0:T(8,128)(2,1)S(1)}, u32[]{:S(2)}, u32[]{:S(2)}) %collective-permute-start.15) | collective-permute-done | bytes 196640 | tf_op jit(solution)/shard_map/ppermute | solution.py:259
  155.2 1.1 convert_add_fusion.1.own_ref.refs_8_
  156.4 4.4 %collective-permute-start.17 = (f32[16,768]{1,0:T(8,128)S(1)}, f32[16,768]{1,0:T(8,128)S(1)}, u32[]{:S(2)}, u32[]{:S(2)}) collective-permute-start(f32[16,768]{1,0:T(8,128)S(1)} %get-tuple-element.29), channel_id=1, source_target_pairs={{1,0},{2,1},{3,2},{4,3},{5,4},{6,5},{7,6},{8,7},{9,8},{10,9},{11,1... | collective-permute-start | bytes 147464 | tf_op jit(solution)/shard_map/ppermute | solution.py:304
  160.8 1.0 convert_add_fusion.2.own_ref.refs_7_
  162.0 4.4 %collective-permute-start.11 = (f32[16,768]{1,0:T(8,128)S(1)}, f32[16,768]{1,0:T(8,128)S(1)}, u32[]{:S(2)}, u32[]{:S(2)}) collective-permute-start(f32[16,768]{1,0:T(8,128)S(1)} %get-tuple-element.31), channel_id=1, source_target_pairs={{1,0},{2,1},{3,2},{4,3},{5,4},{6,5},{7,6},{8,7},{9,8},{10,9},{11,1... | collective-permute-start | bytes 147464 | tf_op jit(solution)/shard_map/ppermute | solution.py:304
  166.4 0.6 gram.8.refs_4_
  167.1 0.6 gram.7.refs_3_
  168.2 0.6 gram.6.refs_2_
  168.8 6.9 %tail.1 = f32[8,2,3072]{2,1,0:T(2,128)} custom-call(f32[24,128]{1,0:T(8,128)S(1)} %concatenate.14.refs_0_, f32[384,160]{1,0:T(8,128)S(1)} %gram.5.refs_1_, f32[384,160]{1,0:T(8,128)S(1)} %gram.6.refs_2_, f32[384,160]{1,0:T(8,128)S(1)} %gram.7.refs_3_, f32[384,160]{1,0:T(8,128)S(1)} %gram.8.refs_4_, f32[384,160]{1,0:T(8,128)S(1)} %gram.9.refs_5_, ...), custom_call_target="tpu_custom_call" | custom-call | tf_op jit(solution)/shard_map/tail/pallas_call | solution.py:234
  (96 shorter events, 8.1 us)
Async XLA Ops:
  0.0 2.2 %copy-start.18 = (s32[16]{0:T(128)S(1)}, s32[16]{0:T(128)}, u32[]{:S(2)}) copy-start(s32[16]{0:T(128)} %constant.35.clone) | copy-start | bytes 196
  6.7 22.2 %collective-permute-start.24 = (bf16[1024,384]{1,0:T(8,128)(2,1)}, bf16[1024,384]{1,0:T(8,128)(2,1)}, u32[]{:S(2)}, u32[]{:S(2)}) collective-permute-start(bf16[1024,384]{1,0:T(8,128)(2,1)} %get-tuple-element.24), channel_id=1, source_target_pairs={{0,1},{1,0},{2,3},{3,2},{4,5},{5,4},{6,7},{7,6},{8,9},{9,8},{10,11... | collective-permute-start | bytes 2359304 | tf_op jit(solution)/shard_map/ppermute | solution.py:259
  11.5 58.7 %copy-start.2 = (f32[1024,768]{1,0:T(8,128)}, f32[1024,768]{1,0:T(8,128)S(1)}, u32[]{:S(2)}) copy-start(f32[1024,768]{1,0:T(8,128)S(1)} %get-tuple-element.21) | copy-start | bytes 9437188
  11.5 58.7 %collective-permute-start.18 = (bf16[1024,768]{1,0:T(8,128)(2,1)S(1)}, bf16[1024,768]{1,0:T(8,128)(2,1)}, u32[]{:S(2)}, u32[]{:S(2)}) collective-permute-start(bf16[1024,768]{1,0:T(8,128)(2,1)S(1)} %get-tuple-element.22), channel_id=1, source_target_pairs={{0,1},{1,0},{2,3},{3,2},{4,5},{5,4},{6,7},{7,6},{8,9},{9,8},{10,11... | collective-permute-start | bytes 4718600 | tf_op jit(solution)/shard_map/ppermute | solution.py:259
  16.3 16.2 %collective-permute-start = (bf16[1024,384]{1,0:T(8,128)(2,1)}, bf16[1024,384]{1,0:T(8,128)(2,1)}, u32[]{:S(2)}, u32[]{:S(2)}) collective-permute-start(bf16[1024,384]{1,0:T(8,128)(2,1)} %get-tuple-element.16), channel_id=1, source_target_pairs={{0,1},{1,0},{2,3},{3,2},{4,5},{5,4},{6,7},{7,6},{8,9},{9,8},{10,11... | collective-permute-start | bytes 2359304 | tf_op jit(solution)/shard_map/ppermute | solution.py:259
  21.4 52.3 %copy-start = (f32[1024,768]{1,0:T(8,128)}, f32[1024,768]{1,0:T(8,128)S(1)}, u32[]{:S(2)}) copy-start(f32[1024,768]{1,0:T(8,128)S(1)} %get-tuple-element.19) | copy-start | bytes 9437188
  21.4 6.8 %copy-start.16 = (s32[8,3072]{1,0:T(8,128)S(1)}, s32[8,3072]{1,0:T(8,128)}, u32[]{:S(2)}) copy-start(s32[8,3072]{1,0:T(8,128)} %param.8) | copy-start | bytes 294916
  21.4 51.0 %collective-permute-start.12 = (bf16[1024,768]{1,0:T(8,128)(2,1)}, bf16[1024,768]{1,0:T(8,128)(2,1)}, u32[]{:S(2)}, u32[]{:S(2)}) collective-permute-start(bf16[1024,768]{1,0:T(8,128)(2,1)} %get-tuple-element.20), channel_id=1, source_target_pairs={{0,1},{1,0},{2,3},{3,2},{4,5},{5,4},{6,7},{7,6},{8,9},{9,8},{10,11... | collective-permute-start | bytes 4718600 | tf_op jit(solution)/shard_map/ppermute | solution.py:259
  27.7 48.2 %collective-permute-start.6 = (bf16[1024,768]{1,0:T(8,128)(2,1)}, bf16[1024,768]{1,0:T(8,128)(2,1)S(1)}, u32[]{:S(2)}, u32[]{:S(2)}) collective-permute-start(bf16[1024,768]{1,0:T(8,128)(2,1)} %get-tuple-element.18), channel_id=1, source_target_pairs={{0,1},{1,0},{2,3},{3,2},{4,5},{5,4},{6,7},{7,6},{8,9},{9,8},{10,11... | collective-permute-start | bytes 4718600 | tf_op jit(solution)/shard_map/ppermute | solution.py:259
  29.9 12.6 %collective-permute-start.25 = (bf16[512,384]{1,0:T(8,128)(2,1)S(1)}, bf16[512,384]{1,0:T(8,128)(2,1)S(1)}, u32[]{:S(2)}, u32[]{:S(2)}) collective-permute-start(bf16[512,384]{1,0:T(8,128)(2,1)S(1)} %add_convert_fusion.3), channel_id=1, source_target_pairs={{0,2},{1,3},{2,0},{3,1},{4,6},{5,7},{6,4},{7,5},{8,10},{9,11},{10,... | collective-permute-start | bytes 1179656 | tf_op jit(solution)/shard_map/ppermute | solution.py:259
  33.6 17.1 %collective-permute-start.1 = (bf16[512,384]{1,0:T(8,128)(2,1)S(1)}, bf16[512,384]{1,0:T(8,128)(2,1)S(1)}, u32[]{:S(2)}, u32[]{:S(2)}) collective-permute-start(bf16[512,384]{1,0:T(8,128)(2,1)S(1)} %add_convert_fusion.7), channel_id=1, source_target_pairs={{0,2},{1,3},{2,0},{3,1},{4,6},{5,7},{6,4},{7,5},{8,10},{9,11},{10,... | collective-permute-start | bytes 1179656 | tf_op jit(solution)/shard_map/ppermute | solution.py:259
  43.5 10.1 %collective-permute-start.26 = (bf16[256,384]{1,0:T(8,128)(2,1)S(1)}, bf16[256,384]{1,0:T(8,128)(2,1)S(1)}, u32[]{:S(2)}, u32[]{:S(2)}) collective-permute-start(bf16[256,384]{1,0:T(8,128)(2,1)S(1)} %add_convert_fusion.8), channel_id=1, source_target_pairs={{0,4},{1,5},{2,6},{3,7},{4,0},{5,1},{6,2},{7,3},{8,12},{9,13},{10,... | collective-permute-start | bytes 589832 | tf_op jit(solution)/shard_map/ppermute | solution.py:259
  51.7 8.6 %collective-permute-start.2 = (bf16[256,384]{1,0:T(8,128)(2,1)S(1)}, bf16[256,384]{1,0:T(8,128)(2,1)S(1)}, u32[]{:S(2)}, u32[]{:S(2)}) collective-permute-start(bf16[256,384]{1,0:T(8,128)(2,1)S(1)} %add_convert_fusion.12), channel_id=1, source_target_pairs={{0,4},{1,5},{2,6},{3,7},{4,0},{5,1},{6,2},{7,3},{8,12},{9,13},{10,... | collective-permute-start | bytes 589832 | tf_op jit(solution)/shard_map/ppermute | solution.py:259
  54.5 8.7 %collective-permute-start.27 = (bf16[128,384]{1,0:T(8,128)(2,1)S(1)}, bf16[128,384]{1,0:T(8,128)(2,1)S(1)}, u32[]{:S(2)}, u32[]{:S(2)}) collective-permute-start(bf16[128,384]{1,0:T(8,128)(2,1)S(1)} %add_convert_fusion.13), channel_id=1, source_target_pairs={{0,8},{1,9},{2,10},{3,11},{4,12},{5,13},{6,14},{7,15},{8,0},{9,1},... | collective-permute-start | bytes 294920 | tf_op jit(solution)/shard_map/ppermute | solution.py:259
  61.2 6.6 %collective-permute-start.3 = (bf16[128,384]{1,0:T(8,128)(2,1)S(1)}, bf16[128,384]{1,0:T(8,128)(2,1)S(1)}, u32[]{:S(2)}, u32[]{:S(2)}) collective-permute-start(bf16[128,384]{1,0:T(8,128)(2,1)S(1)} %add_convert_fusion.14), channel_id=1, source_target_pairs={{0,8},{1,9},{2,10},{3,11},{4,12},{5,13},{6,14},{7,15},{8,0},{9,1},... | collective-permute-start | bytes 294920 | tf_op jit(solution)/shard_map/ppermute | solution.py:259
  64.2 13.6 %collective-permute-start.28 = (f32[16,384]{1,0:T(8,128)S(1)}, f32[16,384]{1,0:T(8,128)S(1)}, u32[]{:S(2)}, u32[]{:S(2)}) collective-permute-start(f32[16,384]{1,0:T(8,128)S(1)} %get-tuple-element.34), channel_id=1, source_target_pairs={{0,1},{1,2},{2,3},{3,4},{4,5},{5,6},{6,7},{7,8},{8,9},{9,10},{10,1... | collective-permute-start | bytes 73736 | tf_op jit(solution)/shard_map/ppermute | solution.py:303
  67.9 14.3 %collective-permute-start.29 = (f32[16,384]{1,0:T(8,128)S(1)}, f32[16,384]{1,0:T(8,128)S(1)}, u32[]{:S(2)}, u32[]{:S(2)}) collective-permute-start(f32[16,384]{1,0:T(8,128)S(1)} %get-tuple-element.33), channel_id=1, source_target_pairs={{1,0},{2,1},{3,2},{4,3},{5,4},{6,5},{7,6},{8,7},{9,8},{10,9},{11,1... | collective-permute-start | bytes 73736 | tf_op jit(solution)/shard_map/ppermute | solution.py:304
  70.2 19.3 %collective-permute-start.4 = (f32[16,384]{1,0:T(8,128)}, f32[16,384]{1,0:T(8,128)}, u32[]{:S(2)}, u32[]{:S(2)}) collective-permute-start(f32[16,384]{1,0:T(8,128)} %get-tuple-element.36), channel_id=1, source_target_pairs={{0,1},{1,2},{2,3},{3,4},{4,5},{5,6},{6,7},{7,8},{8,9},{9,10},{10,1... | collective-permute-start | bytes 73736 | tf_op jit(solution)/shard_map/ppermute | solution.py:303
  72.4 21.0 %collective-permute-start.19 = (bf16[512,768]{1,0:T(8,128)(2,1)}, bf16[512,768]{1,0:T(8,128)(2,1)}, u32[]{:S(2)}, u32[]{:S(2)}) collective-permute-start(bf16[512,768]{1,0:T(8,128)(2,1)} %add_convert_fusion), channel_id=1, source_target_pairs={{0,2},{1,3},{2,0},{3,1},{4,6},{5,7},{6,4},{7,5},{8,10},{9,11},{10,... | collective-permute-start | bytes 2359304 | tf_op jit(solution)/shard_map/ppermute | solution.py:259
  75.9 1.8 %copy-start.14 = (bf16[1024,768]{1,0:T(8,128)(2,1)}, bf16[1024,768]{1,0:T(8,128)(2,1)S(1)}, u32[]{:S(2)}) copy-start(bf16[1024,768]{1,0:T(8,128)(2,1)S(1)} %collective-permute-done.6) | copy-start | bytes 4718596
  75.9 34.3 %collective-permute-start.13 = (bf16[512,768]{1,0:T(8,128)(2,1)}, bf16[512,768]{1,0:T(8,128)(2,1)}, u32[]{:S(2)}, u32[]{:S(2)}) collective-permute-start(bf16[512,768]{1,0:T(8,128)(2,1)} %add_convert_fusion.1), channel_id=1, source_target_pairs={{0,2},{1,3},{2,0},{3,1},{4,6},{5,7},{6,4},{7,5},{8,10},{9,11},{10,... | collective-permute-start | bytes 2359304 | tf_op jit(solution)/shard_map/ppermute | solution.py:259
  76.7 6.2 %copy-start.17 = (f32[2,24]{1,0:T(2,128)S(1)}, f32[2,24]{1,0:T(2,128)}, u32[]{:S(2)}) copy-start(f32[2,24]{1,0:T(2,128)} %param.7) | copy-start | bytes 580
  77.7 0.6 copy-start.3
  78.3 11.2 %collective-permute-start.5 = (f32[16,384]{1,0:T(8,128)}, f32[16,384]{1,0:T(8,128)}, u32[]{:S(2)}, u32[]{:S(2)}) collective-permute-start(f32[16,384]{1,0:T(8,128)} %get-tuple-element.35), channel_id=1, source_target_pairs={{1,0},{2,1},{3,2},{4,3},{5,4},{6,5},{7,6},{8,7},{9,8},{10,9},{11,1... | collective-permute-start | bytes 73736 | tf_op jit(solution)/shard_map/ppermute | solution.py:304
  82.2 0.6 copy-start.6
  82.8 44.5 %collective-permute-start.7 = (bf16[512,768]{1,0:T(8,128)(2,1)}, bf16[512,768]{1,0:T(8,128)(2,1)}, u32[]{:S(2)}, u32[]{:S(2)}) collective-permute-start(bf16[512,768]{1,0:T(8,128)(2,1)} %add_convert_fusion.2), channel_id=1, source_target_pairs={{0,2},{1,3},{2,0},{3,1},{4,6},{5,7},{6,4},{7,5},{8,10},{9,11},{10,... | collective-permute-start | bytes 2359304 | tf_op jit(solution)/shard_map/ppermute | solution.py:259
  86.8 0.7 copy-start.4
  87.6 0.7 copy-start.7
  88.3 0.7 copy-start.10
  89.0 21.2 %copy-start.1 = (f32[1024,768]{1,0:T(8,128)S(1)}, f32[1024,768]{1,0:T(8,128)}, u32[]{:S(2)}) copy-start(f32[1024,768]{1,0:T(8,128)} %copy-done) | copy-start | bytes 9437188
  89.5 1.0 copy-start.9
  91.7 35.6 %copy-start.15 = (bf16[1024,768]{1,0:T(8,128)(2,1)S(1)}, bf16[1024,768]{1,0:T(8,128)(2,1)}, u32[]{:S(2)}) copy-start(bf16[1024,768]{1,0:T(8,128)(2,1)} %copy-done.14) | copy-start | bytes 4718596
  94.9 33.7 %collective-permute-start.20 = (bf16[256,768]{1,0:T(8,128)(2,1)S(1)}, bf16[256,768]{1,0:T(8,128)(2,1)S(1)}, u32[]{:S(2)}, u32[]{:S(2)}) collective-permute-start(bf16[256,768]{1,0:T(8,128)(2,1)S(1)} %add_convert_fusion.4), channel_id=1, source_target_pairs={{0,4},{1,5},{2,6},{3,7},{4,0},{5,1},{6,2},{7,3},{8,12},{9,13},{10,... | collective-permute-start | bytes 1179656 | tf_op jit(solution)/shard_map/ppermute | solution.py:259
  111.5 21.1 %collective-permute-start.14 = (bf16[256,768]{1,0:T(8,128)(2,1)S(1)}, bf16[256,768]{1,0:T(8,128)(2,1)S(1)}, u32[]{:S(2)}, u32[]{:S(2)}) collective-permute-start(bf16[256,768]{1,0:T(8,128)(2,1)S(1)} %add_convert_fusion.5), channel_id=1, source_target_pairs={{0,4},{1,5},{2,6},{3,7},{4,0},{5,1},{6,2},{7,3},{8,12},{9,13},{10,... | collective-permute-start | bytes 1179656 | tf_op jit(solution)/shard_map/ppermute | solution.py:259
  128.4 17.8 %collective-permute-start.8 = (bf16[256,768]{1,0:T(8,128)(2,1)S(1)}, bf16[256,768]{1,0:T(8,128)(2,1)S(1)}, u32[]{:S(2)}, u32[]{:S(2)}) collective-permute-start(bf16[256,768]{1,0:T(8,128)(2,1)S(1)} %add_convert_fusion.6), channel_id=1, source_target_pairs={{0,4},{1,5},{2,6},{3,7},{4,0},{5,1},{6,2},{7,3},{8,12},{9,13},{10,... | collective-permute-start | bytes 1179656 | tf_op jit(solution)/shard_map/ppermute | solution.py:259
  129.8 17.5 %collective-permute-start.21 = (bf16[128,768]{1,0:T(8,128)(2,1)S(1)}, bf16[128,768]{1,0:T(8,128)(2,1)S(1)}, u32[]{:S(2)}, u32[]{:S(2)}) collective-permute-start(bf16[128,768]{1,0:T(8,128)(2,1)S(1)} %add_convert_fusion.9), channel_id=1, source_target_pairs={{0,8},{1,9},{2,10},{3,11},{4,12},{5,13},{6,14},{7,15},{8,0},{9,1},... | collective-permute-start | bytes 589832 | tf_op jit(solution)/shard_map/ppermute | solution.py:259
  133.7 21.5 %collective-permute-start.15 = (bf16[128,768]{1,0:T(8,128)(2,1)S(1)}, bf16[128,768]{1,0:T(8,128)(2,1)S(1)}, u32[]{:S(2)}, u32[]{:S(2)}) collective-permute-start(bf16[128,768]{1,0:T(8,128)(2,1)S(1)} %add_convert_fusion.10), channel_id=1, source_target_pairs={{0,8},{1,9},{2,10},{3,11},{4,12},{5,13},{6,14},{7,15},{8,0},{9,1},... | collective-permute-start | bytes 589832 | tf_op jit(solution)/shard_map/ppermute | solution.py:259
  147.2 13.6 %collective-permute-start.9 = (bf16[128,768]{1,0:T(8,128)(2,1)S(1)}, bf16[128,768]{1,0:T(8,128)(2,1)S(1)}, u32[]{:S(2)}, u32[]{:S(2)}) collective-permute-start(bf16[128,768]{1,0:T(8,128)(2,1)S(1)} %add_convert_fusion.11), channel_id=1, source_target_pairs={{0,8},{1,9},{2,10},{3,11},{4,12},{5,13},{6,14},{7,15},{8,0},{9,1},... | collective-permute-start | bytes 589832 | tf_op jit(solution)/shard_map/ppermute | solution.py:259
  148.6 13.4 %collective-permute-start.22 = (f32[16,768]{1,0:T(8,128)S(1)}, f32[16,768]{1,0:T(8,128)S(1)}, u32[]{:S(2)}, u32[]{:S(2)}) collective-permute-start(f32[16,768]{1,0:T(8,128)S(1)} %get-tuple-element.28), channel_id=1, source_target_pairs={{0,1},{1,2},{2,3},{3,4},{4,5},{5,6},{6,7},{7,8},{8,9},{9,10},{10,1... | collective-permute-start | bytes 147464 | tf_op jit(solution)/shard_map/ppermute | solution.py:303
  148.6 17.8 %copy-start.13 = (s32[8,768]{1,0:T(8,128)S(1)}, s32[8,768]{1,0:T(8,128)}, u32[]{:S(2)}) copy-start(s32[8,768]{1,0:T(8,128)} %get-tuple-element.39.mask_ref) | copy-start | bytes 73732
  148.6 17.8 %collective-permute-start.23 = (f32[16,768]{1,0:T(8,128)S(1)}, f32[16,768]{1,0:T(8,128)S(1)}, u32[]{:S(2)}, u32[]{:S(2)}) collective-permute-start(f32[16,768]{1,0:T(8,128)S(1)} %get-tuple-element.27), channel_id=1, source_target_pairs={{1,0},{2,1},{3,2},{4,3},{5,4},{6,5},{7,6},{8,7},{9,8},{10,9},{11,1... | collective-permute-start | bytes 147464 | tf_op jit(solution)/shard_map/ppermute | solution.py:304
  156.3 10.8 %copy-start.12 = (s32[8,768]{1,0:T(8,128)S(1)}, s32[8,768]{1,0:T(8,128)}, u32[]{:S(2)}) copy-start(s32[8,768]{1,0:T(8,128)} %get-tuple-element.40.mask_ref) | copy-start | bytes 73732
  156.3 10.7 %collective-permute-start.16 = (f32[16,768]{1,0:T(8,128)S(1)}, f32[16,768]{1,0:T(8,128)S(1)}, u32[]{:S(2)}, u32[]{:S(2)}) collective-permute-start(f32[16,768]{1,0:T(8,128)S(1)} %get-tuple-element.30), channel_id=1, source_target_pairs={{0,1},{1,2},{2,3},{3,4},{4,5},{5,6},{6,7},{7,8},{8,9},{9,10},{10,1... | collective-permute-start | bytes 147464 | tf_op jit(solution)/shard_map/ppermute | solution.py:303
  156.4 11.8 %copy-start.11 = (s32[8,768]{1,0:T(8,128)S(1)}, s32[8,768]{1,0:T(8,128)}, u32[]{:S(2)}) copy-start(s32[8,768]{1,0:T(8,128)} %get-tuple-element.41.mask_ref) | copy-start | bytes 73732
  156.4 10.7 %collective-permute-start.17 = (f32[16,768]{1,0:T(8,128)S(1)}, f32[16,768]{1,0:T(8,128)S(1)}, u32[]{:S(2)}, u32[]{:S(2)}) collective-permute-start(f32[16,768]{1,0:T(8,128)S(1)} %get-tuple-element.29), channel_id=1, source_target_pairs={{1,0},{2,1},{3,2},{4,3},{5,4},{6,5},{7,6},{8,7},{9,8},{10,9},{11,1... | collective-permute-start | bytes 147464 | tf_op jit(solution)/shard_map/ppermute | solution.py:304
  161.9 6.3 %collective-permute-start.10 = (f32[16,768]{1,0:T(8,128)S(1)}, f32[16,768]{1,0:T(8,128)S(1)}, u32[]{:S(2)}, u32[]{:S(2)}) collective-permute-start(f32[16,768]{1,0:T(8,128)S(1)} %get-tuple-element.32), channel_id=1, source_target_pairs={{0,1},{1,2},{2,3},{3,4},{4,5},{5,6},{6,7},{7,8},{8,9},{9,10},{10,1... | collective-permute-start | bytes 147464 | tf_op jit(solution)/shard_map/ppermute | solution.py:303
  162.0 6.2 %collective-permute-start.11 = (f32[16,768]{1,0:T(8,128)S(1)}, f32[16,768]{1,0:T(8,128)S(1)}, u32[]{:S(2)}, u32[]{:S(2)}) collective-permute-start(f32[16,768]{1,0:T(8,128)S(1)} %get-tuple-element.31), channel_id=1, source_target_pairs={{1,0},{2,1},{3,2},{4,3},{5,4},{6,5},{7,6},{8,7},{9,8},{10,9},{11,1... | collective-permute-start | bytes 147464 | tf_op jit(solution)/shard_map/ppermute | solution.py:304
  166.4 2.4 %copy-start.5 = (f32[16,384]{1,0:T(8,128)S(1)}, f32[16,384]{1,0:T(8,128)}, u32[]{:S(2)}) copy-start(f32[16,384]{1,0:T(8,128)} %copy-done.3) | copy-start | bytes 73732
  166.4 2.4 %copy-start.8 = (f32[16,384]{1,0:T(8,128)S(1)}, f32[16,384]{1,0:T(8,128)}, u32[]{:S(2)}) copy-start(f32[16,384]{1,0:T(8,128)} %copy-done.6) | copy-start | bytes 73732

commit v2 on v0

v2 whole, which is shorter than its diff:
```python
import functools
import math

import jax
import jax.numpy as jnp
import ml_dtypes
import numpy as np
from jax import lax
from jax.experimental import pallas as pl
from jax.experimental.pallas import tpu as pltpu
from jax.sharding import PartitionSpec as P

LOADING = 1.0
F32 = jnp.float32
BF16 = jnp.bfloat16
GROUP = 8
VMEM = 48 << 20
CHUNKS = ((2, 0, 0), (2, 1, 0), (3, 0, 0), (3, 0, 0), (2, 0, 1))
STEPS = (
    (0, 0), (1, 0), (0, 1), (2, 0), (1, 1), (3, 0), (2, 1), (0, 2), (1, 2), (4, 0), (3, 1), (0, 3), (2, 2), (1, 3),
    (0, 4), (4, 1), (2, 3), (3, 2), (1, 4), (2, 4), (3, 3), (4, 2), (4, 3), (3, 4), ("halo", 0), ("gram", 0), (4, 4),
)


def block_at(strides):
    count = len(strides)
    blocks = []
    for position in range(1 << count):
        blocks.append(sum(s for i, s in enumerate(strides) if position >> (count - 1 - i) & 1))
    return blocks


def row_order(strides, bins_here, extra):
    rows = []
    for block in block_at(strides):
        for j in range(-extra, bins_here + extra):
            rows += [(block, 2 * j), (block, 2 * j + 1)]
    return np.array(rows, np.int32)


def doppler_table(pulses):
    index = np.arange(pulses)
    angles = (-2.0 * math.pi / pulses * (index[:, None] * index[None, :] % pulses)).astype(np.float32)
    cosine = np.cos(angles) / np.float32(math.sqrt(pulses))
    sine_part = np.sin(angles) / np.float32(math.sqrt(pulses))
    real_row = np.concatenate([cosine, -sine_part], axis=1)
    imag_row = np.concatenate([sine_part, cosine], axis=1)
    table = np.stack([real_row, imag_row], axis=1).reshape(2 * pulses, 2 * pulses)
    return table.astype(ml_dtypes.bfloat16)


def beam_picks(beams):
    picks = np.zeros((2, GROUP * 2 * beams, 2 * beams), np.float32)
    for g in range(GROUP):
        for b in range(beams):
            re_row, im_row = g * 2 * beams + b, g * 2 * beams + beams + b
            picks[0, re_row, b] = 1
            picks[0, im_row, beams + b] = 1
            picks[1, re_row, beams + b] = -1
            picks[1, im_row, b] = 1
    return picks.astype(ml_dtypes.bfloat16)


def dot(a, b):
    return jnp.dot(a, b, preferred_element_type=F32)


def front_kernel(
    bins_chip, me_ref, order_ref, natural_ref, picks_ref, beam_ref, mine_ref, theirs_ref,
    send_ref, keep_ref, table_ref, weights_ref, spectra_ref,
):
    elem_dev = mine_ref.shape[0]
    groups = spectra_ref.shape[0]
    width = mine_ref.shape[-1]
    rows_in = natural_ref.shape[0]

    @pl.when(pl.program_id(0) == 0)
    def _():
        me = me_ref[0]
        order = order_ref[...]
        source = jnp.bitwise_xor(order[:, 0:1], me // 2) * (2 * bins_chip) + order[:, 1:2]
        source = lax.rem(source + rows_in, rows_in)
        lane = lax.broadcasted_iota(jnp.int32, (order.shape[0], rows_in), 1)
        picked = jnp.where(source == lane, 1.0, 0.0).astype(BF16)
        table_ref[...] = dot(picked, natural_ref[...]).astype(BF16)
        parts = beam_ref[...].astype(F32)
        parts = jnp.concatenate([parts[:, 0], parts[:, 1]], axis=0).astype(BF16)
        elements = parts.shape[1]
        columns = weights_ref.shape[1]
        row = lax.broadcasted_iota(jnp.int32, (elements, columns), 0)
        column = lax.broadcasted_iota(jnp.int32, (elements, columns), 1)
        held = column // (2 * GROUP)
        first = jnp.where(held < elem_dev, me, jnp.bitwise_xor(me, 1)) * elem_dev
        here = row == first + held % elem_dev
        total = jnp.zeros(weights_ref.shape, F32)
        for part in range(2):
            spread = jnp.where(here & (column % 2 == part), 1.0, 0.0).astype(BF16)
            total += dot(dot(picks_ref[part], parts).astype(BF16), spread)
        row = lax.broadcasted_iota(jnp.int32, weights_ref.shape, 0)
        column = lax.broadcasted_iota(jnp.int32, weights_ref.shape, 1)
        same = row // (weights_ref.shape[0] // GROUP) == column % (2 * GROUP) // 2
        weights_ref[...] = jnp.where(same, total, 0.0).astype(BF16)

    table = table_ref[...]
    for e in range(2 * elem_dev):
        spectra = dot(table, mine_ref[e] if e < elem_dev else theirs_ref[e - elem_dev])
        spectra_ref[:, e] = spectra.astype(BF16).reshape(groups, 2 * GROUP, width)
    weights = weights_ref[...]
    rows = weights.shape[0]
    for g in range(groups):
        sums = dot(weights, spectra_ref[g].reshape(-1, width))
        at = g % (groups // 2) * rows
        if g < groups // 2:
            keep_ref[at : at + rows] = sums
        else:
            send_ref[at : at + rows] = sums.astype(BF16)


def front(me, strides, extra, bins_chip, beam_weights, echo, theirs, start, width):
    elem_dev, rows_in, gate_count = echo.shape
    size = theirs.shape[2]
    beams = beam_weights.shape[0]
    order = row_order([s // 2 for s in strides], bins_chip, extra)
    natural = doppler_table(rows_in // 2)
    picks = beam_picks(beams)
    table_rows = order.shape[0]
    groups = table_rows // 2 // GROUP
    half = table_rows // 4 * 2 * beams
    first, across = start // width, gate_count // 2 // width
    block_rows, block_columns = GROUP * 2 * beams, elem_dev * 4 * GROUP
    whole = lambda shape: pl.BlockSpec(shape, lambda i, me: (0,) * len(shape))
    echo_block = (elem_dev, rows_in, width)
    return pl.pallas_call(
        functools.partial(front_kernel, bins_chip),
        grid_spec=pltpu.PrefetchScalarGridSpec(
            num_scalar_prefetch=1,
            grid=(size // width,),
            in_specs=[
                whole(order.shape),
                whole(natural.shape),
                whole(picks.shape),
                whole(beam_weights.shape),
                pl.BlockSpec(echo_block, lambda i, me: (0, 0, me[0] % 2 * across + first + i)),
                pl.BlockSpec(echo_block, lambda i, me: (0, 0, i)),
            ],
            out_specs=[
                pl.BlockSpec((half, width), lambda i, me: (0, i)),
                pl.BlockSpec((half, width), lambda i, me: (0, i)),
            ],
            scratch_shapes=[
                pltpu.VMEM((table_rows, rows_in), BF16),
                pltpu.VMEM((block_rows, block_columns), BF16),
                pltpu.VMEM((groups, 2 * elem_dev, 2 * GROUP, width), BF16),
            ],
        ),
        out_shape=[
            jax.ShapeDtypeStruct((half, size), BF16),
            jax.ShapeDtypeStruct((half, size), F32),
        ],
        compiler_params=pltpu.CompilerParams(vmem_limit_bytes=VMEM),
        cost_estimate=pl.CostEstimate(flops=1000, bytes_accessed=1000, transcendentals=0),
        name="front",
    )(me, jnp.asarray(order), jnp.asarray(natural), jnp.asarray(picks), beam_weights, echo, theirs)


def gram_sums(window, mask, rows):
    top = window.astype(BF16)
    rest = (window - top.astype(F32)).astype(BF16)
    picked_top, picked_rest = [], []
    for d in range(mask.shape[0]):
        keep = mask[d : d + 1].astype(F32).astype(BF16)
        picked_top.append(top[rows * d : rows * (d + 3)] * keep)
        picked_rest.append(rest[rows * d : rows * (d + 3)] * keep)
    left = jnp.concatenate(picked_top, axis=0)
    left_rest = jnp.concatenate(picked_rest, axis=0)
    dims = (((1,), (1,)), ((), ()))
    gram = lax.dot_general(left, top, dims, preferred_element_type=F32)
    gram += lax.dot_general(left, rest, dims, preferred_element_type=F32)
    gram += lax.dot_general(left_rest, top, dims, preferred_element_type=F32)
    return gram


def half_lanes(core, half, start, size):
    return lambda gates: pl.ds(pl.multiple_of((core ^ half) * (gates // 2) + start, 128), size)


def gram_kernel(spans, me_ref, edge_ref, mask_ref, *refs):
    parts, (gram_ref, window_ref) = refs[:-2], refs[-2:]
    rows = edge_ref.shape[0]
    inner = parts[0].shape[0]
    core = me_ref[0] % 2
    gates = mask_ref.shape[1]
    early = sum(size for _, size in spans)
    total = None
    for index, part in enumerate(parts):
        half, (start, size) = index // len(spans), spans[index % len(spans)]
        lanes = slice(start, start + size)
        inner_at = pl.multiple_of((1 - core) * rows, rows)
        edge_at = pl.multiple_of(core * inner, rows)
        window_ref[half, pl.ds(inner_at, inner), lanes] = part[...]
        edge = edge_ref[:, half * early + start : half * early + start + size]
        window_ref[half, pl.ds(edge_at, rows), lanes] = edge
        mask = mask_ref[:, half_lanes(core, half, start, size)(gates)]
        sums = gram_sums(window_ref[half, :, lanes], mask, rows)
        total = sums if total is None else total + sums
    gram_ref[...] = total


def gram_of(me, spans, mine, theirs, edge, mask):
    bins_here = mask.shape[0]
    rows = edge.shape[0]
    inner = mine[0].shape[0]
    early = sum(size for _, size in spans)
    return pl.pallas_call(
        functools.partial(gram_kernel, spans),
        in_specs=[pl.BlockSpec(memory_space=pltpu.SMEM)]
        + [pl.BlockSpec(memory_space=pltpu.VMEM)] * (2 + 2 * len(mine)),
        out_shape=[
            jax.ShapeDtypeStruct((bins_here * 3 * rows, inner + rows), F32),
            jax.ShapeDtypeStruct((2, inner + rows, early), F32),
        ],
        compiler_params=pltpu.CompilerParams(vmem_limit_bytes=VMEM),
        cost_estimate=pl.CostEstimate(flops=1000, bytes_accessed=1000, transcendentals=0),
        name="gram",
    )(me, edge, mask, *mine, *theirs)


def solve(gram, steer, bins_here, beams):
    rows, order = 2 * beams, 3 * beams
    lane = lax.broadcasted_iota(jnp.int32, (1, 1, 128), 2)
    real_lane = lane // beams % 2 == 0
    row_at = lax.broadcasted_iota(jnp.int32, (1, order, 128), 1)
    lane_at = lax.broadcasted_iota(jnp.int32, (1, order, 128), 2)
    diagonal = (lane_at // rows * beams + lane_at % beams == row_at) & (lane_at // beams % 2 == 0)
    diagonal &= lane_at < 3 * rows
    systems = []
    pad = jnp.zeros((3 * rows, 128 - 3 * rows), F32)
    for d in range(bins_here):
        block = gram[3 * rows * d : 3 * rows * (d + 1), rows * d : rows * (d + 3)]
        block = jnp.concatenate([block, pad], axis=1)
        pieces = [block[i : i + beams] for i in range(0, 3 * rows, beams)]
        from_re = jnp.concatenate(pieces[0::2], axis=0)
        from_im = jnp.concatenate(pieces[1::2], axis=0)
        real = from_re + pltpu.roll(from_im, 128 - beams, 1)
        imag = pltpu.roll(from_im, beams, 1) - from_re
        systems.append(jnp.where(real_lane[0], real, imag))
    system = jnp.stack(systems, axis=0)
    system = jnp.where(lane < 3 * rows, system, 0.0) + jnp.where(diagonal, LOADING, 0.0)
    pick = row_at[0, :, :order] == lane_at[0, :, :order]
    target_re = jnp.sum(jnp.where(pick, steer[0:1], 0.0), axis=1, keepdims=True)[None]
    target_im = jnp.sum(jnp.where(pick, steer[1:2], 0.0), axis=1, keepdims=True)[None]
    system = jnp.where(lane == 3 * rows, target_re, system)
    system = jnp.where(lane == 3 * rows + beams, target_im, system)

    def swapped(row):
        return jnp.where(real_lane, -pltpu.roll(row, 128 - beams, 2), pltpu.roll(row, beams, 2))

    for k in range(order):
        spot = k // beams * rows + k % beams
        pivot_row = system[:, k : k + 1, :]
        pivot_row = pivot_row / pivot_row[:, :, spot : spot + 1]
        factor_re = system[:, :, spot : spot + 1]
        factor_im = system[:, :, spot + beams : spot + beams + 1]
        changed = system - factor_re * pivot_row - factor_im * swapped(pivot_row)
        system = jnp.where(row_at == k, pivot_row, changed)

    solved_re = system[:, :, 3 * rows : 3 * rows + 1]
    solved_im = system[:, :, 3 * rows + beams : 3 * rows + beams + 1]
    response = jnp.sum(solved_re * target_re + solved_im * target_im, axis=1, keepdims=True)
    weight_re = jnp.broadcast_to(solved_re / response, (bins_here, order, 128))
    weight_im = jnp.broadcast_to(solved_im / response, (bins_here, order, 128))
    return weight_re, weight_im


def filter_gates(out_ref, at, blocks, weight_re, weight_im, beams):
    for d in range(weight_re.shape[0]):
        total_re = jnp.zeros((beams, 128), F32)
        total_im = jnp.zeros((beams, 128), F32)
        for w in range(3):
            coeff_re = weight_re[d, w * beams : (w + 1) * beams]
            coeff_im = weight_im[d, w * beams : (w + 1) * beams]
            snap_re, snap_im = blocks[2 * (d + w)], blocks[2 * (d + w) + 1]
            total_re += coeff_re * snap_re + coeff_im * snap_im
            total_im += coeff_re * snap_im - coeff_im * snap_re
        row_re = jnp.sum(total_re, axis=0, keepdims=True)
        row_im = jnp.sum(total_im, axis=0, keepdims=True)
        out_ref[d, :, at] = jnp.concatenate([row_re, row_im], axis=0)


def tail_kernel(me_ref, steer_ref, gram_ref, window_ref, mask_ref, *refs):
    parts, out_ref = refs[:-1], refs[-1]
    bins_here, gates = mask_ref.shape
    rows = window_ref.shape[1] // (bins_here + 2)
    beams = rows // 2
    core = me_ref[0] % 2
    pieces = [(0, 0, window_ref.at[0]), (1, 0, window_ref.at[1])]
    gram = gram_ref[...]
    count = len(parts) // 2
    for half in range(2):
        start = window_ref.shape[2]
        for ref in parts[half * count : (half + 1) * count]:
            size = ref.shape[1]
            mask = mask_ref[:, half_lanes(core, half, start, size)(gates)]
            gram += gram_sums(ref[...], mask, rows)
            pieces.append((half, start, ref))
            start += size
    weight_re, weight_im = solve(gram, steer_ref[...], bins_here, beams)

    def split(value):
        return [value[i : i + beams] for i in range(0, value.shape[0], beams)]

    for half, start, ref in pieces:
        for at in range(0, ref.shape[1], 128):
            lanes = half_lanes(core, half, start + at, 128)(gates)
            blocks = split(ref[:, at : at + 128])
            filter_gates(out_ref, lanes, blocks, weight_re, weight_im, beams)


def tail(me, steer, gram, window, mask, mine, theirs):
    bins_here, gates = mask.shape
    parts = mine + theirs
    return pl.pallas_call(
        tail_kernel,
        in_specs=[pl.BlockSpec(memory_space=pltpu.SMEM)]
        + [pl.BlockSpec(memory_space=pltpu.VMEM)] * (4 + len(parts)),
        out_shape=jax.ShapeDtypeStruct((bins_here, 2, gates), F32),
        compiler_params=pltpu.CompilerParams(vmem_limit_bytes=VMEM),
        cost_estimate=pl.CostEstimate(flops=1000, bytes_accessed=1000, transcendentals=0),
        name="tail",
    )(me, steer, gram, window, mask, *parts)


def slice_kernel(me_ref, echo_ref, part_ref):
    part_ref[...] = echo_ref[...]


def other_half(me, echo, start, size):
    elem_dev, rows_in, gate_count = echo.shape
    first, across = start // 128, gate_count // 2 // 128
    block = (elem_dev, rows_in, 128)
    return pl.pallas_call(
        slice_kernel,
        grid_spec=pltpu.PrefetchScalarGridSpec(
            num_scalar_prefetch=1,
            grid=(size // 128,),
            in_specs=[pl.BlockSpec(block, lambda i, me: (0, 0, (1 - me[0] % 2) * across + first + i))],
            out_specs=pl.BlockSpec(block, lambda i, me: (0, 0, i)),
        ),
        out_shape=jax.ShapeDtypeStruct((elem_dev, rows_in, size), BF16),
        compiler_params=pltpu.CompilerParams(vmem_limit_bytes=VMEM),
        cost_estimate=pl.CostEstimate(flops=1000, bytes_accessed=1000, transcendentals=0),
        name="slice",
    )(me, echo)


def swap(x, stride, count):
    return lax.ppermute(x, "elem", [(i, i ^ stride) for i in range(count)])


def share(keep, received, part):
    total = keep[part]
    for got in received:
        total = total + got[part].astype(F32)
    return total


class Chain:
    def __init__(self):
        self.last = None

    def enter(self, value):
        if self.last is None:
            return value
        value, _ = lax.optimization_barrier((value, self.last))
        return value

    def leave(self, value):
        self.last = value
        return value


def local(raw_echo, beam_weights, steer, train_mask):
    elem_dev, _, pulses, gate_count = raw_echo.shape
    count = lax.axis_size("elem")
    me = lax.axis_index("elem").astype(jnp.int32)
    core = me % 2
    at = me.reshape(1)
    bins_here = pulses // count
    rows = 2 * beam_weights.shape[0]
    echo = raw_echo.reshape(elem_dev, 2 * pulses, gate_count)
    levels = count.bit_length() - 1
    plain = [2 << i for i in range(levels - 1)]
    orders = [plain, plain[1:] + plain[:1]]
    unit = gate_count // 2 // sum(width for width, _, _ in CHUNKS)
    chunks = len(CHUNKS)
    last = sum(1 - wide for _, _, wide in CHUNKS)
    spans = []
    for width, _, _ in CHUNKS:
        start = sum(spans[-1]) if spans else 0
        spans.append((start, width * unit))
    early = tuple(spans[:last])
    theirs = [None] * chunks
    keeps, received = [None] * chunks, [[] for _ in CHUNKS]
    near, far = [None] * chunks, [None] * chunks
    chain = Chain()
    edge = gram = window = None

    steps = []
    for c, stage in STEPS:
        if stage == 3:
            steps += [(c, later) for later in range(3, levels)]
        else:
            steps.append((c, levels if stage == 4 else stage))
    for c, stage in steps:
        if c == "halo":
            edges = [
                lax.dynamic_slice_in_dim(x, core * bins_here * rows, rows, 0)
                for x in far[:last] + near[:last]
            ]
            pairs = [((i + 1) % count, i) for i in range(1, count, 2)]
            pairs += [(i, (i + 1) % count) for i in range(1, count, 2)]
            edge = lax.ppermute(jnp.concatenate(edges, axis=1), "elem", pairs)
        elif c == "gram":
            gram, window = gram_of(at, early, near[:last], far[:last], edge, chain.enter(train_mask))
            chain.leave(gram)
        elif stage == 0:
            part = chain.leave(other_half(at, chain.enter(echo), *spans[c]))
            theirs[c] = swap(part, 1, count)
        elif stage == 1:
            start, size = spans[c]
            strides = orders[CHUNKS[c][1]]
            width = math.gcd(size, start, gate_count // 2)
            send, keeps[c] = front(
                at, strides, CHUNKS[c][2], 2 * bins_here, beam_weights,
                chain.enter(echo), theirs[c], start, width,
            )
            chain.leave(send)
            received[c].append(swap(send, strides[0], count))
        elif stage < levels:
            half = keeps[c].shape[0] >> (stage - 1)
            total = share(chain.enter(keeps[c]), received[c], slice(half, 2 * half))
            send = chain.leave(total.astype(BF16))
            received[c].append(swap(send, orders[CHUNKS[c][1]][stage - 1], count))
        else:
            held = keeps[c].shape[0] >> (levels - 2)
            total = chain.leave(share(chain.enter(keeps[c]), received[c], slice(0, held)))
            step = (bins_here - 1 + CHUNKS[c][2]) * rows
            near[c] = lax.dynamic_slice_in_dim(total, core * step, held - step, 0)
            send = lax.dynamic_slice_in_dim(total, (1 - core) * step, held - step, 0)
            far[c] = swap(send, 1, count)
    return tail(at, steer, gram, window, train_mask, near[last:], far[last:])


def solution(mesh):
    return jax.shard_map(
        local,
        mesh=mesh,
        in_specs=(P(("cpi", "elem"), None, None, None), P(), P(), P(("cpi", "elem"), None)),
        out_specs=P(("cpi", "elem"), None, None),
        check_vma=False,
    )
```

time: 405 us -> 124 us (0.31)
  waiting for transfers between devices: 249 us -> 39.8 us
  other arithmetic: 69.2 us -> 11.1 us
  matrix products: 52.9 us -> 0 us
  Pallas kernels: 0 us -> 38.2 us
  starting transfers between devices: 4.49 us -> 28.1 us
  between operations: 13.7 us -> 0.33 us
  local copies, waits for them, and re-layouts: 14.5 us -> 6.12 us
    reduce_scatter x1 -> x0, waiting for transfers between devices: 246 us -> none  [local(): lax.psum_scatter(jnp.einsum('ok,dkg->dog', columns, spectra_rows, preferr...]
    another operation x15 -> x0, other arithmetic: 68.1 us -> none  [the longest x4 35.6 us: adapt(): factor = jnp.linalg.cholesky(system)]
    dot_general x7 -> x0, matrix products: 52.2 us -> none  [the longest x1 27.2 us: local(): jnp.einsum('ok,dkg->dog', columns, spectra_rows, preferred_element_type=j...]
    pallas_call x0 -> x12, Pallas kernels: none -> 38.2 us  [the longest x5 19.5 us: front(): pl.pallas_call(functools.partial(front_kernel, bins_chip), grid_spec=pltp...]
    ppermute x2 -> x26, waiting for transfers between devices: 3.43 us -> 39.8 us  [the longest x25 34.1 us: swap(): return lax.ppermute(x, 'elem', [(i, i ^ stride) for i in range(count)])]
    ppermute x2 -> x26, starting transfers between devices: 4.49 us -> 28.1 us  [the longest x25 24.8 us: swap(): return lax.ppermute(x, 'elem', [(i, i ^ stride) for i in range(count)])]
    convert_element_type x1 -> x0, local copies, waits for them, and re-layouts: 10.6 us -> none  [local(): spectra_rows = jnp.einsum('dcr,erg->decg', dft_table, echo_rows, preferre...]
    convert_element_type x2 -> x10, other arithmetic: 0.01 us -> 6.98 us  [local(): send = chain.leave(total.astype(BF16))]
  transfers between devices with their start and end apart: 3 -> 26, of which waited for: 2 -> 15; matrix products, arithmetic and copies ran while one was open for 0% -> 10% of each run, Pallas kernels for 0% -> 25%
where the time goes in v2:
time: 124 us
  waiting for transfers between devices  39.8 us (32%)
  Pallas kernels  38.2 us (31%)
  starting transfers between devices  28.1 us (23%)
  other arithmetic  11.1 us (9%)
  local copies, waits for them, and re-layouts  6.12 us (5%)
    ppermute x25, waiting for transfers between devices, swap(): return lax.ppermute(x, 'elem', [(i, i ^ stride) for i in range(count)])  34.1 us
    ppermute x25, starting transfers between devices, swap(): return lax.ppermute(x, 'elem', [(i, i ^ stride) for i in range(count)])  24.8 us
    pallas_call x5, Pallas kernels, front(): pl.pallas_call(functools.partial(front_kernel, bins_chip), grid_spec=pltp...  19.5 us
    pallas_call x5, Pallas kernels, other_half(): pl.pallas_call(slice_kernel, grid_spec=pltpu.PrefetchScalarGridSpec(num_s...  10.3 us
    convert_element_type x10, other arithmetic, local(): send = chain.leave(total.astype(BF16))  6.98 us
    pallas_call x1, Pallas kernels, tail(): pl.pallas_call(tail_kernel, in_specs=[pl.BlockSpec(memory_space=pltpu.SME...  6.3 us
    ppermute x1, waiting for transfers between devices, local(): edge = lax.ppermute(jnp.concatenate(edges, axis=1), 'elem', pairs)  5.72 us
    unnamed x37, local copies, waits for them, and re-layouts  5.35 us
  transfers between devices with their start and end apart: 26, of which 15 were waited for; matrix products, arithmetic and copies ran while one was open for 10% of the time, Pallas kernels for 25%

profile of v2, /device:TPU:0, one launch (start us, length us, event | category | flops | bytes accessed | tf_op | source)
XLA Modules:
  0.0 123.6 jit_solution(12693310635171545726)
XLA Ops:
  0.0 1.4 %slice.230 = bf16[8,256,256]{2,1,0:T(8,128)(2,1)S(1)} custom-call(s32[1]{0:T(128)} %bitcast.me_ref, bf16[8,256,3072]{2,1,0:T(8,128)(2,1)} %bitcast.2), custom_call_target="tpu_custom_call" | custom-call | flops 1000 | bytes 1000 | tf_op jit(solution)/shard_map/slice/pallas_call | solution.py:341
  1.4 0.5 collective-permute-start
  1.9 1.4 %slice.231 = bf16[8,256,256]{2,1,0:T(8,128)(2,1)S(1)} custom-call(s32[1]{0:T(128)} %bitcast.me_ref, bf16[8,256,3072]{2,1,0:T(8,128)(2,1)} %bitcast.3), custom_call_target="tpu_custom_call" | custom-call | flops 1000 | bytes 1000 | tf_op jit(solution)/shard_map/slice/pallas_call | solution.py:341
  3.4 0.8 collective-permute-done.theirs_ref
  4.2 2.6 %front.5 = (bf16[1024,256]{1,0:T(8,128)(2,1)S(1)}, f32[1024,256]{1,0:T(8,128)S(1)}) custom-call(s32[1]{0:T(128)} %bitcast.me_ref, s32[256,2]{1,0:T(8,128)S(1)} %copy-done.2, bf16[256,256]{1,0:T(8,128)(2,1)S(1)} %copy-done, bf16[2,128,16]{2,1,0:T(8,128)(2,1)S(1)} %copy-done.1, bf16[8,2,128]{2,1,0:T(2,128)(2,1)S(1)} %copy-done.10, ...), custom_call_target="tpu_custom_call" | custom-call | flops 1000 | bytes 1000 | tf_op jit(solution)/shard_map/front/pallas_call | solution.py:133
  6.9 2.8 %slice.232 = bf16[8,256,384]{2,1,0:T(8,128)(2,1)S(1)} custom-call(s32[1]{0:T(128)} %bitcast.me_ref, bf16[8,256,3072]{2,1,0:T(8,128)(2,1)} %bitcast.5), custom_call_target="tpu_custom_call" | custom-call | flops 1000 | bytes 1000 | tf_op jit(solution)/shard_map/slice/pallas_call | solution.py:341
  9.7 0.4 collective-permute-start.2
  10.1 3.4 %front.6 = (bf16[1024,256]{1,0:T(8,128)(2,1)}, f32[1024,256]{1,0:T(8,128)S(1)}) custom-call(s32[1]{0:T(128)} %bitcast.me_ref, s32[256,2]{1,0:T(8,128)S(1)} %copy-done.9, bf16[256,256]{1,0:T(8,128)(2,1)S(1)} %copy-done, bf16[2,128,16]{2,1,0:T(8,128)(2,1)S(1)} %copy-done.1, bf16[8,2,128]{2,1,0:T(2,128)(2,1)S(1)} %copy-done.10, bf16[8,256,3072]{2,1,0:T(8,128)(2,1)} %bitcast.6, ...), custom_call_target="tpu_custom_call" | custom-call | flops 1000 | bytes 1000 | tf_op jit(solution)/shard_map/front/pallas_call | solution.py:133
  13.5 1.0 copy-done.3
  14.5 3.4 %slice.233 = bf16[8,256,384]{2,1,0:T(8,128)(2,1)} custom-call(s32[1]{0:T(128)} %bitcast.me_ref, bf16[8,256,3072]{2,1,0:T(8,128)(2,1)} %bitcast.7), custom_call_target="tpu_custom_call" | custom-call | flops 1000 | bytes 1000 | tf_op jit(solution)/shard_map/slice/pallas_call | solution.py:341
  18.0 2.9 %collective-permute-start.3 = (bf16[1024,256]{1,0:T(8,128)(2,1)S(1)}, bf16[1024,256]{1,0:T(8,128)(2,1)S(1)}, u32[]{:S(2)}, u32[]{:S(2)}) collective-permute-start(bf16[1024,256]{1,0:T(8,128)(2,1)S(1)} %get-tuple-element.45), channel_id=1, source_target_pairs={{0,2},{1,3},{2,0},{3,1},{4,6},{5,7},{6,4},{7,5},{8,10},{9,11},{10,... | collective-permute-start | bytes 1572872 | tf_op jit(solution)/shard_map/ppermute | solution.py:357
  20.9 1.6 %collective-permute-start.4 = (bf16[1024,256]{1,0:T(8,128)(2,1)}, bf16[1024,256]{1,0:T(8,128)(2,1)}, u32[]{:S(2)}, u32[]{:S(2)}) collective-permute-start(bf16[1024,256]{1,0:T(8,128)(2,1)} %get-tuple-element.49), channel_id=1, source_target_pairs={{0,4},{1,5},{2,6},{3,7},{4,0},{5,1},{6,2},{7,3},{8,12},{9,13},{10,... | collective-permute-start | bytes 1572872 | tf_op jit(solution)/shard_map/ppermute | solution.py:357
  22.5 5.5 %front.7 = (bf16[1024,384]{1,0:T(8,128)(2,1)}, f32[1024,384]{1,0:T(8,128)S(1)}) custom-call(s32[1]{0:T(128)} %bitcast.me_ref, s32[256,2]{1,0:T(8,128)S(1)} %copy-done.2, bf16[256,256]{1,0:T(8,128)(2,1)S(1)} %copy-done, bf16[2,128,16]{2,1,0:T(8,128)(2,1)S(1)} %copy-done.1, bf16[8,2,128]{2,1,0:T(2,128)(2,1)S(1)} %copy-done.10, bf16[8,256,3072]{2,1,0:T(8,128)(2,1)} %bitcast.8, ...), custom_call_target="tpu_custom_call" | custom-call | flops 1000 | bytes 1000 | tf_op jit(solution)/shard_map/front/pallas_call | solution.py:133
  28.1 0.5 collective-permute-start.7
  28.6 5.1 %collective-permute-done.3 = bf16[1024,256]{1,0:T(8,128)(2,1)S(1)} collective-permute-done((bf16[1024,256]{1,0:T(8,128)(2,1)S(1)}, bf16[1024,256]{1,0:T(8,128)(2,1)S(1)}, u32[]{:S(2)}, u32[]{:S(2)}) %collective-permute-start.3) | collective-permute-done | bytes 524320 | tf_op jit(solution)/shard_map/ppermute | solution.py:357
  33.6 0.9 add_convert_fusion.4
  34.5 2.1 %collective-permute-start.6 = (bf16[512,256]{1,0:T(8,128)(2,1)}, bf16[512,256]{1,0:T(8,128)(2,1)}, u32[]{:S(2)}, u32[]{:S(2)}) collective-permute-start(bf16[512,256]{1,0:T(8,128)(2,1)} %add_convert_fusion.4), channel_id=1, source_target_pairs={{0,4},{1,5},{2,6},{3,7},{4,0},{5,1},{6,2},{7,3},{8,12},{9,13},{10,... | collective-permute-start | bytes 786440 | tf_op jit(solution)/shard_map/ppermute | solution.py:357
  36.6 1.2 add_convert_fusion.3
  37.8 2.7 %collective-permute-start.8 = (bf16[512,256]{1,0:T(8,128)(2,1)S(1)}, bf16[512,256]{1,0:T(8,128)(2,1)S(1)}, u32[]{:S(2)}, u32[]{:S(2)}) collective-permute-start(bf16[512,256]{1,0:T(8,128)(2,1)S(1)} %add_convert_fusion.3), channel_id=1, source_target_pairs={{0,8},{1,9},{2,10},{3,11},{4,12},{5,13},{6,14},{7,15},{8,0},{9,1},... | collective-permute-start | bytes 786440 | tf_op jit(solution)/shard_map/ppermute | solution.py:357
  40.5 1.4 %slice.234 = bf16[8,256,256]{2,1,0:T(8,128)(2,1)S(1)} custom-call(s32[1]{0:T(128)} %bitcast.me_ref, bf16[8,256,3072]{2,1,0:T(8,128)(2,1)} %bitcast.9), custom_call_target="tpu_custom_call" | custom-call | flops 1000 | bytes 1000 | tf_op jit(solution)/shard_map/slice/pallas_call | solution.py:341
  42.0 5.3 %front.8 = (bf16[1024,384]{1,0:T(8,128)(2,1)S(1)}, f32[1024,384]{1,0:T(8,128)S(1)}) custom-call(s32[1]{0:T(128)} %bitcast.me_ref, s32[256,2]{1,0:T(8,128)S(1)} %copy-done.2, bf16[256,256]{1,0:T(8,128)(2,1)S(1)} %copy-done, bf16[2,128,16]{2,1,0:T(8,128)(2,1)S(1)} %copy-done.1, bf16[8,2,128]{2,1,0:T(2,128)(2,1)S(1)} %copy-done.10, ...), custom_call_target="tpu_custom_call" | custom-call | flops 1000 | bytes 1000 | tf_op jit(solution)/shard_map/front/pallas_call | solution.py:133
  47.2 1.6 %collective-permute-start.13 = (bf16[1024,384]{1,0:T(8,128)(2,1)S(1)}, bf16[1024,384]{1,0:T(8,128)(2,1)S(1)}, u32[]{:S(2)}, u32[]{:S(2)}) collective-permute-start(bf16[1024,384]{1,0:T(8,128)(2,1)S(1)} %get-tuple-element.58), channel_id=1, source_target_pairs={{0,2},{1,3},{2,0},{3,1},{4,6},{5,7},{6,4},{7,5},{8,10},{9,11},{10,... | collective-permute-start | bytes 2359304 | tf_op jit(solution)/shard_map/ppermute | solution.py:357
  48.9 0.9 add_convert_fusion.9
  49.8 0.4 collective-permute-start.9
  50.2 1.1 add_convert_fusion.1
  51.4 2.5 %collective-permute-start.12 = (bf16[512,384]{1,0:T(8,128)(2,1)S(1)}, bf16[512,384]{1,0:T(8,128)(2,1)S(1)}, u32[]{:S(2)}, u32[]{:S(2)}) collective-permute-start(bf16[512,384]{1,0:T(8,128)(2,1)S(1)} %add_convert_fusion.1), channel_id=1, source_target_pairs={{0,4},{1,5},{2,6},{3,7},{4,0},{5,1},{6,2},{7,3},{8,12},{9,13},{10,... | collective-permute-start | bytes 1179656 | tf_op jit(solution)/shard_map/ppermute | solution.py:357
  53.9 0.9 add_convert_fusion.8
  54.8 1.6 %collective-permute-start.14 = (bf16[256,256]{1,0:T(8,128)(2,1)S(1)}, bf16[256,256]{1,0:T(8,128)(2,1)S(1)}, u32[]{:S(2)}, u32[]{:S(2)}) collective-permute-start(bf16[256,256]{1,0:T(8,128)(2,1)S(1)} %add_convert_fusion.8), channel_id=1, source_target_pairs={{0,2},{1,3},{2,0},{3,1},{4,6},{5,7},{6,4},{7,5},{8,10},{9,11},{10,... | collective-permute-start | bytes 393224 | tf_op jit(solution)/shard_map/ppermute | solution.py:357
  56.4 2.6 %collective-permute-done.9 = bf16[256,256]{1,0:T(8,128)(2,1)S(1)} collective-permute-done((bf16[256,256]{1,0:T(8,128)(2,1)S(1)}, bf16[256,256]{1,0:T(8,128)(2,1)S(1)}, u32[]{:S(2)}, u32[]{:S(2)}) %collective-permute-start.9) | collective-permute-done | bytes 131104 | tf_op jit(solution)/shard_map/ppermute | solution.py:357
  59.0 1.0 convert_add_fusion.4
  60.1 2.7 %front.9 = (bf16[1152,256]{1,0:T(8,128)(2,1)S(1)}, f32[1152,256]{1,0:T(8,128)S(1)}) custom-call(s32[1]{0:T(128)} %bitcast.me_ref, s32[288,2]{1,0:T(8,128)S(1)} %copy-done.8, bf16[256,256]{1,0:T(8,128)(2,1)S(1)} %copy-done, bf16[2,128,16]{2,1,0:T(8,128)(2,1)S(1)} %copy-done.1, bf16[8,2,128]{2,1,0:T(2,128)(2,1)S(1)} %copy-done.10, ...), custom_call_target="tpu_custom_call" | custom-call | flops 1000 | bytes 1000 | tf_op jit(solution)/shard_map/front/pallas_call | solution.py:133
  62.8 0.6 collective-permute-start.19
  63.4 1.6 %collective-permute-done.12 = bf16[512,384]{1,0:T(8,128)(2,1)S(1)} collective-permute-done((bf16[512,384]{1,0:T(8,128)(2,1)S(1)}, bf16[512,384]{1,0:T(8,128)(2,1)S(1)}, u32[]{:S(2)}, u32[]{:S(2)}) %collective-permute-start.12) | collective-permute-done | bytes 393248 | tf_op jit(solution)/shard_map/ppermute | solution.py:357
  65.0 1.0 add_convert_fusion.6
  66.2 1.4 %collective-permute-done.13 = bf16[1024,384]{1,0:T(8,128)(2,1)S(1)} collective-permute-done((bf16[1024,384]{1,0:T(8,128)(2,1)S(1)}, bf16[1024,384]{1,0:T(8,128)(2,1)S(1)}, u32[]{:S(2)}, u32[]{:S(2)}) %collective-permute-start.13) | collective-permute-done | bytes 786464 | tf_op jit(solution)/shard_map/ppermute | solution.py:357
  67.8 1.8 %collective-permute-start.18 = (bf16[512,384]{1,0:T(8,128)(2,1)S(1)}, bf16[512,384]{1,0:T(8,128)(2,1)S(1)}, u32[]{:S(2)}, u32[]{:S(2)}) collective-permute-start(bf16[512,384]{1,0:T(8,128)(2,1)S(1)} %add_convert_fusion), channel_id=1, source_target_pairs={{0,4},{1,5},{2,6},{3,7},{4,0},{5,1},{6,2},{7,3},{8,12},{9,13},{10,... | collective-permute-start | bytes 1179656 | tf_op jit(solution)/shard_map/ppermute | solution.py:357
  69.6 0.9 collective-permute-done.14
  70.5 1.0 convert_add_fusion.3
  71.4 5.3 %collective-permute-done.16 = bf16[256,384]{1,0:T(8,128)(2,1)S(1)} collective-permute-done((bf16[256,384]{1,0:T(8,128)(2,1)S(1)}, bf16[256,384]{1,0:T(8,128)(2,1)S(1)}, u32[]{:S(2)}, u32[]{:S(2)}) %collective-permute-start.16) | collective-permute-done | bytes 196640 | tf_op jit(solution)/shard_map/ppermute | solution.py:357
  76.7 1.0 convert_add_fusion.1
  77.7 4.2 %collective-permute-done.18 = bf16[512,384]{1,0:T(8,128)(2,1)S(1)} collective-permute-done((bf16[512,384]{1,0:T(8,128)(2,1)S(1)}, bf16[512,384]{1,0:T(8,128)(2,1)S(1)}, u32[]{:S(2)}, u32[]{:S(2)}) %collective-permute-start.18) | collective-permute-done | bytes 393248 | tf_op jit(solution)/shard_map/ppermute | solution.py:357
  82.0 0.5 collective-permute-done.19
  82.7 1.6 %collective-permute-start.20 = (bf16[576,256]{1,0:T(8,128)(2,1)S(1)}, bf16[576,256]{1,0:T(8,128)(2,1)S(1)}, u32[]{:S(2)}, u32[]{:S(2)}) collective-permute-start(bf16[576,256]{1,0:T(8,128)(2,1)S(1)} %add_convert_fusion.2), channel_id=1, source_target_pairs={{0,4},{1,5},{2,6},{3,7},{4,0},{5,1},{6,2},{7,3},{8,12},{9,13},{10,... | collective-permute-start | bytes 884744 | tf_op jit(solution)/shard_map/ppermute | solution.py:357
  84.2 0.6 constant_dynamic-update-slice_fusion.3
  85.0 0.5 collective-permute-start.17
  85.6 2.6 %collective-permute-start.21 = (bf16[256,384]{1,0:T(8,128)(2,1)S(1)}, bf16[256,384]{1,0:T(8,128)(2,1)S(1)}, u32[]{:S(2)}, u32[]{:S(2)}) collective-permute-start(bf16[256,384]{1,0:T(8,128)(2,1)S(1)} %add_convert_fusion.5), channel_id=1, source_target_pairs={{0,8},{1,9},{2,10},{3,11},{4,12},{5,13},{6,14},{7,15},{8,0},{9,1},... | collective-permute-start | bytes 589832 | tf_op jit(solution)/shard_map/ppermute | solution.py:357
  88.1 6.8 %collective-permute-done.20 = bf16[576,256]{1,0:T(8,128)(2,1)S(1)} collective-permute-done((bf16[576,256]{1,0:T(8,128)(2,1)S(1)}, bf16[576,256]{1,0:T(8,128)(2,1)S(1)}, u32[]{:S(2)}, u32[]{:S(2)}) %collective-permute-start.20) | collective-permute-done | bytes 294944 | tf_op jit(solution)/shard_map/ppermute | solution.py:357
  95.0 0.7 add_convert_fusion.7
  95.7 1.9 %collective-permute-done.21 = bf16[256,384]{1,0:T(8,128)(2,1)S(1)} collective-permute-done((bf16[256,384]{1,0:T(8,128)(2,1)S(1)}, bf16[256,384]{1,0:T(8,128)(2,1)S(1)}, u32[]{:S(2)}, u32[]{:S(2)}) %collective-permute-start.21) | collective-permute-done | bytes 196640 | tf_op jit(solution)/shard_map/ppermute | solution.py:357
  97.8 0.6 constant_dynamic-update-slice_fusion.2
  98.5 0.6 dynamic-slice_dynamic-update-slice_fusion.3
  99.1 0.2 collective-permute-done.22.refs_7_
  99.3 0.6 dynamic-slice_dynamic-update-slice_fusion.2
  99.9 0.6 constant_dynamic-update-slice_fusion.1
  100.5 0.6 constant_dynamic-update-slice_fusion
  101.1 0.6 dynamic-slice_dynamic-update-slice_fusion.1
  101.7 0.6 dynamic-slice_dynamic-update-slice_fusion
  102.3 3.3 %collective-permute-start.23 = (f32[16,2560]{1,0:T(8,128)}, f32[16,2560]{1,0:T(8,128)S(1)}, u32[]{:S(2)}, u32[]{:S(2)}) collective-permute-start(f32[16,2560]{1,0:T(8,128)} %dynamic-slice_dynamic-update-slice_fusion), channel_id=1, source_target_pairs={{2,1},{4,3},{6,5},{8,7},{10,9},{12,11},{14,13},{0,15},{1,2},{3,4},... | collective-permute-start | bytes 491528 | tf_op jit(solution)/shard_map/ppermute | solution.py:422
  105.6 5.7 %collective-permute-done.23.edge_ref = f32[16,2560]{1,0:T(8,128)S(1)} collective-permute-done((f32[16,2560]{1,0:T(8,128)}, f32[16,2560]{1,0:T(8,128)S(1)}, u32[]{:S(2)}, u32[]{:S(2)}) %collective-permute-start.23) | collective-permute-done | bytes 163872 | tf_op jit(solution)/shard_map/ppermute | solution.py:422
  111.4 2.1 %gram.1 = (f32[384,160]{1,0:T(8,128)S(1)}, f32[2,160,1280]{2,1,0:T(8,128)S(1)}) custom-call(s32[1]{0:T(128)} %bitcast.me_ref, f32[16,2560]{1,0:T(8,128)S(1)} %collective-permute-done.23.edge_ref, s32[8,3072]{1,0:T(8,128)S(1)} %copy-done.7, f32[144,256]{1,0:T(8,128)S(1)} %get-tuple-element.87.refs_0_, f32[144,256]{1,0:T(8,128)S(1)} %get-tuple-element.85.refs_1_, ...), custom_call_target="tpu_custom_call" | custom-call | flops 1000 | bytes 1000 | tf_op jit(solution)/shard_map/gram/pallas_call | solution.py:214
  113.5 1.3 %collective-permute-done.24 = bf16[288,256]{1,0:T(8,128)(2,1)} collective-permute-done((bf16[288,256]{1,0:T(8,128)(2,1)}, bf16[288,256]{1,0:T(8,128)(2,1)}, u32[]{:S(2)}, u32[]{:S(2)}) %collective-permute-start.24) | collective-permute-done | bytes 147488 | tf_op jit(solution)/shard_map/ppermute | solution.py:357
  114.8 1.1 convert_add_fusion.2
  116.0 1.4 %collective-permute-done.25.refs_1_ = f32[160,256]{1,0:T(8,128)S(1)} collective-permute-done((f32[160,256]{1,0:T(8,128)S(1)}, f32[160,256]{1,0:T(8,128)S(1)}, u32[]{:S(2)}, u32[]{:S(2)}) %collective-permute-start.25) | collective-permute-done | bytes 163872 | tf_op jit(solution)/shard_map/ppermute | solution.py:357
  117.3 6.3 %tail.1 = f32[8,2,3072]{2,1,0:T(2,128)} custom-call(s32[1]{0:T(128)} %bitcast.me_ref, f32[2,24]{1,0:T(2,128)S(1)} %copy-done.11, f32[384,160]{1,0:T(8,128)S(1)} %get-tuple-element.76.gram_ref, f32[2,160,1280]{2,1,0:T(8,128)S(1)} %get-tuple-element.77.window_ref, s32[8,3072]{1,0:T(8,128)S(1)} %copy-done.7, f32[160,256]{1,0:T(8,128)S(1)} %get-tuple-element.84.refs_0_, ...), custom_call_target="tpu_custom_call" | custom-call | flops 1000 | bytes 1000 | tf_op jit(solution)/shard_map/tail/pallas_call | solution.py:322
  (58 shorter events, 1.4 us)
Async XLA Ops:
  1.4 2.9 %copy-start = (bf16[256,256]{1,0:T(8,128)(2,1)S(1)}, bf16[256,256]{1,0:T(8,128)(2,1)}, u32[]{:S(2)}) copy-start(bf16[256,256]{1,0:T(8,128)(2,1)} %constant.79.clone.natural_ref) | copy-start | bytes 393220
  1.4 2.8 %copy-start.1 = (bf16[2,128,16]{2,1,0:T(8,128)(2,1)S(1)}, bf16[2,128,16]{2,1,0:T(8,128)(2,1)}, u32[]{:S(2)}) copy-start(bf16[2,128,16]{2,1,0:T(8,128)(2,1)} %constant.80.clone.picks_ref) | copy-start | bytes 24580
  1.4 2.8 %copy-start.2 = (s32[256,2]{1,0:T(8,128)S(1)}, s32[256,2]{1,0:T(8,128)}, u32[]{:S(2)}) copy-start(s32[256,2]{1,0:T(8,128)} %constant.78.clone.order_ref) | copy-start | bytes 6148
  1.4 2.8 %copy-start.10 = (bf16[8,2,128]{2,1,0:T(2,128)(2,1)S(1)}, bf16[8,2,128]{2,1,0:T(2,128)(2,1)}, u32[]{:S(2)}) copy-start(bf16[8,2,128]{2,1,0:T(2,128)(2,1)} %beam_ref.9) | copy-start | bytes 12292
  1.4 2.8 %collective-permute-start = (bf16[8,256,256]{2,1,0:T(8,128)(2,1)S(1)}, bf16[8,256,256]{2,1,0:T(8,128)(2,1)S(1)}, u32[]{:S(2)}, u32[]{:S(2)}) collective-permute-start(bf16[8,256,256]{2,1,0:T(8,128)(2,1)S(1)} %slice.230), channel_id=1, source_target_pairs={{0,1},{1,0},{2,3},{3,2},{4,5},{5,4},{6,7},{7,6},{8,9},{9,8},{10,11... | collective-permute-start | bytes 3145736 | tf_op jit(solution)/shard_map/ppermute | solution.py:357
  3.3 6.8 %collective-permute-start.1 = (bf16[8,256,256]{2,1,0:T(8,128)(2,1)S(1)}, bf16[8,256,256]{2,1,0:T(8,128)(2,1)S(1)}, u32[]{:S(2)}, u32[]{:S(2)}) collective-permute-start(bf16[8,256,256]{2,1,0:T(8,128)(2,1)S(1)} %slice.231), channel_id=1, source_target_pairs={{0,1},{1,0},{2,3},{3,2},{4,5},{5,4},{6,7},{7,6},{8,9},{9,8},{10,11... | collective-permute-start | bytes 3145736 | tf_op jit(solution)/shard_map/ppermute | solution.py:357
  6.8 26.8 %copy-start.5 = (f32[1024,256]{1,0:T(8,128)}, f32[1024,256]{1,0:T(8,128)S(1)}, u32[]{:S(2)}) copy-start(f32[1024,256]{1,0:T(8,128)S(1)} %get-tuple-element.62) | copy-start | bytes 3145732
  6.9 3.3 %copy-start.9 = (s32[256,2]{1,0:T(8,128)S(1)}, s32[256,2]{1,0:T(8,128)}, u32[]{:S(2)}) copy-start(s32[256,2]{1,0:T(8,128)} %constant.81.clone.order_ref) | copy-start | bytes 6148
  9.7 12.8 %collective-permute-start.2 = (bf16[8,256,384]{2,1,0:T(8,128)(2,1)S(1)}, bf16[8,256,384]{2,1,0:T(8,128)(2,1)S(1)}, u32[]{:S(2)}, u32[]{:S(2)}) collective-permute-start(bf16[8,256,384]{2,1,0:T(8,128)(2,1)S(1)} %slice.232), channel_id=1, source_target_pairs={{0,1},{1,0},{2,3},{3,2},{4,5},{5,4},{6,7},{7,6},{8,9},{9,8},{10,11... | collective-permute-start | bytes 4718600 | tf_op jit(solution)/shard_map/ppermute | solution.py:357
  13.5 1.0 copy-start.3
  17.9 24.1 %collective-permute-start.5 = (bf16[8,256,384]{2,1,0:T(8,128)(2,1)}, bf16[8,256,384]{2,1,0:T(8,128)(2,1)S(1)}, u32[]{:S(2)}, u32[]{:S(2)}) collective-permute-start(bf16[8,256,384]{2,1,0:T(8,128)(2,1)} %slice.233), channel_id=1, source_target_pairs={{0,1},{1,0},{2,3},{3,2},{4,5},{5,4},{6,7},{7,6},{8,9},{9,8},{10,11... | collective-permute-start | bytes 4718600 | tf_op jit(solution)/shard_map/ppermute | solution.py:357
  18.0 15.6 %collective-permute-start.3 = (bf16[1024,256]{1,0:T(8,128)(2,1)S(1)}, bf16[1024,256]{1,0:T(8,128)(2,1)S(1)}, u32[]{:S(2)}, u32[]{:S(2)}) collective-permute-start(bf16[1024,256]{1,0:T(8,128)(2,1)S(1)} %get-tuple-element.45), channel_id=1, source_target_pairs={{0,2},{1,3},{2,0},{3,1},{4,6},{5,7},{6,4},{7,5},{8,10},{9,11},{10,... | collective-permute-start | bytes 1572872 | tf_op jit(solution)/shard_map/ppermute | solution.py:357
  20.9 15.7 %collective-permute-start.4 = (bf16[1024,256]{1,0:T(8,128)(2,1)}, bf16[1024,256]{1,0:T(8,128)(2,1)}, u32[]{:S(2)}, u32[]{:S(2)}) collective-permute-start(bf16[1024,256]{1,0:T(8,128)(2,1)} %get-tuple-element.49), channel_id=1, source_target_pairs={{0,4},{1,5},{2,6},{3,7},{4,0},{5,1},{6,2},{7,3},{8,12},{9,13},{10,... | collective-permute-start | bytes 1572872 | tf_op jit(solution)/shard_map/ppermute | solution.py:357
  28.1 22.2 %collective-permute-start.7 = (bf16[1024,384]{1,0:T(8,128)(2,1)}, bf16[1024,384]{1,0:T(8,128)(2,1)}, u32[]{:S(2)}, u32[]{:S(2)}) collective-permute-start(bf16[1024,384]{1,0:T(8,128)(2,1)} %get-tuple-element.53), channel_id=1, source_target_pairs={{0,2},{1,3},{2,0},{3,1},{4,6},{5,7},{6,4},{7,5},{8,10},{9,11},{10,... | collective-permute-start | bytes 2359304 | tf_op jit(solution)/shard_map/ppermute | solution.py:357
  33.6 0.9 copy-start.13
  34.5 14.3 %collective-permute-start.6 = (bf16[512,256]{1,0:T(8,128)(2,1)}, bf16[512,256]{1,0:T(8,128)(2,1)}, u32[]{:S(2)}, u32[]{:S(2)}) collective-permute-start(bf16[512,256]{1,0:T(8,128)(2,1)} %add_convert_fusion.4), channel_id=1, source_target_pairs={{0,4},{1,5},{2,6},{3,7},{4,0},{5,1},{6,2},{7,3},{8,12},{9,13},{10,... | collective-permute-start | bytes 786440 | tf_op jit(solution)/shard_map/ppermute | solution.py:357
  37.8 16.1 %collective-permute-start.8 = (bf16[512,256]{1,0:T(8,128)(2,1)S(1)}, bf16[512,256]{1,0:T(8,128)(2,1)S(1)}, u32[]{:S(2)}, u32[]{:S(2)}) collective-permute-start(bf16[512,256]{1,0:T(8,128)(2,1)S(1)} %add_convert_fusion.3), channel_id=1, source_target_pairs={{0,8},{1,9},{2,10},{3,11},{4,12},{5,13},{6,14},{7,15},{8,0},{9,1},... | collective-permute-start | bytes 786440 | tf_op jit(solution)/shard_map/ppermute | solution.py:357
  41.8 7.0 %copy-start.6 = (f32[1024,256]{1,0:T(8,128)S(1)}, f32[1024,256]{1,0:T(8,128)}, u32[]{:S(2)}) copy-start(f32[1024,256]{1,0:T(8,128)} %copy-done.5) | copy-start | bytes 3145732
  41.9 7.0 %copy-start.14 = (bf16[1024,256]{1,0:T(8,128)(2,1)S(1)}, bf16[1024,256]{1,0:T(8,128)(2,1)}, u32[]{:S(2)}) copy-start(bf16[1024,256]{1,0:T(8,128)(2,1)} %copy-done.13) | copy-start | bytes 1572868
  41.9 18.3 %collective-permute-start.11 = (bf16[8,256,256]{2,1,0:T(8,128)(2,1)S(1)}, bf16[8,256,256]{2,1,0:T(8,128)(2,1)S(1)}, u32[]{:S(2)}, u32[]{:S(2)}) collective-permute-start(bf16[8,256,256]{2,1,0:T(8,128)(2,1)S(1)} %slice.234), channel_id=1, source_target_pairs={{0,1},{1,0},{2,3},{3,2},{4,5},{5,4},{6,7},{7,6},{8,9},{9,8},{10,11... | collective-permute-start | bytes 3145736 | tf_op jit(solution)/shard_map/ppermute | solution.py:357
  47.2 6.6 %copy-start.4 = (f32[1024,256]{1,0:T(8,128)S(1)}, f32[1024,256]{1,0:T(8,128)}, u32[]{:S(2)}) copy-start(f32[1024,256]{1,0:T(8,128)} %copy-done.3) | copy-start | bytes 3145732
  47.2 20.4 %collective-permute-start.13 = (bf16[1024,384]{1,0:T(8,128)(2,1)S(1)}, bf16[1024,384]{1,0:T(8,128)(2,1)S(1)}, u32[]{:S(2)}, u32[]{:S(2)}) collective-permute-start(bf16[1024,384]{1,0:T(8,128)(2,1)S(1)} %get-tuple-element.58), channel_id=1, source_target_pairs={{0,2},{1,3},{2,0},{3,1},{4,6},{5,7},{6,4},{7,5},{8,10},{9,11},{10,... | collective-permute-start | bytes 2359304 | tf_op jit(solution)/shard_map/ppermute | solution.py:357
  49.8 9.2 %collective-permute-start.9 = (bf16[256,256]{1,0:T(8,128)(2,1)S(1)}, bf16[256,256]{1,0:T(8,128)(2,1)S(1)}, u32[]{:S(2)}, u32[]{:S(2)}) collective-permute-start(bf16[256,256]{1,0:T(8,128)(2,1)S(1)} %add_convert_fusion.9), channel_id=1, source_target_pairs={{0,8},{1,9},{2,10},{3,11},{4,12},{5,13},{6,14},{7,15},{8,0},{9,1},... | collective-permute-start | bytes 393224 | tf_op jit(solution)/shard_map/ppermute | solution.py:357
  50.2 9.9 %copy-start.8 = (s32[288,2]{1,0:T(8,128)S(1)}, s32[288,2]{1,0:T(8,128)}, u32[]{:S(2)}) copy-start(s32[288,2]{1,0:T(8,128)} %constant.82.clone.order_ref) | copy-start | bytes 6916
  51.4 13.7 %collective-permute-start.12 = (bf16[512,384]{1,0:T(8,128)(2,1)S(1)}, bf16[512,384]{1,0:T(8,128)(2,1)S(1)}, u32[]{:S(2)}, u32[]{:S(2)}) collective-permute-start(bf16[512,384]{1,0:T(8,128)(2,1)S(1)} %add_convert_fusion.1), channel_id=1, source_target_pairs={{0,4},{1,5},{2,6},{3,7},{4,0},{5,1},{6,2},{7,3},{8,12},{9,13},{10,... | collective-permute-start | bytes 1179656 | tf_op jit(solution)/shard_map/ppermute | solution.py:357
  54.8 15.7 %collective-permute-start.14 = (bf16[256,256]{1,0:T(8,128)(2,1)S(1)}, bf16[256,256]{1,0:T(8,128)(2,1)S(1)}, u32[]{:S(2)}, u32[]{:S(2)}) collective-permute-start(bf16[256,256]{1,0:T(8,128)(2,1)S(1)} %add_convert_fusion.8), channel_id=1, source_target_pairs={{0,2},{1,3},{2,0},{3,1},{4,6},{5,7},{6,4},{7,5},{8,10},{9,11},{10,... | collective-permute-start | bytes 393224 | tf_op jit(solution)/shard_map/ppermute | solution.py:357
  60.0 24.2 %collective-permute-start.10 = (f32[144,256]{1,0:T(8,128)S(1)}, f32[144,256]{1,0:T(8,128)S(1)}, u32[]{:S(2)}, u32[]{:S(2)}) collective-permute-start(f32[144,256]{1,0:T(8,128)S(1)} %get-tuple-element.88), channel_id=1, source_target_pairs={{0,1},{1,0},{2,3},{3,2},{4,5},{5,4},{6,7},{7,6},{8,9},{9,8},{10,11... | collective-permute-start | bytes 442376 | tf_op jit(solution)/shard_map/ppermute | solution.py:357
  62.8 19.7 %collective-permute-start.19 = (bf16[1152,256]{1,0:T(8,128)(2,1)S(1)}, bf16[1152,256]{1,0:T(8,128)(2,1)S(1)}, u32[]{:S(2)}, u32[]{:S(2)}) collective-permute-start(bf16[1152,256]{1,0:T(8,128)(2,1)S(1)} %get-tuple-element.65), channel_id=1, source_target_pairs={{0,2},{1,3},{2,0},{3,1},{4,6},{5,7},{6,4},{7,5},{8,10},{9,11},{10,... | collective-permute-start | bytes 1769480 | tf_op jit(solution)/shard_map/ppermute | solution.py:357
  66.0 10.7 %collective-permute-start.16 = (bf16[256,384]{1,0:T(8,128)(2,1)S(1)}, bf16[256,384]{1,0:T(8,128)(2,1)S(1)}, u32[]{:S(2)}, u32[]{:S(2)}) collective-permute-start(bf16[256,384]{1,0:T(8,128)(2,1)S(1)} %add_convert_fusion.6), channel_id=1, source_target_pairs={{0,8},{1,9},{2,10},{3,11},{4,12},{5,13},{6,14},{7,15},{8,0},{9,1},... | collective-permute-start | bytes 589832 | tf_op jit(solution)/shard_map/ppermute | solution.py:357
  67.8 14.2 %collective-permute-start.18 = (bf16[512,384]{1,0:T(8,128)(2,1)S(1)}, bf16[512,384]{1,0:T(8,128)(2,1)S(1)}, u32[]{:S(2)}, u32[]{:S(2)}) collective-permute-start(bf16[512,384]{1,0:T(8,128)(2,1)S(1)} %add_convert_fusion), channel_id=1, source_target_pairs={{0,4},{1,5},{2,6},{3,7},{4,0},{5,1},{6,2},{7,3},{8,12},{9,13},{10,... | collective-permute-start | bytes 1179656 | tf_op jit(solution)/shard_map/ppermute | solution.py:357
  82.6 13.1 %copy-start.12 = (bf16[1152,256]{1,0:T(8,128)(2,1)}, bf16[1152,256]{1,0:T(8,128)(2,1)S(1)}, u32[]{:S(2)}) copy-start(bf16[1152,256]{1,0:T(8,128)(2,1)S(1)} %collective-permute-done.19) | copy-start | bytes 1769476
  82.7 12.3 %collective-permute-start.20 = (bf16[576,256]{1,0:T(8,128)(2,1)S(1)}, bf16[576,256]{1,0:T(8,128)(2,1)S(1)}, u32[]{:S(2)}, u32[]{:S(2)}) collective-permute-start(bf16[576,256]{1,0:T(8,128)(2,1)S(1)} %add_convert_fusion.2), channel_id=1, source_target_pairs={{0,4},{1,5},{2,6},{3,7},{4,0},{5,1},{6,2},{7,3},{8,12},{9,13},{10,... | collective-permute-start | bytes 884744 | tf_op jit(solution)/shard_map/ppermute | solution.py:357
  84.9 12.9 %collective-permute-start.15 = (f32[144,256]{1,0:T(8,128)S(1)}, f32[144,256]{1,0:T(8,128)S(1)}, u32[]{:S(2)}, u32[]{:S(2)}) collective-permute-start(f32[144,256]{1,0:T(8,128)S(1)} %get-tuple-element.86), channel_id=1, source_target_pairs={{0,1},{1,0},{2,3},{3,2},{4,5},{5,4},{6,7},{7,6},{8,9},{9,8},{10,11... | collective-permute-start | bytes 442376 | tf_op jit(solution)/shard_map/ppermute | solution.py:357
  85.0 26.4 %copy-start.7 = (s32[8,3072]{1,0:T(8,128)S(1)}, s32[8,3072]{1,0:T(8,128)}, u32[]{:S(2)}) copy-start(s32[8,3072]{1,0:T(8,128)} %mask_ref.2) | copy-start | bytes 294916
  85.0 13.4 %collective-permute-start.17 = (f32[144,384]{1,0:T(8,128)S(1)}, f32[144,384]{1,0:T(8,128)S(1)}, u32[]{:S(2)}, u32[]{:S(2)}) collective-permute-start(f32[144,384]{1,0:T(8,128)S(1)} %get-tuple-element.82), channel_id=1, source_target_pairs={{0,1},{1,0},{2,3},{3,2},{4,5},{5,4},{6,7},{7,6},{8,9},{9,8},{10,11... | collective-permute-start | bytes 663560 | tf_op jit(solution)/shard_map/ppermute | solution.py:357
  85.6 12.0 %collective-permute-start.21 = (bf16[256,384]{1,0:T(8,128)(2,1)S(1)}, bf16[256,384]{1,0:T(8,128)(2,1)S(1)}, u32[]{:S(2)}, u32[]{:S(2)}) collective-permute-start(bf16[256,384]{1,0:T(8,128)(2,1)S(1)} %add_convert_fusion.5), channel_id=1, source_target_pairs={{0,8},{1,9},{2,10},{3,11},{4,12},{5,13},{6,14},{7,15},{8,0},{9,1},... | collective-permute-start | bytes 589832 | tf_op jit(solution)/shard_map/ppermute | solution.py:357
  97.7 1.5 %collective-permute-start.22 = (f32[144,384]{1,0:T(8,128)S(1)}, f32[144,384]{1,0:T(8,128)S(1)}, u32[]{:S(2)}, u32[]{:S(2)}) collective-permute-start(f32[144,384]{1,0:T(8,128)S(1)} %get-tuple-element.80), channel_id=1, source_target_pairs={{0,1},{1,0},{2,3},{3,2},{4,5},{5,4},{6,7},{7,6},{8,9},{9,8},{10,11... | collective-permute-start | bytes 663560 | tf_op jit(solution)/shard_map/ppermute | solution.py:357
  102.3 9.0 %collective-permute-start.23 = (f32[16,2560]{1,0:T(8,128)}, f32[16,2560]{1,0:T(8,128)S(1)}, u32[]{:S(2)}, u32[]{:S(2)}) collective-permute-start(f32[16,2560]{1,0:T(8,128)} %dynamic-slice_dynamic-update-slice_fusion), channel_id=1, source_target_pairs={{2,1},{4,3},{6,5},{8,7},{10,9},{12,11},{14,13},{0,15},{1,2},{3,4},... | collective-permute-start | bytes 491528 | tf_op jit(solution)/shard_map/ppermute | solution.py:422
  105.6 9.1 %collective-permute-start.24 = (bf16[288,256]{1,0:T(8,128)(2,1)}, bf16[288,256]{1,0:T(8,128)(2,1)}, u32[]{:S(2)}, u32[]{:S(2)}) collective-permute-start(bf16[288,256]{1,0:T(8,128)(2,1)} %add_convert_fusion.7), channel_id=1, source_target_pairs={{0,8},{1,9},{2,10},{3,11},{4,12},{5,13},{6,14},{7,15},{8,0},{9,1},... | collective-permute-start | bytes 442376 | tf_op jit(solution)/shard_map/ppermute | solution.py:357
  111.4 6.0 %copy-start.11 = (f32[2,24]{1,0:T(2,128)S(1)}, f32[2,24]{1,0:T(2,128)}, u32[]{:S(2)}) copy-start(f32[2,24]{1,0:T(2,128)} %steer_ref.1) | copy-start | bytes 580
  115.9 1.5 %collective-permute-start.25 = (f32[160,256]{1,0:T(8,128)S(1)}, f32[160,256]{1,0:T(8,128)S(1)}, u32[]{:S(2)}, u32[]{:S(2)}) collective-permute-start(f32[160,256]{1,0:T(8,128)S(1)} %get-tuple-element.83), channel_id=1, source_target_pairs={{0,1},{1,0},{2,3},{3,2},{4,5},{5,4},{6,7},{7,6},{8,9},{9,8},{10,11... | collective-permute-start | bytes 491528 | tf_op jit(solution)/shard_map/ppermute | solution.py:357

commit v3 on v2

--- a/solution.py
+++ b/solution.py
@@ -15,10 +15,12 @@
 BF16 = jnp.bfloat16
 GROUP = 8
 VMEM = 48 << 20
-CHUNKS = ((2, 0, 0), (2, 1, 0), (3, 0, 0), (3, 0, 0), (2, 0, 1))
+CHUNKS = ((2, 1, 0, 0), (3, 0, 0, 0), (3, 0, 0, 0), (2, 0, 1, 0), (2, 0, 1, 0))
+AHEAD = 2
 STEPS = (
-    (0, 0), (1, 0), (0, 1), (2, 0), (1, 1), (3, 0), (2, 1), (0, 2), (1, 2), (4, 0), (3, 1), (0, 3), (2, 2), (1, 3),
-    (0, 4), (4, 1), (2, 3), (3, 2), (1, 4), (2, 4), (3, 3), (4, 2), (4, 3), (3, 4), ("halo", 0), ("gram", 0), (4, 4),
+    (1, 0), (2, 0), (1, 1), (2, 1), (0, 1), (1, 2), (0, 2), (4, 1), (3, 1), (1, 3),
+    (0, 3), (2, 2), (2, 11), (2, 3), (3, 2), (4, 2), (0, 4), (1, 4), (2, 4), (3, 3),
+    (4, 3), (3, 4), ("halo", 0), ("gram", 0), (4, 4),
 )
 
 
@@ -66,40 +68,40 @@
 
 
 def front_kernel(
-    bins_chip, me_ref, order_ref, natural_ref, picks_ref, beam_ref, mine_ref, theirs_ref,
-    send_ref, keep_ref, table_ref, weights_ref, spectra_ref,
+    bins_chip, ahead, parts, me_ref, order_ref, natural_ref, picks_ref, beam_ref, mine_ref, theirs_ref, *refs
 ):
+    if ahead:
+        refs[2 + parts][...] = refs[0][...]
+        refs = refs[1 : 2 + parts] + refs[3 + parts :]
+    sends, keep_ref, table_ref, weights_ref, spectra_ref = refs[:parts], *refs[parts:]
     elem_dev = mine_ref.shape[0]
     groups = spectra_ref.shape[0]
     width = mine_ref.shape[-1]
     rows_in = natural_ref.shape[0]
-
-    @pl.when(pl.program_id(0) == 0)
-    def _():
-        me = me_ref[0]
-        order = order_ref[...]
-        source = jnp.bitwise_xor(order[:, 0:1], me // 2) * (2 * bins_chip) + order[:, 1:2]
-        source = lax.rem(source + rows_in, rows_in)
-        lane = lax.broadcasted_iota(jnp.int32, (order.shape[0], rows_in), 1)
-        picked = jnp.where(source == lane, 1.0, 0.0).astype(BF16)
-        table_ref[...] = dot(picked, natural_ref[...]).astype(BF16)
-        parts = beam_ref[...].astype(F32)
-        parts = jnp.concatenate([parts[:, 0], parts[:, 1]], axis=0).astype(BF16)
-        elements = parts.shape[1]
-        columns = weights_ref.shape[1]
-        row = lax.broadcasted_iota(jnp.int32, (elements, columns), 0)
-        column = lax.broadcasted_iota(jnp.int32, (elements, columns), 1)
-        held = column // (2 * GROUP)
-        first = jnp.where(held < elem_dev, me, jnp.bitwise_xor(me, 1)) * elem_dev
-        here = row == first + held % elem_dev
-        total = jnp.zeros(weights_ref.shape, F32)
-        for part in range(2):
-            spread = jnp.where(here & (column % 2 == part), 1.0, 0.0).astype(BF16)
-            total += dot(dot(picks_ref[part], parts).astype(BF16), spread)
-        row = lax.broadcasted_iota(jnp.int32, weights_ref.shape, 0)
-        column = lax.broadcasted_iota(jnp.int32, weights_ref.shape, 1)
-        same = row // (weights_ref.shape[0] // GROUP) == column % (2 * GROUP) // 2
-        weights_ref[...] = jnp.where(same, total, 0.0).astype(BF16)
+    me = me_ref[0]
+    order = order_ref[...]
+    source = jnp.bitwise_xor(order[:, 0:1], me // 2) * (2 * bins_chip) + order[:, 1:2]
+    source = lax.rem(source + rows_in, rows_in)
+    lane = lax.broadcasted_iota(jnp.int32, (order.shape[0], rows_in), 1)
+    picked = jnp.where(source == lane, 1.0, 0.0).astype(BF16)
+    table_ref[...] = dot(picked, natural_ref[...]).astype(BF16)
+    given = beam_ref[...].astype(F32)
+    given = jnp.concatenate([given[:, 0], given[:, 1]], axis=0).astype(BF16)
+    elements = given.shape[1]
+    columns = weights_ref.shape[1]
+    row = lax.broadcasted_iota(jnp.int32, (elements, columns), 0)
+    column = lax.broadcasted_iota(jnp.int32, (elements, columns), 1)
+    held = column // (2 * GROUP)
+    first = jnp.where(held < elem_dev, me, jnp.bitwise_xor(me, 1)) * elem_dev
+    here = row == first + held % elem_dev
+    total = jnp.zeros(weights_ref.shape, F32)
+    for part in range(2):
+        spread = jnp.where(here & (column % 2 == part), 1.0, 0.0).astype(BF16)
+        total += dot(dot(picks_ref[part], given).astype(BF16), spread)
+    row = lax.broadcasted_iota(jnp.int32, weights_ref.shape, 0)
+    column = lax.broadcasted_iota(jnp.int32, weights_ref.shape, 1)
+    same = row // (weights_ref.shape[0] // GROUP) == column % (2 * GROUP) // 2
+    weights_ref[...] = jnp.where(same, total, 0.0).astype(BF16)
 
     table = table_ref[...]
     for e in range(2 * elem_dev):
@@ -107,18 +109,22 @@
         spectra_ref[:, e] = spectra.astype(BF16).reshape(groups, 2 * GROUP, width)
     weights = weights_ref[...]
     rows = weights.shape[0]
+    tall = sends[0].shape[0]
     for g in range(groups):
         sums = dot(weights, spectra_ref[g].reshape(-1, width))
-        at = g % (groups // 2) * rows
         if g < groups // 2:
-            keep_ref[at : at + rows] = sums
-        else:
-            send_ref[at : at + rows] = sums.astype(BF16)
-
-
-def front(me, strides, extra, bins_chip, beam_weights, echo, theirs, start, width):
+            keep_ref[g * rows : (g + 1) * rows] = sums
+            continue
+        sums = sums.astype(BF16)
+        for low in range(0, rows, 16):
+            at = (g - groups // 2) * rows + low
+            out_ref = sends[parts - 1 - at // tall]
+            out_ref[at % tall : at % tall + 16] = sums[low : low + 16]
+
+
+def front(me, strides, extra, bins_chip, beam_weights, echo, theirs, span, ahead, parts):
     elem_dev, rows_in, gate_count = echo.shape
-    size = theirs.shape[2]
+    start, size = span
     beams = beam_weights.shape[0]
     order = row_order([s // 2 for s in strides], bins_chip, extra)
     natural = doppler_table(rows_in // 2)
@@ -126,41 +132,43 @@
     table_rows = order.shape[0]
     groups = table_rows // 2 // GROUP
     half = table_rows // 4 * 2 * beams
-    first, across = start // width, gate_count // 2 // width
     block_rows, block_columns = GROUP * 2 * beams, elem_dev * 4 * GROUP
     whole = lambda shape: pl.BlockSpec(shape, lambda i, me: (0,) * len(shape))
-    echo_block = (elem_dev, rows_in, width)
-    return pl.pallas_call(
-        functools.partial(front_kernel, bins_chip),
+
+    def gates(which, start, size):
+        lane = lambda me: ((me[0] + which) % 2) * (gate_count // 2) + start
+        return pl.BlockSpec(
+            (pl.Element(elem_dev), pl.Element(rows_in), pl.Element(size)),
+            lambda i, me: (0, 0, pl.multiple_of(lane(me), 128)),
+        )
+
+    in_specs = [whole(x.shape) for x in (order, natural, picks, beam_weights)]
+    in_specs += [gates(0, start, size), whole(theirs.shape)]
+    out_shape = [jax.ShapeDtypeStruct((half // parts, size), BF16)] * parts
+    out_shape += [jax.ShapeDtypeStruct((half, size), F32)]
+    operands = [me, jnp.asarray(order), jnp.asarray(natural), jnp.asarray(picks), beam_weights, echo, theirs]
+    if ahead:
+        in_specs.append(gates(1, *ahead))
+        operands.append(echo)
+        out_shape.append(jax.ShapeDtypeStruct((elem_dev, rows_in, ahead[1]), BF16))
+    return pl.pallas_call(
+        functools.partial(front_kernel, bins_chip, ahead is not None, parts),
         grid_spec=pltpu.PrefetchScalarGridSpec(
             num_scalar_prefetch=1,
-            grid=(size // width,),
-            in_specs=[
-                whole(order.shape),
-                whole(natural.shape),
-                whole(picks.shape),
-                whole(beam_weights.shape),
-                pl.BlockSpec(echo_block, lambda i, me: (0, 0, me[0] % 2 * across + first + i)),
-                pl.BlockSpec(echo_block, lambda i, me: (0, 0, i)),
-            ],
-            out_specs=[
-                pl.BlockSpec((half, width), lambda i, me: (0, i)),
-                pl.BlockSpec((half, width), lambda i, me: (0, i)),
-            ],
+            grid=(1,),
+            in_specs=in_specs,
+            out_specs=[whole(x.shape) for x in out_shape],
             scratch_shapes=[
                 pltpu.VMEM((table_rows, rows_in), BF16),
                 pltpu.VMEM((block_rows, block_columns), BF16),
-                pltpu.VMEM((groups, 2 * elem_dev, 2 * GROUP, width), BF16),
+                pltpu.VMEM((groups, 2 * elem_dev, 2 * GROUP, size), BF16),
             ],
         ),
-        out_shape=[
-            jax.ShapeDtypeStruct((half, size), BF16),
-            jax.ShapeDtypeStruct((half, size), F32),
-        ],
+        out_shape=out_shape,
         compiler_params=pltpu.CompilerParams(vmem_limit_bytes=VMEM),
         cost_estimate=pl.CostEstimate(flops=1000, bytes_accessed=1000, transcendentals=0),
         name="front",
-    )(me, jnp.asarray(order), jnp.asarray(natural), jnp.asarray(picks), beam_weights, echo, theirs)
+    )(*operands)
 
 
 def gram_sums(window, mask, rows):
@@ -258,10 +266,13 @@
     for k in range(order):
         spot = k // beams * rows + k % beams
         pivot_row = system[:, k : k + 1, :]
-        pivot_row = pivot_row / pivot_row[:, :, spot : spot + 1]
+        turned = swapped(pivot_row)
+        pivot = jnp.broadcast_to(pivot_row[:, :, spot : spot + 1], pivot_row.shape)
         factor_re = system[:, :, spot : spot + 1]
         factor_im = system[:, :, spot + beams : spot + beams + 1]
-        changed = system - factor_re * pivot_row - factor_im * swapped(pivot_row)
+        scale = 1.0 / pivot
+        pivot_row = pivot_row * scale
+        changed = system - factor_re * pivot_row - factor_im * (turned * scale)
         system = jnp.where(row_at == k, pivot_row, changed)
 
     solved_re = system[:, :, 3 * rows : 3 * rows + 1]
@@ -357,11 +368,89 @@
     return lax.ppermute(x, "elem", [(i, i ^ stride) for i in range(count)])
 
 
-def share(keep, received, part):
-    total = keep[part]
+def share_kernel(count, keep_ref, *refs):
+    received, sends = refs[:count], refs[count:]
+    total = keep_ref[...]
     for got in received:
-        total = total + got[part].astype(F32)
-    return total
+        total = total + got[...].astype(F32)
+    total = total.astype(BF16)
+    tall = sends[0].shape[0]
+    for i, out_ref in enumerate(reversed(sends)):
+        out_ref[...] = total[i * tall : (i + 1) * tall]
+
+
+def share(keep, received, height, parts):
+    size = keep.shape[1]
+    block = (height, size)
+    second = pl.BlockSpec(block, lambda i: (1, 0))
+    operands, specs = [keep], [second]
+    for got in received[:-1]:
+        operands.append(got[-1])
+        specs.append(second)
+    operands.append(received[-1][0])
+    specs.append(second if len(received[-1]) == 1 else pl.BlockSpec(block, lambda i: (0, 0)))
+    return pl.pallas_call(
+        functools.partial(share_kernel, len(received)),
+        grid=(1,),
+        in_specs=specs,
+        out_specs=[pl.BlockSpec((height // parts, size), lambda i: (0, 0))] * parts,
+        out_shape=[jax.ShapeDtypeStruct((height // parts, size), BF16)] * parts,
+        compiler_params=pltpu.CompilerParams(vmem_limit_bytes=VMEM),
+        cost_estimate=pl.CostEstimate(flops=1000, bytes_accessed=1000, transcendentals=0),
+        name="share",
+    )(*operands)
+
+
+def finish_kernel(step, me_ref, keep_ref, *refs):
+    received, near_ref, send_ref, total_ref = refs[:-3], *refs[-3:]
+    total = keep_ref[...]
+    for got in received:
+        total = total + got[...].astype(F32)
+    total_ref[...] = total
+    core = me_ref[0] % 2
+    height = near_ref.shape[0]
+    near_ref[...] = total_ref[pl.ds(pl.multiple_of(core * step, 8), height)]
+    send_ref[...] = total_ref[pl.ds(pl.multiple_of((1 - core) * step, 8), height)]
+
+
+def finish(me, keep, received, held, step):
+    size = keep.shape[1]
+    part = pl.BlockSpec((held, size), lambda i: (0, 0))
+    out = pl.BlockSpec((held - step, size), lambda i: (0, 0))
+    return pl.pallas_call(
+        functools.partial(finish_kernel, step),
+        grid=(1,),
+        in_specs=[pl.BlockSpec(memory_space=pltpu.SMEM)] + [part] * (1 + len(received)),
+        out_specs=[out, out],
+        out_shape=[jax.ShapeDtypeStruct((held - step, size), F32)] * 2,
+        scratch_shapes=[pltpu.VMEM((held, size), F32)],
+        compiler_params=pltpu.CompilerParams(vmem_limit_bytes=VMEM),
+        cost_estimate=pl.CostEstimate(flops=1000, bytes_accessed=1000, transcendentals=0),
+        name="finish",
+    )(me, keep, *received)
+
+
+def edges_kernel(rows, step, me_ref, *refs):
+    parts, out_ref = refs[:-1], refs[-1]
+    first = pl.multiple_of(me_ref[0] % 2 * step, 8)
+    start = 0
+    for part in parts:
+        size = part.shape[1]
+        out_ref[:, start : start + size] = part[pl.ds(first, rows)]
+        start += size
+
+
+def edges(me, parts, rows):
+    width = sum(x.shape[1] for x in parts)
+    return pl.pallas_call(
+        functools.partial(edges_kernel, rows, parts[0].shape[0] - rows),
+        in_specs=[pl.BlockSpec(memory_space=pltpu.SMEM)]
+        + [pl.BlockSpec(memory_space=pltpu.VMEM)] * len(parts),
+        out_shape=jax.ShapeDtypeStruct((rows, width), F32),
+        compiler_params=pltpu.CompilerParams(vmem_limit_bytes=VMEM),
+        cost_estimate=pl.CostEstimate(flops=1000, bytes_accessed=1000, transcendentals=0),
+        name="edges",
+    )(me, *parts)
 
 
 class Chain:
@@ -383,19 +472,18 @@
     elem_dev, _, pulses, gate_count = raw_echo.shape
     count = lax.axis_size("elem")
     me = lax.axis_index("elem").astype(jnp.int32)
-    core = me % 2
     at = me.reshape(1)
     bins_here = pulses // count
     rows = 2 * beam_weights.shape[0]
     echo = raw_echo.reshape(elem_dev, 2 * pulses, gate_count)
     levels = count.bit_length() - 1
     plain = [2 << i for i in range(levels - 1)]
-    orders = [plain, plain[1:] + plain[:1]]
-    unit = gate_count // 2 // sum(width for width, _, _ in CHUNKS)
+    orders = [plain, plain[1:] + plain[:1], [plain[1], plain[0]] + plain[2:]]
+    unit = gate_count // 2 // sum(width for width, _, _, _ in CHUNKS)
     chunks = len(CHUNKS)
-    last = sum(1 - wide for _, _, wide in CHUNKS)
+    last = sum(1 - wide for _, _, wide, _ in CHUNKS)
     spans = []
-    for width, _, _ in CHUNKS:
+    for width, _, _, _ in CHUNKS:
         start = sum(spans[-1]) if spans else 0
         spans.append((start, width * unit))
     early = tuple(spans[:last])
@@ -411,42 +499,47 @@
             steps += [(c, later) for later in range(3, levels)]
         else:
             steps.append((c, levels if stage == 4 else stage))
+    turns = [c for c, stage in steps if stage == 1]
     for c, stage in steps:
         if c == "halo":
-            edges = [
-                lax.dynamic_slice_in_dim(x, core * bins_here * rows, rows, 0)
-                for x in far[:last] + near[:last]
-            ]
+            out = edges(at, far[:last] + near[:last], rows)
             pairs = [((i + 1) % count, i) for i in range(1, count, 2)]
             pairs += [(i, (i + 1) % count) for i in range(1, count, 2)]
-            edge = lax.ppermute(jnp.concatenate(edges, axis=1), "elem", pairs)
+            edge = lax.ppermute(out, "elem", pairs)
         elif c == "gram":
             gram, window = gram_of(at, early, near[:last], far[:last], edge, chain.enter(train_mask))
             chain.leave(gram)
         elif stage == 0:
             part = chain.leave(other_half(at, chain.enter(echo), *spans[c]))
             theirs[c] = swap(part, 1, count)
+        elif stage >= 10:
+            got = received[c][stage - 10]
+            got[0] = chain.leave(chain.enter(got[0]))
         elif stage == 1:
-            start, size = spans[c]
             strides = orders[CHUNKS[c][1]]
-            width = math.gcd(size, start, gate_count // 2)
-            send, keeps[c] = front(
+            later = turns.index(c) + AHEAD
+            later = turns[later] if later < chunks else None
+            parts = 1 + CHUNKS[c][3]
+            out = front(
                 at, strides, CHUNKS[c][2], 2 * bins_here, beam_weights,
-                chain.enter(echo), theirs[c], start, width,
+                chain.enter(echo), theirs[c], spans[c], None if later is None else spans[later], parts,
             )
-            chain.leave(send)
-            received[c].append(swap(send, strides[0], count))
+            send, keeps[c], part = out[:parts], out[parts], out[parts + 1 :]
+            if part:
+                theirs[later] = swap(part[0], 1, count)
+            chain.leave(send[0])
+            received[c].append([swap(x, strides[0], count) for x in send])
         elif stage < levels:
             half = keeps[c].shape[0] >> (stage - 1)
-            total = share(chain.enter(keeps[c]), received[c], slice(half, 2 * half))
-            send = chain.leave(total.astype(BF16))
-            received[c].append(swap(send, orders[CHUNKS[c][1]][stage - 1], count))
+            parts = 1 + CHUNKS[c][3] * (stage < levels - 1)
+            send = share(chain.enter(keeps[c]), received[c], half, parts)
+            chain.leave(send[0])
+            received[c].append([swap(x, orders[CHUNKS[c][1]][stage - 1], count) for x in send])
         else:
             held = keeps[c].shape[0] >> (levels - 2)
-            total = chain.leave(share(chain.enter(keeps[c]), received[c], slice(0, held)))
             step = (bins_here - 1 + CHUNKS[c][2]) * rows
-            near[c] = lax.dynamic_slice_in_dim(total, core * step, held - step, 0)
-            send = lax.dynamic_slice_in_dim(total, (1 - core) * step, held - step, 0)
+            near[c], send = finish(at, chain.enter(keeps[c]), [x[-1] for x in received[c]], held, step)
+            chain.leave(send)
             far[c] = swap(send, 1, count)
     return tail(at, steer, gram, window, train_mask, near[last:], far[last:])
 

time: 124 us -> 105 us (0.85); the launches traced: 124 us -> 103 us
  other arithmetic: 11.1 us -> 0 us
  Pallas kernels: 38.2 us -> 30.4 us
  waiting for transfers between devices: 39.8 us -> 46.3 us
  local copies, waits for them, and re-layouts: 6.12 us -> 0.05 us
  starting transfers between devices: 28.1 us -> 26.1 us
    ppermute x25, waiting for transfers between devices: 34.1 us -> 44.4 us  [swap(): return lax.ppermute(x, 'elem', [(i, i ^ stride) for i in range(count)])]
    convert_element_type x10 -> x0, other arithmetic: 6.98 us -> none  [local(): send = chain.leave(total.astype(BF16))]
    pallas_call x5 -> x2, Pallas kernels: 10.3 us -> 4.76 us  [other_half(): pl.pallas_call(slice_kernel, grid_spec=pltpu.PrefetchScalarGridSpec(num_s...]
    unnamed x37 -> x16, local copies, waits for them, and re-layouts: 5.35 us -> 0.05 us
    add x5 -> x0, other arithmetic: 4.09 us -> none  [share(): total = total + got[part].astype(F32)]
    ppermute x1, waiting for transfers between devices: 5.72 us -> 1.91 us  [local(): edge = lax.ppermute(out, 'elem', pairs)]
    ppermute x1, starting transfers between devices: 3.3 us -> 0.07 us  [local(): edge = lax.ppermute(out, 'elem', pairs)]
    pallas_call x5 -> x21, Pallas kernels: 19.5 us -> 18.3 us  [the longest x5 17.1 us: front(): pl.pallas_call(functools.partial(front_kernel, bins_chip, ahead is not No...]
  transfers between devices with their start and end apart: 26 -> 26, of which waited for: 15 -> 12; matrix products, arithmetic and copies ran while one was open for 10% -> 0% of each run, Pallas kernels for 25% -> 22%
where the time goes in v3:
time: 105 us; the launch traced here: 103 us
  waiting for transfers between devices  46.3 us (44%)
  Pallas kernels  30.4 us (29%)
  starting transfers between devices  26.1 us (25%)
    ppermute x25, waiting for transfers between devices, swap(): return lax.ppermute(x, 'elem', [(i, i ^ stride) for i in range(count)])  44.4 us
    ppermute x25, starting transfers between devices, swap(): return lax.ppermute(x, 'elem', [(i, i ^ stride) for i in range(count)])  26 us
    pallas_call x5, Pallas kernels, front(): pl.pallas_call(functools.partial(front_kernel, bins_chip, ahead is not No...  17.1 us
    pallas_call x1, Pallas kernels, tail(): pl.pallas_call(tail_kernel, in_specs=[pl.BlockSpec(memory_space=pltpu.SME...  5.34 us
    pallas_call x2, Pallas kernels, other_half(): pl.pallas_call(slice_kernel, grid_spec=pltpu.PrefetchScalarGridSpec(num_s...  4.76 us
  transfers between devices with their start and end apart: 26, of which 12 were waited for; matrix products, arithmetic and copies ran while one was open for 0% of the time, Pallas kernels for 22%

profile of v3, /device:TPU:0, one launch (start us, length us, event | category | flops | bytes accessed | tf_op | source)
XLA Modules:
  0.0 103.1 jit_solution(769860043688233586)
XLA Ops:
  0.0 2.4 %slice.2 = bf16[8,256,384]{2,1,0:T(8,128)(2,1)S(1)} custom-call(s32[1]{0:T(128)} %bitcast.me_ref, bf16[8,256,3072]{2,1,0:T(8,128)(2,1)} %bitcast.2), custom_call_target="tpu_custom_call" | custom-call | flops 1000 | bytes 1000 | tf_op jit(solution)/shard_map/slice/pallas_call | solution.py:352
  2.4 0.0 copy-start
  2.4 0.0 copy-start.1
  2.4 0.0 copy-start.3
  2.4 0.5 collective-permute-start
  3.0 2.4 %slice.3 = bf16[8,256,384]{2,1,0:T(8,128)(2,1)S(1)} custom-call(s32[1]{0:T(128)} %bitcast.me_ref, bf16[8,256,3072]{2,1,0:T(8,128)(2,1)} %bitcast.3), custom_call_target="tpu_custom_call" | custom-call | flops 1000 | bytes 1000 | tf_op jit(solution)/shard_map/slice/pallas_call | solution.py:352
  5.3 0.1 collective-permute-start.1
  5.5 0.5 collective-permute-done.theirs_ref
  6.0 4.0 %front.5 = (bf16[1024,384]{1,0:T(8,128)(2,1)S(1)}, f32[1024,384]{1,0:T(8,128)S(1)}, bf16[8,256,256]{2,1,0:T(8,128)(2,1)S(1)}) custom-call(s32[1]{0:T(128)} %bitcast.me_ref, s32[256,2]{1,0:T(8,128)S(1)} %copy-done.3, bf16[256,256]{1,0:T(8,128)(2,1)S(1)} %copy-done, bf16[2,128,16]{2,1,0:T(8,128)(2,1)S(1)} %copy-done.1, bf16[8,2,128]{2,1,0:T(2,128)(2,1)S(1)} %copy-done.6, ...), custom_call_target="tpu_custom_call" | custom-call | flops 1000 | bytes 1000 | tf_op jit(solution)/shard_map/front/pallas_call | solution.py:154
  10.0 0.4 collective-permute-start.2
  10.4 2.7 %collective-permute-start.3 = (bf16[1024,384]{1,0:T(8,128)(2,1)S(1)}, bf16[1024,384]{1,0:T(8,128)(2,1)S(1)}, u32[]{:S(2)}, u32[]{:S(2)}) collective-permute-start(bf16[1024,384]{1,0:T(8,128)(2,1)S(1)} %get-tuple-element.55), channel_id=1, source_target_pairs={{0,2},{1,3},{2,0},{3,1},{4,6},{5,7},{6,4},{7,5},{8,10},{9,11},{10,... | collective-permute-start | bytes 2359304 | tf_op jit(solution)/shard_map/ppermute | solution.py:368
  13.1 4.0 %front.6 = (bf16[1024,384]{1,0:T(8,128)(2,1)S(1)}, f32[1024,384]{1,0:T(8,128)S(1)}, bf16[8,256,256]{2,1,0:T(8,128)(2,1)S(1)}) custom-call(s32[1]{0:T(128)} %bitcast.me_ref, s32[256,2]{1,0:T(8,128)S(1)} %copy-done.3, bf16[256,256]{1,0:T(8,128)(2,1)S(1)} %copy-done, bf16[2,128,16]{2,1,0:T(8,128)(2,1)S(1)} %copy-done.1, bf16[8,2,128]{2,1,0:T(2,128)(2,1)S(1)} %copy-done.6, ...), custom_call_target="tpu_custom_call" | custom-call | flops 1000 | bytes 1000 | tf_op jit(solution)/shard_map/front/pallas_call | solution.py:154
  17.1 0.1 collective-permute-start.5
  17.2 3.0 %front.7 = (bf16[1024,256]{1,0:T(8,128)(2,1)S(1)}, f32[1024,256]{1,0:T(8,128)S(1)}, bf16[8,256,256]{2,1,0:T(8,128)(2,1)S(1)}) custom-call(s32[1]{0:T(128)} %bitcast.me_ref, s32[256,2]{1,0:T(8,128)S(1)} %copy-done.5, bf16[256,256]{1,0:T(8,128)(2,1)S(1)} %copy-done, bf16[2,128,16]{2,1,0:T(8,128)(2,1)S(1)} %copy-done.1, bf16[8,2,128]{2,1,0:T(2,128)(2,1)S(1)} %copy-done.6, ...), custom_call_target="tpu_custom_call" | custom-call | flops 1000 | bytes 1000 | tf_op jit(solution)/shard_map/front/pallas_call | solution.py:154
  20.2 0.5 collective-permute-start.6
  20.7 1.6 %collective-permute-start.4 = (bf16[1024,256]{1,0:T(8,128)(2,1)S(1)}, bf16[1024,256]{1,0:T(8,128)(2,1)S(1)}, u32[]{:S(2)}, u32[]{:S(2)}) collective-permute-start(bf16[1024,256]{1,0:T(8,128)(2,1)S(1)} %get-tuple-element.62), channel_id=1, source_target_pairs={{0,4},{1,5},{2,6},{3,7},{4,0},{5,1},{6,2},{7,3},{8,12},{9,13},{10,... | collective-permute-start | bytes 1572872 | tf_op jit(solution)/shard_map/ppermute | solution.py:368
  22.3 0.5 collective-permute-start.9
  22.8 8.7 %collective-permute-done.3.refs_0_ = bf16[1024,384]{1,0:T(8,128)(2,1)S(1)} collective-permute-done((bf16[1024,384]{1,0:T(8,128)(2,1)S(1)}, bf16[1024,384]{1,0:T(8,128)(2,1)S(1)}, u32[]{:S(2)}, u32[]{:S(2)}) %collective-permute-start.3) | collective-permute-done | bytes 786464 | tf_op jit(solution)/shard_map/ppermute | solution.py:368
  31.5 0.1 share.10
  31.5 0.0 copy-start.2
  31.6 2.1 %collective-permute-start.7 = (bf16[512,384]{1,0:T(8,128)(2,1)S(1)}, bf16[512,384]{1,0:T(8,128)(2,1)S(1)}, u32[]{:S(2)}, u32[]{:S(2)}) collective-permute-start(bf16[512,384]{1,0:T(8,128)(2,1)S(1)} %share.10), channel_id=1, source_target_pairs={{0,4},{1,5},{2,6},{3,7},{4,0},{5,1},{6,2},{7,3},{8,12},{9,13},{10,... | collective-permute-start | bytes 1179656 | tf_op jit(solution)/shard_map/ppermute | solution.py:368
  33.7 1.8 %collective-permute-done.4.refs_0_ = bf16[1024,256]{1,0:T(8,128)(2,1)S(1)} collective-permute-done((bf16[1024,256]{1,0:T(8,128)(2,1)S(1)}, bf16[1024,256]{1,0:T(8,128)(2,1)S(1)}, u32[]{:S(2)}, u32[]{:S(2)}) %collective-permute-start.4) | collective-permute-done | bytes 524320 | tf_op jit(solution)/shard_map/ppermute | solution.py:368
  35.5 2.6 %collective-permute-start.8 = (bf16[512,256]{1,0:T(8,128)(2,1)S(1)}, bf16[512,256]{1,0:T(8,128)(2,1)S(1)}, u32[]{:S(2)}, u32[]{:S(2)}) collective-permute-start(bf16[512,256]{1,0:T(8,128)(2,1)S(1)} %share.11), channel_id=1, source_target_pairs={{0,8},{1,9},{2,10},{3,11},{4,12},{5,13},{6,14},{7,15},{8,0},{9,1},... | collective-permute-start | bytes 786440 | tf_op jit(solution)/shard_map/ppermute | solution.py:368
  38.2 3.5 %front.8 = (bf16[1152,256]{1,0:T(8,128)(2,1)}, f32[1152,256]{1,0:T(8,128)S(1)}) custom-call(s32[1]{0:T(128)} %bitcast.me_ref, s32[288,2]{1,0:T(8,128)S(1)} %copy-done.2, bf16[256,256]{1,0:T(8,128)(2,1)S(1)} %copy-done, bf16[2,128,16]{2,1,0:T(8,128)(2,1)S(1)} %copy-done.1, bf16[8,2,128]{2,1,0:T(2,128)(2,1)S(1)} %copy-done.6, bf16[8,256,3072]{2,1,0:T(8,128)(2,1)} %bitcast.10, ...), custom_call_target="tpu_custom_call" | custom-call | flops 1000 | bytes 1000 | tf_op jit(solution)/shard_map/front/pallas_call | solution.py:154
  41.7 2.7 %front.9 = (bf16[1152,256]{1,0:T(8,128)(2,1)S(1)}, f32[1152,256]{1,0:T(8,128)S(1)}) custom-call(s32[1]{0:T(128)} %bitcast.me_ref, s32[288,2]{1,0:T(8,128)S(1)} %copy-done.2, bf16[256,256]{1,0:T(8,128)(2,1)S(1)} %copy-done, bf16[2,128,16]{2,1,0:T(8,128)(2,1)S(1)} %copy-done.1, bf16[8,2,128]{2,1,0:T(2,128)(2,1)S(1)} %copy-done.6, ...), custom_call_target="tpu_custom_call" | custom-call | flops 1000 | bytes 1000 | tf_op jit(solution)/shard_map/front/pallas_call | solution.py:154
  44.4 0.1 collective-permute-start.11
  44.5 2.0 %collective-permute-start.12 = (bf16[1152,256]{1,0:T(8,128)(2,1)}, bf16[1152,256]{1,0:T(8,128)(2,1)S(1)}, u32[]{:S(2)}, u32[]{:S(2)}) collective-permute-start(bf16[1152,256]{1,0:T(8,128)(2,1)} %get-tuple-element.68), channel_id=1, source_target_pairs={{0,2},{1,3},{2,0},{3,1},{4,6},{5,7},{6,4},{7,5},{8,10},{9,11},{10,... | collective-permute-start | bytes 1769480 | tf_op jit(solution)/shard_map/ppermute | solution.py:368
  46.5 2.2 %collective-permute-done.7.refs_1_ = bf16[512,384]{1,0:T(8,128)(2,1)S(1)} collective-permute-done((bf16[512,384]{1,0:T(8,128)(2,1)S(1)}, bf16[512,384]{1,0:T(8,128)(2,1)S(1)}, u32[]{:S(2)}, u32[]{:S(2)}) %collective-permute-start.7) | collective-permute-done | bytes 393248 | tf_op jit(solution)/shard_map/ppermute | solution.py:368
  48.7 0.1 share.12
  48.7 0.1 share.13
  48.8 0.1 share.14
  48.9 2.6 %collective-permute-start.10 = (bf16[512,384]{1,0:T(8,128)(2,1)S(1)}, bf16[512,384]{1,0:T(8,128)(2,1)S(1)}, u32[]{:S(2)}, u32[]{:S(2)}) collective-permute-start(bf16[512,384]{1,0:T(8,128)(2,1)S(1)} %share.14), channel_id=1, source_target_pairs={{0,4},{1,5},{2,6},{3,7},{4,0},{5,1},{6,2},{7,3},{8,12},{9,13},{10,... | collective-permute-start | bytes 1179656 | tf_op jit(solution)/shard_map/ppermute | solution.py:368
  51.5 1.7 %collective-permute-start.15 = (bf16[256,384]{1,0:T(8,128)(2,1)S(1)}, bf16[256,384]{1,0:T(8,128)(2,1)S(1)}, u32[]{:S(2)}, u32[]{:S(2)}) collective-permute-start(bf16[256,384]{1,0:T(8,128)(2,1)S(1)} %share.12), channel_id=1, source_target_pairs={{0,8},{1,9},{2,10},{3,11},{4,12},{5,13},{6,14},{7,15},{8,0},{9,1},... | collective-permute-start | bytes 589832 | tf_op jit(solution)/shard_map/ppermute | solution.py:368
  53.1 10.8 %collective-permute-done.10.refs_1_ = bf16[512,384]{1,0:T(8,128)(2,1)S(1)} collective-permute-done((bf16[512,384]{1,0:T(8,128)(2,1)S(1)}, bf16[512,384]{1,0:T(8,128)(2,1)S(1)}, u32[]{:S(2)}, u32[]{:S(2)}) %collective-permute-start.10) | collective-permute-done | bytes 393248 | tf_op jit(solution)/shard_map/ppermute | solution.py:368
  64.0 0.1 share.15
  64.0 1.0 collective-permute-start.17
  65.0 1.5 %collective-permute-start.13 = (bf16[256,256]{1,0:T(8,128)(2,1)S(1)}, bf16[256,256]{1,0:T(8,128)(2,1)S(1)}, u32[]{:S(2)}, u32[]{:S(2)}) collective-permute-start(bf16[256,256]{1,0:T(8,128)(2,1)S(1)} %share.13), channel_id=1, source_target_pairs={{0,2},{1,3},{2,0},{3,1},{4,6},{5,7},{6,4},{7,5},{8,10},{9,11},{10,... | collective-permute-start | bytes 393224 | tf_op jit(solution)/shard_map/ppermute | solution.py:368
  66.5 0.1 share.16
  66.6 2.5 %collective-permute-start.20 = (bf16[576,256]{1,0:T(8,128)(2,1)S(1)}, bf16[576,256]{1,0:T(8,128)(2,1)S(1)}, u32[]{:S(2)}, u32[]{:S(2)}) collective-permute-start(bf16[576,256]{1,0:T(8,128)(2,1)S(1)} %share.16), channel_id=1, source_target_pairs={{0,4},{1,5},{2,6},{3,7},{4,0},{5,1},{6,2},{7,3},{8,12},{9,13},{10,... | collective-permute-start | bytes 884744 | tf_op jit(solution)/shard_map/ppermute | solution.py:368
  69.1 4.5 %collective-permute-done.12.refs_0_ = bf16[1152,256]{1,0:T(8,128)(2,1)S(1)} collective-permute-done((bf16[1152,256]{1,0:T(8,128)(2,1)}, bf16[1152,256]{1,0:T(8,128)(2,1)S(1)}, u32[]{:S(2)}, u32[]{:S(2)}) %collective-permute-start.12) | collective-permute-done | bytes 589856 | tf_op jit(solution)/shard_map/ppermute | solution.py:368
  73.6 0.1 share.17
  73.7 2.1 %collective-permute-start.21 = (bf16[576,256]{1,0:T(8,128)(2,1)S(1)}, bf16[576,256]{1,0:T(8,128)(2,1)S(1)}, u32[]{:S(2)}, u32[]{:S(2)}) collective-permute-start(bf16[576,256]{1,0:T(8,128)(2,1)S(1)} %share.17), channel_id=1, source_target_pairs={{0,4},{1,5},{2,6},{3,7},{4,0},{5,1},{6,2},{7,3},{8,12},{9,13},{10,... | collective-permute-start | bytes 884744 | tf_op jit(solution)/shard_map/ppermute | solution.py:368
  75.8 0.3 collective-permute-done.13.refs_2_
  76.1 0.1 finish.5
  76.2 0.2 finish.6
  76.4 0.1 collective-permute-start.16
  76.5 0.2 finish.7
  76.6 0.6 collective-permute-start.18
  77.2 0.1 collective-permute-start.14
  77.3 2.5 %collective-permute-done.20.refs_1_ = bf16[576,256]{1,0:T(8,128)(2,1)S(1)} collective-permute-done((bf16[576,256]{1,0:T(8,128)(2,1)S(1)}, bf16[576,256]{1,0:T(8,128)(2,1)S(1)}, u32[]{:S(2)}, u32[]{:S(2)}) %collective-permute-start.20) | collective-permute-done | bytes 294944 | tf_op jit(solution)/shard_map/ppermute | solution.py:368
  79.8 0.4 collective-permute-start.22
  80.2 6.5 %collective-permute-done.21.refs_1_ = bf16[576,256]{1,0:T(8,128)(2,1)S(1)} collective-permute-done((bf16[576,256]{1,0:T(8,128)(2,1)S(1)}, bf16[576,256]{1,0:T(8,128)(2,1)S(1)}, u32[]{:S(2)}, u32[]{:S(2)}) %collective-permute-start.21) | collective-permute-done | bytes 294944 | tf_op jit(solution)/shard_map/ppermute | solution.py:368
  86.7 0.1 share.19
  86.8 0.1 collective-permute-start.23
  86.9 0.1 collective-permute-start.19
  87.0 5.1 %collective-permute-done.22.refs_2_ = bf16[288,256]{1,0:T(8,128)(2,1)S(1)} collective-permute-done((bf16[288,256]{1,0:T(8,128)(2,1)S(1)}, bf16[288,256]{1,0:T(8,128)(2,1)S(1)}, u32[]{:S(2)}, u32[]{:S(2)}) %collective-permute-start.22) | collective-permute-done | bytes 147488 | tf_op jit(solution)/shard_map/ppermute | solution.py:368
  92.1 0.1 finish.8
  92.2 0.1 collective-permute-start.24
  92.3 1.9 %collective-permute-done.19.edge_ref = f32[16,2048]{1,0:T(8,128)S(1)} collective-permute-done((f32[16,2048]{1,0:T(8,128)S(1)}, f32[16,2048]{1,0:T(8,128)S(1)}, u32[]{:S(2)}, u32[]{:S(2)}) %collective-permute-start.19) | collective-permute-done | bytes 131104 | tf_op jit(solution)/shard_map/ppermute | solution.py:508
  94.2 2.0 %gram.1 = (f32[384,160]{1,0:T(8,128)S(1)}, f32[2,160,1024]{2,1,0:T(8,128)S(1)}) custom-call(s32[1]{0:T(128)} %bitcast.me_ref, f32[16,2048]{1,0:T(8,128)S(1)} %collective-permute-done.19.edge_ref, s32[8,3072]{1,0:T(8,128)S(1)} %copy-done.4, f32[144,256]{1,0:T(8,128)S(1)} %get-tuple-element.87.refs_3_.refs_0_, ...), custom_call_target="tpu_custom_call" | custom-call | flops 1000 | bytes 1000 | tf_op jit(solution)/shard_map/gram/pallas_call | solution.py:222
  96.2 0.1 finish.9
  96.3 0.1 collective-permute-start.25
  96.4 1.4 %collective-permute-done.25.refs_3_ = f32[160,256]{1,0:T(8,128)S(1)} collective-permute-done((f32[160,256]{1,0:T(8,128)S(1)}, f32[160,256]{1,0:T(8,128)S(1)}, u32[]{:S(2)}, u32[]{:S(2)}) %collective-permute-start.25) | collective-permute-done | bytes 163872 | tf_op jit(solution)/shard_map/ppermute | solution.py:368
  97.8 5.3 %tail.1 = f32[8,2,3072]{2,1,0:T(2,128)} custom-call(s32[1]{0:T(128)} %bitcast.me_ref, f32[2,24]{1,0:T(2,128)S(1)} %copy-done.7, f32[384,160]{1,0:T(8,128)S(1)} %get-tuple-element.95.gram_ref, f32[2,160,1024]{2,1,0:T(8,128)S(1)} %get-tuple-element.96.window_ref, s32[8,3072]{1,0:T(8,128)S(1)} %copy-done.4, f32[160,256]{1,0:T(8,128)S(1)} %get-tuple-element.97.refs_0_, ...), custom_call_target="tpu_custom_call" | custom-call | flops 1000 | bytes 1000 | tf_op jit(solution)/shard_map/tail/pallas_call | solution.py:333
  (29 shorter events, 0.2 us)
Async XLA Ops:
  2.4 3.6 %copy-start = (bf16[256,256]{1,0:T(8,128)(2,1)S(1)}, bf16[256,256]{1,0:T(8,128)(2,1)}, u32[]{:S(2)}) copy-start(bf16[256,256]{1,0:T(8,128)(2,1)} %constant.15.clone.natural_ref) | copy-start | bytes 393220
  2.4 3.6 %copy-start.1 = (bf16[2,128,16]{2,1,0:T(8,128)(2,1)S(1)}, bf16[2,128,16]{2,1,0:T(8,128)(2,1)}, u32[]{:S(2)}) copy-start(bf16[2,128,16]{2,1,0:T(8,128)(2,1)} %constant.16.clone.picks_ref) | copy-start | bytes 24580
  2.4 3.6 %copy-start.3 = (s32[256,2]{1,0:T(8,128)S(1)}, s32[256,2]{1,0:T(8,128)}, u32[]{:S(2)}) copy-start(s32[256,2]{1,0:T(8,128)} %constant.14.clone.order_ref) | copy-start | bytes 6148
  2.4 3.6 %copy-start.6 = (bf16[8,2,128]{2,1,0:T(2,128)(2,1)S(1)}, bf16[8,2,128]{2,1,0:T(2,128)(2,1)}, u32[]{:S(2)}) copy-start(bf16[8,2,128]{2,1,0:T(2,128)(2,1)} %beam_ref.9) | copy-start | bytes 12292
  2.4 3.6 %collective-permute-start = (bf16[8,256,384]{2,1,0:T(8,128)(2,1)S(1)}, bf16[8,256,384]{2,1,0:T(8,128)(2,1)S(1)}, u32[]{:S(2)}, u32[]{:S(2)}) collective-permute-start(bf16[8,256,384]{2,1,0:T(8,128)(2,1)S(1)} %slice.2), channel_id=1, source_target_pairs={{0,1},{1,0},{2,3},{3,2},{4,5},{5,4},{6,7},{7,6},{8,9},{9,8},{10,11... | collective-permute-start | bytes 4718600 | tf_op jit(solution)/shard_map/ppermute | solution.py:368
  5.3 7.8 %collective-permute-start.1 = (bf16[8,256,384]{2,1,0:T(8,128)(2,1)S(1)}, bf16[8,256,384]{2,1,0:T(8,128)(2,1)S(1)}, u32[]{:S(2)}, u32[]{:S(2)}) collective-permute-start(bf16[8,256,384]{2,1,0:T(8,128)(2,1)S(1)} %slice.3), channel_id=1, source_target_pairs={{0,1},{1,0},{2,3},{3,2},{4,5},{5,4},{6,7},{7,6},{8,9},{9,8},{10,11... | collective-permute-start | bytes 4718600 | tf_op jit(solution)/shard_map/ppermute | solution.py:368
  10.0 7.2 %collective-permute-start.2 = (bf16[8,256,256]{2,1,0:T(8,128)(2,1)S(1)}, bf16[8,256,256]{2,1,0:T(8,128)(2,1)S(1)}, u32[]{:S(2)}, u32[]{:S(2)}) collective-permute-start(bf16[8,256,256]{2,1,0:T(8,128)(2,1)S(1)} %get-tuple-element.59), channel_id=1, source_target_pairs={{0,1},{1,0},{2,3},{3,2},{4,5},{5,4},{6,7},{7,6},{8,9},{9,8},{10,11... | collective-permute-start | bytes 3145736 | tf_op jit(solution)/shard_map/ppermute | solution.py:368
  10.4 6.8 %copy-start.5 = (s32[256,2]{1,0:T(8,128)S(1)}, s32[256,2]{1,0:T(8,128)}, u32[]{:S(2)}) copy-start(s32[256,2]{1,0:T(8,128)} %constant.17.clone.order_ref) | copy-start | bytes 6148
  10.4 21.0 %collective-permute-start.3 = (bf16[1024,384]{1,0:T(8,128)(2,1)S(1)}, bf16[1024,384]{1,0:T(8,128)(2,1)S(1)}, u32[]{:S(2)}, u32[]{:S(2)}) collective-permute-start(bf16[1024,384]{1,0:T(8,128)(2,1)S(1)} %get-tuple-element.55), channel_id=1, source_target_pairs={{0,2},{1,3},{2,0},{3,1},{4,6},{5,7},{6,4},{7,5},{8,10},{9,11},{10,... | collective-permute-start | bytes 2359304 | tf_op jit(solution)/shard_map/ppermute | solution.py:368
  17.1 21.1 %collective-permute-start.5 = (bf16[8,256,256]{2,1,0:T(8,128)(2,1)S(1)}, bf16[8,256,256]{2,1,0:T(8,128)(2,1)S(1)}, u32[]{:S(2)}, u32[]{:S(2)}) collective-permute-start(bf16[8,256,256]{2,1,0:T(8,128)(2,1)S(1)} %get-tuple-element.66), channel_id=1, source_target_pairs={{0,1},{1,0},{2,3},{3,2},{4,5},{5,4},{6,7},{7,6},{8,9},{9,8},{10,11... | collective-permute-start | bytes 3145736 | tf_op jit(solution)/shard_map/ppermute | solution.py:368
  20.2 21.5 %collective-permute-start.6 = (bf16[8,256,256]{2,1,0:T(8,128)(2,1)S(1)}, bf16[8,256,256]{2,1,0:T(8,128)(2,1)S(1)}, u32[]{:S(2)}, u32[]{:S(2)}) collective-permute-start(bf16[8,256,256]{2,1,0:T(8,128)(2,1)S(1)} %get-tuple-element.70), channel_id=1, source_target_pairs={{0,1},{1,0},{2,3},{3,2},{4,5},{5,4},{6,7},{7,6},{8,9},{9,8},{10,11... | collective-permute-start | bytes 3145736 | tf_op jit(solution)/shard_map/ppermute | solution.py:368
  20.7 14.8 %collective-permute-start.4 = (bf16[1024,256]{1,0:T(8,128)(2,1)S(1)}, bf16[1024,256]{1,0:T(8,128)(2,1)S(1)}, u32[]{:S(2)}, u32[]{:S(2)}) collective-permute-start(bf16[1024,256]{1,0:T(8,128)(2,1)S(1)} %get-tuple-element.62), channel_id=1, source_target_pairs={{0,4},{1,5},{2,6},{3,7},{4,0},{5,1},{6,2},{7,3},{8,12},{9,13},{10,... | collective-permute-start | bytes 1572872 | tf_op jit(solution)/shard_map/ppermute | solution.py:368
  22.3 26.5 %collective-permute-start.9 = (bf16[1024,384]{1,0:T(8,128)(2,1)S(1)}, bf16[1024,384]{1,0:T(8,128)(2,1)S(1)}, u32[]{:S(2)}, u32[]{:S(2)}) collective-permute-start(bf16[1024,384]{1,0:T(8,128)(2,1)S(1)} %get-tuple-element.57), channel_id=1, source_target_pairs={{0,2},{1,3},{2,0},{3,1},{4,6},{5,7},{6,4},{7,5},{8,10},{9,11},{10,... | collective-permute-start | bytes 2359304 | tf_op jit(solution)/shard_map/ppermute | solution.py:368
  31.5 6.6 %copy-start.2 = (s32[288,2]{1,0:T(8,128)S(1)}, s32[288,2]{1,0:T(8,128)}, u32[]{:S(2)}) copy-start(s32[288,2]{1,0:T(8,128)} %constant.18.clone.order_ref) | copy-start | bytes 6916
  31.6 17.1 %collective-permute-start.7 = (bf16[512,384]{1,0:T(8,128)(2,1)S(1)}, bf16[512,384]{1,0:T(8,128)(2,1)S(1)}, u32[]{:S(2)}, u32[]{:S(2)}) collective-permute-start(bf16[512,384]{1,0:T(8,128)(2,1)S(1)} %share.10), channel_id=1, source_target_pairs={{0,4},{1,5},{2,6},{3,7},{4,0},{5,1},{6,2},{7,3},{8,12},{9,13},{10,... | collective-permute-start | bytes 1179656 | tf_op jit(solution)/shard_map/ppermute | solution.py:368
  35.5 13.2 %collective-permute-start.8 = (bf16[512,256]{1,0:T(8,128)(2,1)S(1)}, bf16[512,256]{1,0:T(8,128)(2,1)S(1)}, u32[]{:S(2)}, u32[]{:S(2)}) collective-permute-start(bf16[512,256]{1,0:T(8,128)(2,1)S(1)} %share.11), channel_id=1, source_target_pairs={{0,8},{1,9},{2,10},{3,11},{4,12},{5,13},{6,14},{7,15},{8,0},{9,1},... | collective-permute-start | bytes 786440 | tf_op jit(solution)/shard_map/ppermute | solution.py:368
  44.4 22.1 %collective-permute-start.11 = (bf16[1152,256]{1,0:T(8,128)(2,1)S(1)}, bf16[1152,256]{1,0:T(8,128)(2,1)S(1)}, u32[]{:S(2)}, u32[]{:S(2)}) collective-permute-start(bf16[1152,256]{1,0:T(8,128)(2,1)S(1)} %get-tuple-element.73), channel_id=1, source_target_pairs={{0,2},{1,3},{2,0},{3,1},{4,6},{5,7},{6,4},{7,5},{8,10},{9,11},{10,... | collective-permute-start | bytes 1769480 | tf_op jit(solution)/shard_map/ppermute | solution.py:368
  44.5 29.2 %collective-permute-start.12 = (bf16[1152,256]{1,0:T(8,128)(2,1)}, bf16[1152,256]{1,0:T(8,128)(2,1)S(1)}, u32[]{:S(2)}, u32[]{:S(2)}) collective-permute-start(bf16[1152,256]{1,0:T(8,128)(2,1)} %get-tuple-element.68), channel_id=1, source_target_pairs={{0,2},{1,3},{2,0},{3,1},{4,6},{5,7},{6,4},{7,5},{8,10},{9,11},{10,... | collective-permute-start | bytes 1769480 | tf_op jit(solution)/shard_map/ppermute | solution.py:368
  48.9 15.1 %collective-permute-start.10 = (bf16[512,384]{1,0:T(8,128)(2,1)S(1)}, bf16[512,384]{1,0:T(8,128)(2,1)S(1)}, u32[]{:S(2)}, u32[]{:S(2)}) collective-permute-start(bf16[512,384]{1,0:T(8,128)(2,1)S(1)} %share.14), channel_id=1, source_target_pairs={{0,4},{1,5},{2,6},{3,7},{4,0},{5,1},{6,2},{7,3},{8,12},{9,13},{10,... | collective-permute-start | bytes 1179656 | tf_op jit(solution)/shard_map/ppermute | solution.py:368
  51.5 24.8 %collective-permute-start.15 = (bf16[256,384]{1,0:T(8,128)(2,1)S(1)}, bf16[256,384]{1,0:T(8,128)(2,1)S(1)}, u32[]{:S(2)}, u32[]{:S(2)}) collective-permute-start(bf16[256,384]{1,0:T(8,128)(2,1)S(1)} %share.12), channel_id=1, source_target_pairs={{0,8},{1,9},{2,10},{3,11},{4,12},{5,13},{6,14},{7,15},{8,0},{9,1},... | collective-permute-start | bytes 589832 | tf_op jit(solution)/shard_map/ppermute | solution.py:368
  64.0 12.4 %collective-permute-start.17 = (bf16[256,384]{1,0:T(8,128)(2,1)S(1)}, bf16[256,384]{1,0:T(8,128)(2,1)S(1)}, u32[]{:S(2)}, u32[]{:S(2)}) collective-permute-start(bf16[256,384]{1,0:T(8,128)(2,1)S(1)} %share.15), channel_id=1, source_target_pairs={{0,8},{1,9},{2,10},{3,11},{4,12},{5,13},{6,14},{7,15},{8,0},{9,1},... | collective-permute-start | bytes 589832 | tf_op jit(solution)/shard_map/ppermute | solution.py:368
  65.0 11.1 %collective-permute-start.13 = (bf16[256,256]{1,0:T(8,128)(2,1)S(1)}, bf16[256,256]{1,0:T(8,128)(2,1)S(1)}, u32[]{:S(2)}, u32[]{:S(2)}) collective-permute-start(bf16[256,256]{1,0:T(8,128)(2,1)S(1)} %share.13), channel_id=1, source_target_pairs={{0,2},{1,3},{2,0},{3,1},{4,6},{5,7},{6,4},{7,5},{8,10},{9,11},{10,... | collective-permute-start | bytes 393224 | tf_op jit(solution)/shard_map/ppermute | solution.py:368
  66.6 13.1 %collective-permute-start.20 = (bf16[576,256]{1,0:T(8,128)(2,1)S(1)}, bf16[576,256]{1,0:T(8,128)(2,1)S(1)}, u32[]{:S(2)}, u32[]{:S(2)}) collective-permute-start(bf16[576,256]{1,0:T(8,128)(2,1)S(1)} %share.16), channel_id=1, source_target_pairs={{0,4},{1,5},{2,6},{3,7},{4,0},{5,1},{6,2},{7,3},{8,12},{9,13},{10,... | collective-permute-start | bytes 884744 | tf_op jit(solution)/shard_map/ppermute | solution.py:368
  73.7 13.1 %collective-permute-start.21 = (bf16[576,256]{1,0:T(8,128)(2,1)S(1)}, bf16[576,256]{1,0:T(8,128)(2,1)S(1)}, u32[]{:S(2)}, u32[]{:S(2)}) collective-permute-start(bf16[576,256]{1,0:T(8,128)(2,1)S(1)} %share.17), channel_id=1, source_target_pairs={{0,4},{1,5},{2,6},{3,7},{4,0},{5,1},{6,2},{7,3},{8,12},{9,13},{10,... | collective-permute-start | bytes 884744 | tf_op jit(solution)/shard_map/ppermute | solution.py:368
  76.4 10.5 %collective-permute-start.16 = (f32[144,384]{1,0:T(8,128)S(1)}, f32[144,384]{1,0:T(8,128)S(1)}, u32[]{:S(2)}, u32[]{:S(2)}) collective-permute-start(f32[144,384]{1,0:T(8,128)S(1)} %get-tuple-element.84), channel_id=1, source_target_pairs={{0,1},{1,0},{2,3},{3,2},{4,5},{5,4},{6,7},{7,6},{8,9},{9,8},{10,11... | collective-permute-start | bytes 663560 | tf_op jit(solution)/shard_map/ppermute | solution.py:368
  76.6 10.3 %collective-permute-start.18 = (f32[144,384]{1,0:T(8,128)S(1)}, f32[144,384]{1,0:T(8,128)S(1)}, u32[]{:S(2)}, u32[]{:S(2)}) collective-permute-start(f32[144,384]{1,0:T(8,128)S(1)} %get-tuple-element.86), channel_id=1, source_target_pairs={{0,1},{1,0},{2,3},{3,2},{4,5},{5,4},{6,7},{7,6},{8,9},{9,8},{10,11... | collective-permute-start | bytes 663560 | tf_op jit(solution)/shard_map/ppermute | solution.py:368
  77.2 9.7 %collective-permute-start.14 = (f32[144,256]{1,0:T(8,128)S(1)}, f32[144,256]{1,0:T(8,128)S(1)}, u32[]{:S(2)}, u32[]{:S(2)}) collective-permute-start(f32[144,256]{1,0:T(8,128)S(1)} %get-tuple-element.82), channel_id=1, source_target_pairs={{0,1},{1,0},{2,3},{3,2},{4,5},{5,4},{6,7},{7,6},{8,9},{9,8},{10,11... | collective-permute-start | bytes 442376 | tf_op jit(solution)/shard_map/ppermute | solution.py:368
  79.8 12.3 %collective-permute-start.22 = (bf16[288,256]{1,0:T(8,128)(2,1)S(1)}, bf16[288,256]{1,0:T(8,128)(2,1)S(1)}, u32[]{:S(2)}, u32[]{:S(2)}) collective-permute-start(bf16[288,256]{1,0:T(8,128)(2,1)S(1)} %share.18), channel_id=1, source_target_pairs={{0,8},{1,9},{2,10},{3,11},{4,12},{5,13},{6,14},{7,15},{8,0},{9,1},... | collective-permute-start | bytes 442376 | tf_op jit(solution)/shard_map/ppermute | solution.py:368
  86.8 9.4 %collective-permute-start.23 = (bf16[288,256]{1,0:T(8,128)(2,1)S(1)}, bf16[288,256]{1,0:T(8,128)(2,1)S(1)}, u32[]{:S(2)}, u32[]{:S(2)}) collective-permute-start(bf16[288,256]{1,0:T(8,128)(2,1)S(1)} %share.19), channel_id=1, source_target_pairs={{0,8},{1,9},{2,10},{3,11},{4,12},{5,13},{6,14},{7,15},{8,0},{9,1},... | collective-permute-start | bytes 442376 | tf_op jit(solution)/shard_map/ppermute | solution.py:368
  86.9 7.3 %copy-start.4 = (s32[8,3072]{1,0:T(8,128)S(1)}, s32[8,3072]{1,0:T(8,128)}, u32[]{:S(2)}) copy-start(s32[8,3072]{1,0:T(8,128)} %mask_ref.2) | copy-start | bytes 294916
  86.9 7.3 %collective-permute-start.19 = (f32[16,2048]{1,0:T(8,128)S(1)}, f32[16,2048]{1,0:T(8,128)S(1)}, u32[]{:S(2)}, u32[]{:S(2)}) collective-permute-start(f32[16,2048]{1,0:T(8,128)S(1)} %edges.1), channel_id=1, source_target_pairs={{2,1},{4,3},{6,5},{8,7},{10,9},{12,11},{14,13},{0,15},{1,2},{3,4},... | collective-permute-start | bytes 393224 | tf_op jit(solution)/shard_map/ppermute | solution.py:508
  92.2 5.6 %copy-start.7 = (f32[2,24]{1,0:T(2,128)S(1)}, f32[2,24]{1,0:T(2,128)}, u32[]{:S(2)}) copy-start(f32[2,24]{1,0:T(2,128)} %steer_ref.1) | copy-start | bytes 580
  92.2 4.2 %collective-permute-start.24 = (f32[160,256]{1,0:T(8,128)S(1)}, f32[160,256]{1,0:T(8,128)S(1)}, u32[]{:S(2)}, u32[]{:S(2)}) collective-permute-start(f32[160,256]{1,0:T(8,128)S(1)} %get-tuple-element.93), channel_id=1, source_target_pairs={{0,1},{1,0},{2,3},{3,2},{4,5},{5,4},{6,7},{7,6},{8,9},{9,8},{10,11... | collective-permute-start | bytes 491528 | tf_op jit(solution)/shard_map/ppermute | solution.py:368
  96.3 1.5 %collective-permute-start.25 = (f32[160,256]{1,0:T(8,128)S(1)}, f32[160,256]{1,0:T(8,128)S(1)}, u32[]{:S(2)}, u32[]{:S(2)}) collective-permute-start(f32[160,256]{1,0:T(8,128)S(1)} %get-tuple-element.100), channel_id=1, source_target_pairs={{0,1},{1,0},{2,3},{3,2},{4,5},{5,4},{6,7},{7,6},{8,9},{9,8},{10,11... | collective-permute-start | bytes 491528 | tf_op jit(solution)/shard_map/ppermute | solution.py:368

commit v4 on v3

--- a/solution.py
+++ b/solution.py
@@ -261,26 +261,32 @@
     system = jnp.where(lane == 3 * rows + beams, target_im, system)
 
     def swapped(row):
-        return jnp.where(real_lane, -pltpu.roll(row, 128 - beams, 2), pltpu.roll(row, beams, 2))
-
+        return jnp.where(real_lane[0], -pltpu.roll(row, 128 - beams, 1), pltpu.roll(row, beams, 1))
+
+    across = jnp.transpose(system, (1, 0, 2))
+    held = [across[i] for i in range(order)]
     for k in range(order):
         spot = k // beams * rows + k % beams
-        pivot_row = system[:, k : k + 1, :]
+        pivot_row = held[k]
         turned = swapped(pivot_row)
-        pivot = jnp.broadcast_to(pivot_row[:, :, spot : spot + 1], pivot_row.shape)
-        factor_re = system[:, :, spot : spot + 1]
-        factor_im = system[:, :, spot + beams : spot + beams + 1]
-        scale = 1.0 / pivot
-        pivot_row = pivot_row * scale
-        changed = system - factor_re * pivot_row - factor_im * (turned * scale)
-        system = jnp.where(row_at == k, pivot_row, changed)
-
-    solved_re = system[:, :, 3 * rows : 3 * rows + 1]
-    solved_im = system[:, :, 3 * rows + beams : 3 * rows + beams + 1]
-    response = jnp.sum(solved_re * target_re + solved_im * target_im, axis=1, keepdims=True)
-    weight_re = jnp.broadcast_to(solved_re / response, (bins_here, order, 128))
-    weight_im = jnp.broadcast_to(solved_im / response, (bins_here, order, 128))
-    return weight_re, weight_im
+        scale = 1.0 / jnp.broadcast_to(pivot_row[:, spot : spot + 1], pivot_row.shape)
+        pivot_row, turned = pivot_row * scale, turned * scale
+        for i in range(order):
+            if i != k:
+                factor_re = held[i][:, spot : spot + 1]
+                factor_im = held[i][:, spot + beams : spot + beams + 1]
+                held[i] = held[i] - factor_re * pivot_row - factor_im * turned
+        held[k] = pivot_row
+
+    solved_re = [row[:, 3 * rows : 3 * rows + 1] for row in held]
+    solved_im = [row[:, 3 * rows + beams : 3 * rows + beams + 1] for row in held]
+    response = jnp.zeros((bins_here, 1), F32)
+    for i in range(order):
+        response += solved_re[i] * target_re[0, i : i + 1] + solved_im[i] * target_im[0, i : i + 1]
+    scale = 1.0 / jnp.broadcast_to(response, (bins_here, 128))
+    weight_re = jnp.stack([part * scale for part in solved_re], axis=0)
+    weight_im = jnp.stack([part * scale for part in solved_im], axis=0)
+    return jnp.transpose(weight_re, (1, 0, 2)), jnp.transpose(weight_im, (1, 0, 2))
 
 
 def filter_gates(out_ref, at, blocks, weight_re, weight_im, beams):
@@ -347,15 +353,23 @@
 
 def other_half(me, echo, start, size):
     elem_dev, rows_in, gate_count = echo.shape
-    first, across = start // 128, gate_count // 2 // 128
-    block = (elem_dev, rows_in, 128)
+    each = elem_dev // 2
+
+    def lane(me):
+        return pl.multiple_of((1 - me[0] % 2) * (gate_count // 2) + start, 128)
+
     return pl.pallas_call(
         slice_kernel,
         grid_spec=pltpu.PrefetchScalarGridSpec(
             num_scalar_prefetch=1,
-            grid=(size // 128,),
-            in_specs=[pl.BlockSpec(block, lambda i, me: (0, 0, (1 - me[0] % 2) * across + first + i))],
-            out_specs=pl.BlockSpec(block, lambda i, me: (0, 0, i)),
+            grid=(2,),
+            in_specs=[
+                pl.BlockSpec(
+                    (pl.Element(each), pl.Element(rows_in), pl.Element(size)),
+                    lambda i, me: (i * each, 0, lane(me)),
+                )
+            ],
+            out_specs=pl.BlockSpec((each, rows_in, size), lambda i, me: (i, 0, 0)),
         ),
         out_shape=jax.ShapeDtypeStruct((elem_dev, rows_in, size), BF16),
         compiler_params=pltpu.CompilerParams(vmem_limit_bytes=VMEM),
@@ -518,7 +532,7 @@
         elif stage == 1:
             strides = orders[CHUNKS[c][1]]
             later = turns.index(c) + AHEAD
-            later = turns[later] if later < chunks else None
+            later = turns[later] if later < chunks and (turns[later], 0) not in steps else None
             parts = 1 + CHUNKS[c][3]
             out = front(
                 at, strides, CHUNKS[c][2], 2 * bins_here, beam_weights,

time: 105 us -> 104 us (level)
  Pallas kernels: 30.4 us -> 28.3 us
    pallas_call x2, Pallas kernels: 4.76 us -> 2.94 us  [other_half(): pl.pallas_call(slice_kernel, grid_spec=pltpu.PrefetchScalarGridSpec(num_s...]
  transfers between devices with their start and end apart: 26 -> 26, of which waited for: 12 -> 12; matrix products, arithmetic and copies ran while one was open for 0% -> 0% of each run, Pallas kernels for 22% -> 21%
where the time goes in v4:
time: 104 us; the launch traced here: 102 us
  waiting for transfers between devices  47.2 us (45%)
  Pallas kernels  28.3 us (27%)
  starting transfers between devices  26 us (25%)
    ppermute x25, waiting for transfers between devices, swap(): return lax.ppermute(x, 'elem', [(i, i ^ stride) for i in range(count)])  45.3 us
    ppermute x25, starting transfers between devices, swap(): return lax.ppermute(x, 'elem', [(i, i ^ stride) for i in range(count)])  26 us
    pallas_call x5, Pallas kernels, front(): pl.pallas_call(functools.partial(front_kernel, bins_chip, ahead is not No...  17.1 us
    pallas_call x1, Pallas kernels, tail(): pl.pallas_call(tail_kernel, in_specs=[pl.BlockSpec(memory_space=pltpu.SME...  5.06 us
    pallas_call x2, Pallas kernels, other_half(): pl.pallas_call(slice_kernel, grid_spec=pltpu.PrefetchScalarGridSpec(num_s...  2.94 us
  transfers between devices with their start and end apart: 26, of which 12 were waited for; matrix products, arithmetic and copies ran while one was open for 0% of the time, Pallas kernels for 21%

profile of v4, /device:TPU:0, one launch (start us, length us, event | category | flops | bytes accessed | tf_op | source)
XLA Modules:
  0.0 101.9 jit_solution(13103842992564696178)
XLA Ops:
  0.0 1.5 %slice.2 = bf16[8,256,384]{2,1,0:T(8,128)(2,1)S(1)} custom-call(s32[1]{0:T(128)} %bitcast.me_ref, bf16[8,256,3072]{2,1,0:T(8,128)(2,1)} %bitcast.2), custom_call_target="tpu_custom_call" | custom-call | flops 1000 | bytes 1000 | tf_op jit(solution)/shard_map/slice/pallas_call | solution.py:361
  1.5 0.0 copy-start
  1.5 0.0 copy-start.1
  1.5 0.0 copy-start.3
  1.5 0.5 collective-permute-start
  2.0 1.5 %slice.3 = bf16[8,256,384]{2,1,0:T(8,128)(2,1)S(1)} custom-call(s32[1]{0:T(128)} %bitcast.me_ref, bf16[8,256,3072]{2,1,0:T(8,128)(2,1)} %bitcast.3), custom_call_target="tpu_custom_call" | custom-call | flops 1000 | bytes 1000 | tf_op jit(solution)/shard_map/slice/pallas_call | solution.py:361
  3.5 0.1 collective-permute-start.1
  3.7 1.4 %collective-permute-done.theirs_ref = bf16[8,256,384]{2,1,0:T(8,128)(2,1)S(1)} collective-permute-done((bf16[8,256,384]{2,1,0:T(8,128)(2,1)S(1)}, bf16[8,256,384]{2,1,0:T(8,128)(2,1)S(1)}, u32[]{:S(2)}, u32[]{:S(2)}) %collective-permute-start) | collective-permute-done | bytes 1572896 | tf_op jit(solution)/shard_map/ppermute | solution.py:382
  5.1 4.0 %front.5 = (bf16[1024,384]{1,0:T(8,128)(2,1)S(1)}, f32[1024,384]{1,0:T(8,128)S(1)}, bf16[8,256,256]{2,1,0:T(8,128)(2,1)S(1)}) custom-call(s32[1]{0:T(128)} %bitcast.me_ref, s32[256,2]{1,0:T(8,128)S(1)} %copy-done.3, bf16[256,256]{1,0:T(8,128)(2,1)S(1)} %copy-done, bf16[2,128,16]{2,1,0:T(8,128)(2,1)S(1)} %copy-done.1, bf16[8,2,128]{2,1,0:T(2,128)(2,1)S(1)} %copy-done.6, ...), custom_call_target="tpu_custom_call" | custom-call | flops 1000 | bytes 1000 | tf_op jit(solution)/shard_map/front/pallas_call | solution.py:154
  9.1 0.4 collective-permute-start.2
  9.5 2.7 %collective-permute-start.3 = (bf16[1024,384]{1,0:T(8,128)(2,1)S(1)}, bf16[1024,384]{1,0:T(8,128)(2,1)S(1)}, u32[]{:S(2)}, u32[]{:S(2)}) collective-permute-start(bf16[1024,384]{1,0:T(8,128)(2,1)S(1)} %get-tuple-element.55), channel_id=1, source_target_pairs={{0,2},{1,3},{2,0},{3,1},{4,6},{5,7},{6,4},{7,5},{8,10},{9,11},{10,... | collective-permute-start | bytes 2359304 | tf_op jit(solution)/shard_map/ppermute | solution.py:382
  12.2 4.0 %front.6 = (bf16[1024,384]{1,0:T(8,128)(2,1)S(1)}, f32[1024,384]{1,0:T(8,128)S(1)}, bf16[8,256,256]{2,1,0:T(8,128)(2,1)S(1)}) custom-call(s32[1]{0:T(128)} %bitcast.me_ref, s32[256,2]{1,0:T(8,128)S(1)} %copy-done.3, bf16[256,256]{1,0:T(8,128)(2,1)S(1)} %copy-done, bf16[2,128,16]{2,1,0:T(8,128)(2,1)S(1)} %copy-done.1, bf16[8,2,128]{2,1,0:T(2,128)(2,1)S(1)} %copy-done.6, ...), custom_call_target="tpu_custom_call" | custom-call | flops 1000 | bytes 1000 | tf_op jit(solution)/shard_map/front/pallas_call | solution.py:154
  16.1 0.1 collective-permute-start.5
  16.3 3.0 %front.7 = (bf16[1024,256]{1,0:T(8,128)(2,1)S(1)}, f32[1024,256]{1,0:T(8,128)S(1)}, bf16[8,256,256]{2,1,0:T(8,128)(2,1)S(1)}) custom-call(s32[1]{0:T(128)} %bitcast.me_ref, s32[256,2]{1,0:T(8,128)S(1)} %copy-done.5, bf16[256,256]{1,0:T(8,128)(2,1)S(1)} %copy-done, bf16[2,128,16]{2,1,0:T(8,128)(2,1)S(1)} %copy-done.1, bf16[8,2,128]{2,1,0:T(2,128)(2,1)S(1)} %copy-done.6, ...), custom_call_target="tpu_custom_call" | custom-call | flops 1000 | bytes 1000 | tf_op jit(solution)/shard_map/front/pallas_call | solution.py:154
  19.3 0.5 collective-permute-start.6
  19.8 1.6 %collective-permute-start.4 = (bf16[1024,256]{1,0:T(8,128)(2,1)S(1)}, bf16[1024,256]{1,0:T(8,128)(2,1)S(1)}, u32[]{:S(2)}, u32[]{:S(2)}) collective-permute-start(bf16[1024,256]{1,0:T(8,128)(2,1)S(1)} %get-tuple-element.62), channel_id=1, source_target_pairs={{0,4},{1,5},{2,6},{3,7},{4,0},{5,1},{6,2},{7,3},{8,12},{9,13},{10,... | collective-permute-start | bytes 1572872 | tf_op jit(solution)/shard_map/ppermute | solution.py:382
  21.4 0.5 collective-permute-start.9
  21.9 8.7 %collective-permute-done.3.refs_0_ = bf16[1024,384]{1,0:T(8,128)(2,1)S(1)} collective-permute-done((bf16[1024,384]{1,0:T(8,128)(2,1)S(1)}, bf16[1024,384]{1,0:T(8,128)(2,1)S(1)}, u32[]{:S(2)}, u32[]{:S(2)}) %collective-permute-start.3) | collective-permute-done | bytes 786464 | tf_op jit(solution)/shard_map/ppermute | solution.py:382
  30.6 0.1 share.10
  30.6 0.0 copy-start.2
  30.7 2.1 %collective-permute-start.7 = (bf16[512,384]{1,0:T(8,128)(2,1)S(1)}, bf16[512,384]{1,0:T(8,128)(2,1)S(1)}, u32[]{:S(2)}, u32[]{:S(2)}) collective-permute-start(bf16[512,384]{1,0:T(8,128)(2,1)S(1)} %share.10), channel_id=1, source_target_pairs={{0,4},{1,5},{2,6},{3,7},{4,0},{5,1},{6,2},{7,3},{8,12},{9,13},{10,... | collective-permute-start | bytes 1179656 | tf_op jit(solution)/shard_map/ppermute | solution.py:382
  32.7 1.8 %collective-permute-done.4.refs_0_ = bf16[1024,256]{1,0:T(8,128)(2,1)S(1)} collective-permute-done((bf16[1024,256]{1,0:T(8,128)(2,1)S(1)}, bf16[1024,256]{1,0:T(8,128)(2,1)S(1)}, u32[]{:S(2)}, u32[]{:S(2)}) %collective-permute-start.4) | collective-permute-done | bytes 524320 | tf_op jit(solution)/shard_map/ppermute | solution.py:382
  34.6 2.6 %collective-permute-start.8 = (bf16[512,256]{1,0:T(8,128)(2,1)S(1)}, bf16[512,256]{1,0:T(8,128)(2,1)S(1)}, u32[]{:S(2)}, u32[]{:S(2)}) collective-permute-start(bf16[512,256]{1,0:T(8,128)(2,1)S(1)} %share.11), channel_id=1, source_target_pairs={{0,8},{1,9},{2,10},{3,11},{4,12},{5,13},{6,14},{7,15},{8,0},{9,1},... | collective-permute-start | bytes 786440 | tf_op jit(solution)/shard_map/ppermute | solution.py:382
  37.3 3.5 %front.8 = (bf16[1152,256]{1,0:T(8,128)(2,1)}, f32[1152,256]{1,0:T(8,128)S(1)}) custom-call(s32[1]{0:T(128)} %bitcast.me_ref, s32[288,2]{1,0:T(8,128)S(1)} %copy-done.2, bf16[256,256]{1,0:T(8,128)(2,1)S(1)} %copy-done, bf16[2,128,16]{2,1,0:T(8,128)(2,1)S(1)} %copy-done.1, bf16[8,2,128]{2,1,0:T(2,128)(2,1)S(1)} %copy-done.6, bf16[8,256,3072]{2,1,0:T(8,128)(2,1)} %bitcast.10, ...), custom_call_target="tpu_custom_call" | custom-call | flops 1000 | bytes 1000 | tf_op jit(solution)/shard_map/front/pallas_call | solution.py:154
  40.8 2.7 %front.9 = (bf16[1152,256]{1,0:T(8,128)(2,1)S(1)}, f32[1152,256]{1,0:T(8,128)S(1)}) custom-call(s32[1]{0:T(128)} %bitcast.me_ref, s32[288,2]{1,0:T(8,128)S(1)} %copy-done.2, bf16[256,256]{1,0:T(8,128)(2,1)S(1)} %copy-done, bf16[2,128,16]{2,1,0:T(8,128)(2,1)S(1)} %copy-done.1, bf16[8,2,128]{2,1,0:T(2,128)(2,1)S(1)} %copy-done.6, ...), custom_call_target="tpu_custom_call" | custom-call | flops 1000 | bytes 1000 | tf_op jit(solution)/shard_map/front/pallas_call | solution.py:154
  43.5 0.1 collective-permute-start.11
  43.5 2.0 %collective-permute-start.12 = (bf16[1152,256]{1,0:T(8,128)(2,1)}, bf16[1152,256]{1,0:T(8,128)(2,1)S(1)}, u32[]{:S(2)}, u32[]{:S(2)}) collective-permute-start(bf16[1152,256]{1,0:T(8,128)(2,1)} %get-tuple-element.68), channel_id=1, source_target_pairs={{0,2},{1,3},{2,0},{3,1},{4,6},{5,7},{6,4},{7,5},{8,10},{9,11},{10,... | collective-permute-start | bytes 1769480 | tf_op jit(solution)/shard_map/ppermute | solution.py:382
  45.5 2.2 %collective-permute-done.7.refs_1_ = bf16[512,384]{1,0:T(8,128)(2,1)S(1)} collective-permute-done((bf16[512,384]{1,0:T(8,128)(2,1)S(1)}, bf16[512,384]{1,0:T(8,128)(2,1)S(1)}, u32[]{:S(2)}, u32[]{:S(2)}) %collective-permute-start.7) | collective-permute-done | bytes 393248 | tf_op jit(solution)/shard_map/ppermute | solution.py:382
  47.7 0.1 share.12
  47.8 0.1 share.13
  47.9 0.1 share.14
  48.0 2.6 %collective-permute-start.10 = (bf16[512,384]{1,0:T(8,128)(2,1)S(1)}, bf16[512,384]{1,0:T(8,128)(2,1)S(1)}, u32[]{:S(2)}, u32[]{:S(2)}) collective-permute-start(bf16[512,384]{1,0:T(8,128)(2,1)S(1)} %share.14), channel_id=1, source_target_pairs={{0,4},{1,5},{2,6},{3,7},{4,0},{5,1},{6,2},{7,3},{8,12},{9,13},{10,... | collective-permute-start | bytes 1179656 | tf_op jit(solution)/shard_map/ppermute | solution.py:382
  50.5 1.7 %collective-permute-start.15 = (bf16[256,384]{1,0:T(8,128)(2,1)S(1)}, bf16[256,384]{1,0:T(8,128)(2,1)S(1)}, u32[]{:S(2)}, u32[]{:S(2)}) collective-permute-start(bf16[256,384]{1,0:T(8,128)(2,1)S(1)} %share.12), channel_id=1, source_target_pairs={{0,8},{1,9},{2,10},{3,11},{4,12},{5,13},{6,14},{7,15},{8,0},{9,1},... | collective-permute-start | bytes 589832 | tf_op jit(solution)/shard_map/ppermute | solution.py:382
  52.2 10.8 %collective-permute-done.10.refs_1_ = bf16[512,384]{1,0:T(8,128)(2,1)S(1)} collective-permute-done((bf16[512,384]{1,0:T(8,128)(2,1)S(1)}, bf16[512,384]{1,0:T(8,128)(2,1)S(1)}, u32[]{:S(2)}, u32[]{:S(2)}) %collective-permute-start.10) | collective-permute-done | bytes 393248 | tf_op jit(solution)/shard_map/ppermute | solution.py:382
  63.1 0.1 share.15
  63.1 1.0 collective-permute-start.17
  64.1 1.5 %collective-permute-start.13 = (bf16[256,256]{1,0:T(8,128)(2,1)S(1)}, bf16[256,256]{1,0:T(8,128)(2,1)S(1)}, u32[]{:S(2)}, u32[]{:S(2)}) collective-permute-start(bf16[256,256]{1,0:T(8,128)(2,1)S(1)} %share.13), channel_id=1, source_target_pairs={{0,2},{1,3},{2,0},{3,1},{4,6},{5,7},{6,4},{7,5},{8,10},{9,11},{10,... | collective-permute-start | bytes 393224 | tf_op jit(solution)/shard_map/ppermute | solution.py:382
  65.6 0.1 share.16
  65.7 2.5 %collective-permute-start.20 = (bf16[576,256]{1,0:T(8,128)(2,1)S(1)}, bf16[576,256]{1,0:T(8,128)(2,1)S(1)}, u32[]{:S(2)}, u32[]{:S(2)}) collective-permute-start(bf16[576,256]{1,0:T(8,128)(2,1)S(1)} %share.16), channel_id=1, source_target_pairs={{0,4},{1,5},{2,6},{3,7},{4,0},{5,1},{6,2},{7,3},{8,12},{9,13},{10,... | collective-permute-start | bytes 884744 | tf_op jit(solution)/shard_map/ppermute | solution.py:382
  68.2 4.5 %collective-permute-done.12.refs_0_ = bf16[1152,256]{1,0:T(8,128)(2,1)S(1)} collective-permute-done((bf16[1152,256]{1,0:T(8,128)(2,1)}, bf16[1152,256]{1,0:T(8,128)(2,1)S(1)}, u32[]{:S(2)}, u32[]{:S(2)}) %collective-permute-start.12) | collective-permute-done | bytes 589856 | tf_op jit(solution)/shard_map/ppermute | solution.py:382
  72.7 0.1 share.17
  72.8 2.1 %collective-permute-start.21 = (bf16[576,256]{1,0:T(8,128)(2,1)S(1)}, bf16[576,256]{1,0:T(8,128)(2,1)S(1)}, u32[]{:S(2)}, u32[]{:S(2)}) collective-permute-start(bf16[576,256]{1,0:T(8,128)(2,1)S(1)} %share.17), channel_id=1, source_target_pairs={{0,4},{1,5},{2,6},{3,7},{4,0},{5,1},{6,2},{7,3},{8,12},{9,13},{10,... | collective-permute-start | bytes 884744 | tf_op jit(solution)/shard_map/ppermute | solution.py:382
  74.8 0.3 collective-permute-done.13.refs_2_
  75.2 0.1 finish.5
  75.3 0.2 finish.6
  75.5 0.1 collective-permute-start.16
  75.5 0.2 finish.7
  75.7 0.6 collective-permute-start.18
  76.3 0.1 collective-permute-start.14
  76.3 2.5 %collective-permute-done.20.refs_1_ = bf16[576,256]{1,0:T(8,128)(2,1)S(1)} collective-permute-done((bf16[576,256]{1,0:T(8,128)(2,1)S(1)}, bf16[576,256]{1,0:T(8,128)(2,1)S(1)}, u32[]{:S(2)}, u32[]{:S(2)}) %collective-permute-start.20) | collective-permute-done | bytes 294944 | tf_op jit(solution)/shard_map/ppermute | solution.py:382
  78.9 0.4 collective-permute-start.22
  79.3 6.5 %collective-permute-done.21.refs_1_ = bf16[576,256]{1,0:T(8,128)(2,1)S(1)} collective-permute-done((bf16[576,256]{1,0:T(8,128)(2,1)S(1)}, bf16[576,256]{1,0:T(8,128)(2,1)S(1)}, u32[]{:S(2)}, u32[]{:S(2)}) %collective-permute-start.21) | collective-permute-done | bytes 294944 | tf_op jit(solution)/shard_map/ppermute | solution.py:382
  85.8 0.1 share.19
  85.9 0.1 collective-permute-start.23
  86.0 0.1 collective-permute-start.19
  86.1 5.1 %collective-permute-done.22.refs_2_ = bf16[288,256]{1,0:T(8,128)(2,1)S(1)} collective-permute-done((bf16[288,256]{1,0:T(8,128)(2,1)S(1)}, bf16[288,256]{1,0:T(8,128)(2,1)S(1)}, u32[]{:S(2)}, u32[]{:S(2)}) %collective-permute-start.22) | collective-permute-done | bytes 147488 | tf_op jit(solution)/shard_map/ppermute | solution.py:382
  91.2 0.1 finish.8
  91.3 0.1 collective-permute-start.24
  91.4 1.9 %collective-permute-done.19.edge_ref = f32[16,2048]{1,0:T(8,128)S(1)} collective-permute-done((f32[16,2048]{1,0:T(8,128)S(1)}, f32[16,2048]{1,0:T(8,128)S(1)}, u32[]{:S(2)}, u32[]{:S(2)}) %collective-permute-start.19) | collective-permute-done | bytes 131104 | tf_op jit(solution)/shard_map/ppermute | solution.py:522
  93.3 2.0 %gram.1 = (f32[384,160]{1,0:T(8,128)S(1)}, f32[2,160,1024]{2,1,0:T(8,128)S(1)}) custom-call(s32[1]{0:T(128)} %bitcast.me_ref, f32[16,2048]{1,0:T(8,128)S(1)} %collective-permute-done.19.edge_ref, s32[8,3072]{1,0:T(8,128)S(1)} %copy-done.4, f32[144,256]{1,0:T(8,128)S(1)} %get-tuple-element.87.refs_3_.refs_0_, ...), custom_call_target="tpu_custom_call" | custom-call | flops 1000 | bytes 1000 | tf_op jit(solution)/shard_map/gram/pallas_call | solution.py:222
  95.3 0.1 finish.9
  95.4 0.1 collective-permute-start.25
  95.5 1.4 %collective-permute-done.25.refs_3_ = f32[160,256]{1,0:T(8,128)S(1)} collective-permute-done((f32[160,256]{1,0:T(8,128)S(1)}, f32[160,256]{1,0:T(8,128)S(1)}, u32[]{:S(2)}, u32[]{:S(2)}) %collective-permute-start.25) | collective-permute-done | bytes 163872 | tf_op jit(solution)/shard_map/ppermute | solution.py:382
  96.9 5.1 %tail.1 = f32[8,2,3072]{2,1,0:T(2,128)} custom-call(s32[1]{0:T(128)} %bitcast.me_ref, f32[2,24]{1,0:T(2,128)S(1)} %copy-done.7, f32[384,160]{1,0:T(8,128)S(1)} %get-tuple-element.95.gram_ref, f32[2,160,1024]{2,1,0:T(8,128)S(1)} %get-tuple-element.96.window_ref, s32[8,3072]{1,0:T(8,128)S(1)} %copy-done.4, f32[160,256]{1,0:T(8,128)S(1)} %get-tuple-element.97.refs_0_, ...), custom_call_target="tpu_custom_call" | custom-call | flops 1000 | bytes 1000 | tf_op jit(solution)/shard_map/tail/pallas_call | solution.py:339
  (29 shorter events, 0.2 us)
Async XLA Ops:
  1.5 3.6 %copy-start = (bf16[256,256]{1,0:T(8,128)(2,1)S(1)}, bf16[256,256]{1,0:T(8,128)(2,1)}, u32[]{:S(2)}) copy-start(bf16[256,256]{1,0:T(8,128)(2,1)} %constant.15.clone.natural_ref) | copy-start | bytes 393220
  1.5 3.6 %copy-start.1 = (bf16[2,128,16]{2,1,0:T(8,128)(2,1)S(1)}, bf16[2,128,16]{2,1,0:T(8,128)(2,1)}, u32[]{:S(2)}) copy-start(bf16[2,128,16]{2,1,0:T(8,128)(2,1)} %constant.16.clone.picks_ref) | copy-start | bytes 24580
  1.5 3.6 %copy-start.3 = (s32[256,2]{1,0:T(8,128)S(1)}, s32[256,2]{1,0:T(8,128)}, u32[]{:S(2)}) copy-start(s32[256,2]{1,0:T(8,128)} %constant.14.clone.order_ref) | copy-start | bytes 6148
  1.5 3.6 %copy-start.6 = (bf16[8,2,128]{2,1,0:T(2,128)(2,1)S(1)}, bf16[8,2,128]{2,1,0:T(2,128)(2,1)}, u32[]{:S(2)}) copy-start(bf16[8,2,128]{2,1,0:T(2,128)(2,1)} %beam_ref.9) | copy-start | bytes 12292
  1.5 3.6 %collective-permute-start = (bf16[8,256,384]{2,1,0:T(8,128)(2,1)S(1)}, bf16[8,256,384]{2,1,0:T(8,128)(2,1)S(1)}, u32[]{:S(2)}, u32[]{:S(2)}) collective-permute-start(bf16[8,256,384]{2,1,0:T(8,128)(2,1)S(1)} %slice.2), channel_id=1, source_target_pairs={{0,1},{1,0},{2,3},{3,2},{4,5},{5,4},{6,7},{7,6},{8,9},{9,8},{10,11... | collective-permute-start | bytes 4718600 | tf_op jit(solution)/shard_map/ppermute | solution.py:382
  3.5 8.7 %collective-permute-start.1 = (bf16[8,256,384]{2,1,0:T(8,128)(2,1)S(1)}, bf16[8,256,384]{2,1,0:T(8,128)(2,1)S(1)}, u32[]{:S(2)}, u32[]{:S(2)}) collective-permute-start(bf16[8,256,384]{2,1,0:T(8,128)(2,1)S(1)} %slice.3), channel_id=1, source_target_pairs={{0,1},{1,0},{2,3},{3,2},{4,5},{5,4},{6,7},{7,6},{8,9},{9,8},{10,11... | collective-permute-start | bytes 4718600 | tf_op jit(solution)/shard_map/ppermute | solution.py:382
  9.1 7.2 %collective-permute-start.2 = (bf16[8,256,256]{2,1,0:T(8,128)(2,1)S(1)}, bf16[8,256,256]{2,1,0:T(8,128)(2,1)S(1)}, u32[]{:S(2)}, u32[]{:S(2)}) collective-permute-start(bf16[8,256,256]{2,1,0:T(8,128)(2,1)S(1)} %get-tuple-element.59), channel_id=1, source_target_pairs={{0,1},{1,0},{2,3},{3,2},{4,5},{5,4},{6,7},{7,6},{8,9},{9,8},{10,11... | collective-permute-start | bytes 3145736 | tf_op jit(solution)/shard_map/ppermute | solution.py:382
  9.5 6.8 %copy-start.5 = (s32[256,2]{1,0:T(8,128)S(1)}, s32[256,2]{1,0:T(8,128)}, u32[]{:S(2)}) copy-start(s32[256,2]{1,0:T(8,128)} %constant.17.clone.order_ref) | copy-start | bytes 6148
  9.5 21.0 %collective-permute-start.3 = (bf16[1024,384]{1,0:T(8,128)(2,1)S(1)}, bf16[1024,384]{1,0:T(8,128)(2,1)S(1)}, u32[]{:S(2)}, u32[]{:S(2)}) collective-permute-start(bf16[1024,384]{1,0:T(8,128)(2,1)S(1)} %get-tuple-element.55), channel_id=1, source_target_pairs={{0,2},{1,3},{2,0},{3,1},{4,6},{5,7},{6,4},{7,5},{8,10},{9,11},{10,... | collective-permute-start | bytes 2359304 | tf_op jit(solution)/shard_map/ppermute | solution.py:382
  16.1 21.1 %collective-permute-start.5 = (bf16[8,256,256]{2,1,0:T(8,128)(2,1)S(1)}, bf16[8,256,256]{2,1,0:T(8,128)(2,1)S(1)}, u32[]{:S(2)}, u32[]{:S(2)}) collective-permute-start(bf16[8,256,256]{2,1,0:T(8,128)(2,1)S(1)} %get-tuple-element.66), channel_id=1, source_target_pairs={{0,1},{1,0},{2,3},{3,2},{4,5},{5,4},{6,7},{7,6},{8,9},{9,8},{10,11... | collective-permute-start | bytes 3145736 | tf_op jit(solution)/shard_map/ppermute | solution.py:382
  19.3 21.5 %collective-permute-start.6 = (bf16[8,256,256]{2,1,0:T(8,128)(2,1)S(1)}, bf16[8,256,256]{2,1,0:T(8,128)(2,1)S(1)}, u32[]{:S(2)}, u32[]{:S(2)}) collective-permute-start(bf16[8,256,256]{2,1,0:T(8,128)(2,1)S(1)} %get-tuple-element.70), channel_id=1, source_target_pairs={{0,1},{1,0},{2,3},{3,2},{4,5},{5,4},{6,7},{7,6},{8,9},{9,8},{10,11... | collective-permute-start | bytes 3145736 | tf_op jit(solution)/shard_map/ppermute | solution.py:382
  19.8 14.8 %collective-permute-start.4 = (bf16[1024,256]{1,0:T(8,128)(2,1)S(1)}, bf16[1024,256]{1,0:T(8,128)(2,1)S(1)}, u32[]{:S(2)}, u32[]{:S(2)}) collective-permute-start(bf16[1024,256]{1,0:T(8,128)(2,1)S(1)} %get-tuple-element.62), channel_id=1, source_target_pairs={{0,4},{1,5},{2,6},{3,7},{4,0},{5,1},{6,2},{7,3},{8,12},{9,13},{10,... | collective-permute-start | bytes 1572872 | tf_op jit(solution)/shard_map/ppermute | solution.py:382
  21.4 26.5 %collective-permute-start.9 = (bf16[1024,384]{1,0:T(8,128)(2,1)S(1)}, bf16[1024,384]{1,0:T(8,128)(2,1)S(1)}, u32[]{:S(2)}, u32[]{:S(2)}) collective-permute-start(bf16[1024,384]{1,0:T(8,128)(2,1)S(1)} %get-tuple-element.57), channel_id=1, source_target_pairs={{0,2},{1,3},{2,0},{3,1},{4,6},{5,7},{6,4},{7,5},{8,10},{9,11},{10,... | collective-permute-start | bytes 2359304 | tf_op jit(solution)/shard_map/ppermute | solution.py:382
  30.6 6.6 %copy-start.2 = (s32[288,2]{1,0:T(8,128)S(1)}, s32[288,2]{1,0:T(8,128)}, u32[]{:S(2)}) copy-start(s32[288,2]{1,0:T(8,128)} %constant.18.clone.order_ref) | copy-start | bytes 6916
  30.7 17.1 %collective-permute-start.7 = (bf16[512,384]{1,0:T(8,128)(2,1)S(1)}, bf16[512,384]{1,0:T(8,128)(2,1)S(1)}, u32[]{:S(2)}, u32[]{:S(2)}) collective-permute-start(bf16[512,384]{1,0:T(8,128)(2,1)S(1)} %share.10), channel_id=1, source_target_pairs={{0,4},{1,5},{2,6},{3,7},{4,0},{5,1},{6,2},{7,3},{8,12},{9,13},{10,... | collective-permute-start | bytes 1179656 | tf_op jit(solution)/shard_map/ppermute | solution.py:382
  34.6 13.2 %collective-permute-start.8 = (bf16[512,256]{1,0:T(8,128)(2,1)S(1)}, bf16[512,256]{1,0:T(8,128)(2,1)S(1)}, u32[]{:S(2)}, u32[]{:S(2)}) collective-permute-start(bf16[512,256]{1,0:T(8,128)(2,1)S(1)} %share.11), channel_id=1, source_target_pairs={{0,8},{1,9},{2,10},{3,11},{4,12},{5,13},{6,14},{7,15},{8,0},{9,1},... | collective-permute-start | bytes 786440 | tf_op jit(solution)/shard_map/ppermute | solution.py:382
  43.5 22.2 %collective-permute-start.11 = (bf16[1152,256]{1,0:T(8,128)(2,1)S(1)}, bf16[1152,256]{1,0:T(8,128)(2,1)S(1)}, u32[]{:S(2)}, u32[]{:S(2)}) collective-permute-start(bf16[1152,256]{1,0:T(8,128)(2,1)S(1)} %get-tuple-element.73), channel_id=1, source_target_pairs={{0,2},{1,3},{2,0},{3,1},{4,6},{5,7},{6,4},{7,5},{8,10},{9,11},{10,... | collective-permute-start | bytes 1769480 | tf_op jit(solution)/shard_map/ppermute | solution.py:382
  43.5 29.2 %collective-permute-start.12 = (bf16[1152,256]{1,0:T(8,128)(2,1)}, bf16[1152,256]{1,0:T(8,128)(2,1)S(1)}, u32[]{:S(2)}, u32[]{:S(2)}) collective-permute-start(bf16[1152,256]{1,0:T(8,128)(2,1)} %get-tuple-element.68), channel_id=1, source_target_pairs={{0,2},{1,3},{2,0},{3,1},{4,6},{5,7},{6,4},{7,5},{8,10},{9,11},{10,... | collective-permute-start | bytes 1769480 | tf_op jit(solution)/shard_map/ppermute | solution.py:382
  48.0 15.1 %collective-permute-start.10 = (bf16[512,384]{1,0:T(8,128)(2,1)S(1)}, bf16[512,384]{1,0:T(8,128)(2,1)S(1)}, u32[]{:S(2)}, u32[]{:S(2)}) collective-permute-start(bf16[512,384]{1,0:T(8,128)(2,1)S(1)} %share.14), channel_id=1, source_target_pairs={{0,4},{1,5},{2,6},{3,7},{4,0},{5,1},{6,2},{7,3},{8,12},{9,13},{10,... | collective-permute-start | bytes 1179656 | tf_op jit(solution)/shard_map/ppermute | solution.py:382
  50.5 24.7 %collective-permute-start.15 = (bf16[256,384]{1,0:T(8,128)(2,1)S(1)}, bf16[256,384]{1,0:T(8,128)(2,1)S(1)}, u32[]{:S(2)}, u32[]{:S(2)}) collective-permute-start(bf16[256,384]{1,0:T(8,128)(2,1)S(1)} %share.12), channel_id=1, source_target_pairs={{0,8},{1,9},{2,10},{3,11},{4,12},{5,13},{6,14},{7,15},{8,0},{9,1},... | collective-permute-start | bytes 589832 | tf_op jit(solution)/shard_map/ppermute | solution.py:382
  63.1 12.4 %collective-permute-start.17 = (bf16[256,384]{1,0:T(8,128)(2,1)S(1)}, bf16[256,384]{1,0:T(8,128)(2,1)S(1)}, u32[]{:S(2)}, u32[]{:S(2)}) collective-permute-start(bf16[256,384]{1,0:T(8,128)(2,1)S(1)} %share.15), channel_id=1, source_target_pairs={{0,8},{1,9},{2,10},{3,11},{4,12},{5,13},{6,14},{7,15},{8,0},{9,1},... | collective-permute-start | bytes 589832 | tf_op jit(solution)/shard_map/ppermute | solution.py:382
  64.1 11.1 %collective-permute-start.13 = (bf16[256,256]{1,0:T(8,128)(2,1)S(1)}, bf16[256,256]{1,0:T(8,128)(2,1)S(1)}, u32[]{:S(2)}, u32[]{:S(2)}) collective-permute-start(bf16[256,256]{1,0:T(8,128)(2,1)S(1)} %share.13), channel_id=1, source_target_pairs={{0,2},{1,3},{2,0},{3,1},{4,6},{5,7},{6,4},{7,5},{8,10},{9,11},{10,... | collective-permute-start | bytes 393224 | tf_op jit(solution)/shard_map/ppermute | solution.py:382
  65.7 13.2 %collective-permute-start.20 = (bf16[576,256]{1,0:T(8,128)(2,1)S(1)}, bf16[576,256]{1,0:T(8,128)(2,1)S(1)}, u32[]{:S(2)}, u32[]{:S(2)}) collective-permute-start(bf16[576,256]{1,0:T(8,128)(2,1)S(1)} %share.16), channel_id=1, source_target_pairs={{0,4},{1,5},{2,6},{3,7},{4,0},{5,1},{6,2},{7,3},{8,12},{9,13},{10,... | collective-permute-start | bytes 884744 | tf_op jit(solution)/shard_map/ppermute | solution.py:382
  72.8 13.1 %collective-permute-start.21 = (bf16[576,256]{1,0:T(8,128)(2,1)S(1)}, bf16[576,256]{1,0:T(8,128)(2,1)S(1)}, u32[]{:S(2)}, u32[]{:S(2)}) collective-permute-start(bf16[576,256]{1,0:T(8,128)(2,1)S(1)} %share.17), channel_id=1, source_target_pairs={{0,4},{1,5},{2,6},{3,7},{4,0},{5,1},{6,2},{7,3},{8,12},{9,13},{10,... | collective-permute-start | bytes 884744 | tf_op jit(solution)/shard_map/ppermute | solution.py:382
  75.5 10.5 %collective-permute-start.16 = (f32[144,384]{1,0:T(8,128)S(1)}, f32[144,384]{1,0:T(8,128)S(1)}, u32[]{:S(2)}, u32[]{:S(2)}) collective-permute-start(f32[144,384]{1,0:T(8,128)S(1)} %get-tuple-element.84), channel_id=1, source_target_pairs={{0,1},{1,0},{2,3},{3,2},{4,5},{5,4},{6,7},{7,6},{8,9},{9,8},{10,11... | collective-permute-start | bytes 663560 | tf_op jit(solution)/shard_map/ppermute | solution.py:382
  75.7 10.3 %collective-permute-start.18 = (f32[144,384]{1,0:T(8,128)S(1)}, f32[144,384]{1,0:T(8,128)S(1)}, u32[]{:S(2)}, u32[]{:S(2)}) collective-permute-start(f32[144,384]{1,0:T(8,128)S(1)} %get-tuple-element.86), channel_id=1, source_target_pairs={{0,1},{1,0},{2,3},{3,2},{4,5},{5,4},{6,7},{7,6},{8,9},{9,8},{10,11... | collective-permute-start | bytes 663560 | tf_op jit(solution)/shard_map/ppermute | solution.py:382
  76.3 9.7 %collective-permute-start.14 = (f32[144,256]{1,0:T(8,128)S(1)}, f32[144,256]{1,0:T(8,128)S(1)}, u32[]{:S(2)}, u32[]{:S(2)}) collective-permute-start(f32[144,256]{1,0:T(8,128)S(1)} %get-tuple-element.82), channel_id=1, source_target_pairs={{0,1},{1,0},{2,3},{3,2},{4,5},{5,4},{6,7},{7,6},{8,9},{9,8},{10,11... | collective-permute-start | bytes 442376 | tf_op jit(solution)/shard_map/ppermute | solution.py:382
  78.9 12.3 %collective-permute-start.22 = (bf16[288,256]{1,0:T(8,128)(2,1)S(1)}, bf16[288,256]{1,0:T(8,128)(2,1)S(1)}, u32[]{:S(2)}, u32[]{:S(2)}) collective-permute-start(bf16[288,256]{1,0:T(8,128)(2,1)S(1)} %share.18), channel_id=1, source_target_pairs={{0,8},{1,9},{2,10},{3,11},{4,12},{5,13},{6,14},{7,15},{8,0},{9,1},... | collective-permute-start | bytes 442376 | tf_op jit(solution)/shard_map/ppermute | solution.py:382
  85.9 9.4 %collective-permute-start.23 = (bf16[288,256]{1,0:T(8,128)(2,1)S(1)}, bf16[288,256]{1,0:T(8,128)(2,1)S(1)}, u32[]{:S(2)}, u32[]{:S(2)}) collective-permute-start(bf16[288,256]{1,0:T(8,128)(2,1)S(1)} %share.19), channel_id=1, source_target_pairs={{0,8},{1,9},{2,10},{3,11},{4,12},{5,13},{6,14},{7,15},{8,0},{9,1},... | collective-permute-start | bytes 442376 | tf_op jit(solution)/shard_map/ppermute | solution.py:382
  86.0 7.3 %copy-start.4 = (s32[8,3072]{1,0:T(8,128)S(1)}, s32[8,3072]{1,0:T(8,128)}, u32[]{:S(2)}) copy-start(s32[8,3072]{1,0:T(8,128)} %mask_ref.2) | copy-start | bytes 294916
  86.0 7.3 %collective-permute-start.19 = (f32[16,2048]{1,0:T(8,128)S(1)}, f32[16,2048]{1,0:T(8,128)S(1)}, u32[]{:S(2)}, u32[]{:S(2)}) collective-permute-start(f32[16,2048]{1,0:T(8,128)S(1)} %edges.1), channel_id=1, source_target_pairs={{2,1},{4,3},{6,5},{8,7},{10,9},{12,11},{14,13},{0,15},{1,2},{3,4},... | collective-permute-start | bytes 393224 | tf_op jit(solution)/shard_map/ppermute | solution.py:522
  91.3 5.6 %copy-start.7 = (f32[2,24]{1,0:T(2,128)S(1)}, f32[2,24]{1,0:T(2,128)}, u32[]{:S(2)}) copy-start(f32[2,24]{1,0:T(2,128)} %steer_ref.1) | copy-start | bytes 580
  91.3 4.2 %collective-permute-start.24 = (f32[160,256]{1,0:T(8,128)S(1)}, f32[160,256]{1,0:T(8,128)S(1)}, u32[]{:S(2)}, u32[]{:S(2)}) collective-permute-start(f32[160,256]{1,0:T(8,128)S(1)} %get-tuple-element.93), channel_id=1, source_target_pairs={{0,1},{1,0},{2,3},{3,2},{4,5},{5,4},{6,7},{7,6},{8,9},{9,8},{10,11... | collective-permute-start | bytes 491528 | tf_op jit(solution)/shard_map/ppermute | solution.py:382
  95.4 1.5 %collective-permute-start.25 = (f32[160,256]{1,0:T(8,128)S(1)}, f32[160,256]{1,0:T(8,128)S(1)}, u32[]{:S(2)}, u32[]{:S(2)}) collective-permute-start(f32[160,256]{1,0:T(8,128)S(1)} %get-tuple-element.100), channel_id=1, source_target_pairs={{0,1},{1,0},{2,3},{3,2},{4,5},{5,4},{6,7},{7,6},{8,9},{9,8},{10,11... | collective-permute-start | bytes 491528 | tf_op jit(solution)/shard_map/ppermute | solution.py:382

commit v5 on v4

--- a/solution.py
+++ b/solution.py
@@ -15,12 +15,12 @@
 BF16 = jnp.bfloat16
 GROUP = 8
 VMEM = 48 << 20
-CHUNKS = ((2, 1, 0, 0), (3, 0, 0, 0), (3, 0, 0, 0), (2, 0, 1, 0), (2, 0, 1, 0))
+CHUNKS = ((3, 0, 0, 0), (3, 0, 0, 0), (2, 1, 0, 0), (2, 0, 1, 0), (2, 0, 1, 1))
 AHEAD = 2
 STEPS = (
-    (1, 0), (2, 0), (1, 1), (2, 1), (0, 1), (1, 2), (0, 2), (4, 1), (3, 1), (1, 3),
-    (0, 3), (2, 2), (2, 11), (2, 3), (3, 2), (4, 2), (0, 4), (1, 4), (2, 4), (3, 3),
-    (4, 3), (3, 4), ("halo", 0), ("gram", 0), (4, 4),
+    (1, 0), (3, 0), (0, 0), (1, 1), (0, 1), (2, 1), (1, 2), (2, 2), (3, 1), (4, 1),
+    (2, 3), (1, 3), (0, 2), (3, 2), (0, 11), (0, 3), (1, 4), (4, 2), (2, 4), (0, 4),
+    (3, 3), ("halo", 0), (4, 3), (3, 4), ("gram", 0), (4, 4),
 )
 
 
@@ -104,22 +104,28 @@
     weights_ref[...] = jnp.where(same, total, 0.0).astype(BF16)
 
     table = table_ref[...]
-    for e in range(2 * elem_dev):
-        spectra = dot(table, mine_ref[e] if e < elem_dev else theirs_ref[e - elem_dev])
-        spectra_ref[:, e] = spectra.astype(BF16).reshape(groups, 2 * GROUP, width)
+    echoes = [mine_ref[e] for e in range(elem_dev)] + [theirs_ref[e] for e in range(elem_dev)]
+    for e in range(0, 2 * elem_dev, 2):
+        spectra = dot(table, jnp.concatenate(echoes[e : e + 2], axis=1)).astype(BF16)
+        for i in range(2):
+            part = spectra[:, i * width : (i + 1) * width]
+            spectra_ref[:, e + i] = part.reshape(groups, 2 * GROUP, width)
     weights = weights_ref[...]
     rows = weights.shape[0]
     tall = sends[0].shape[0]
-    for g in range(groups):
-        sums = dot(weights, spectra_ref[g].reshape(-1, width))
-        if g < groups // 2:
-            keep_ref[g * rows : (g + 1) * rows] = sums
-            continue
-        sums = sums.astype(BF16)
-        for low in range(0, rows, 16):
-            at = (g - groups // 2) * rows + low
-            out_ref = sends[parts - 1 - at // tall]
-            out_ref[at % tall : at % tall + 16] = sums[low : low + 16]
+    for pair in range(0, groups, 2):
+        spectra = [spectra_ref[g].reshape(-1, width) for g in (pair, pair + 1)]
+        both = dot(weights, jnp.concatenate(spectra, axis=1))
+        for g in (pair, pair + 1):
+            sums = both[:, (g - pair) * width : (g - pair + 1) * width]
+            if g < groups // 2:
+                keep_ref[g * rows : (g + 1) * rows] = sums
+                continue
+            sums = sums.astype(BF16)
+            for low in range(0, rows, 16):
+                at = (g - groups // 2) * rows + low
+                out_ref = sends[parts - 1 - at // tall]
+                out_ref[at % tall : at % tall + 16] = sums[low : low + 16]
 
 
 def front(me, strides, extra, bins_chip, beam_weights, echo, theirs, span, ahead, parts):

time: 104 us -> 102 us (0.981); the launches traced: 102 us -> 101 us
    ppermute x25 -> x27, waiting for transfers between devices: 45.3 us -> 40.4 us  [swap(): return lax.ppermute(x, 'elem', [(i, i ^ stride) for i in range(count)])]
    ppermute x1, waiting for transfers between devices: 1.9 us -> 6.17 us  [local(): edge = lax.ppermute(out, 'elem', pairs)]
    pallas_call x2 -> x3, Pallas kernels: 2.94 us -> 4.31 us  [other_half(): pl.pallas_call(slice_kernel, grid_spec=pltpu.PrefetchScalarGridSpec(num_s...]
    pallas_call x5, Pallas kernels: 17.1 us -> 16 us  [front(): pl.pallas_call(functools.partial(front_kernel, bins_chip, ahead is not No...]
    ppermute x25 -> x27, starting transfers between devices: 26 us -> 25.6 us  [swap(): return lax.ppermute(x, 'elem', [(i, i ^ stride) for i in range(count)])]
  transfers between devices with their start and end apart: 26 -> 28, of which waited for: 12 -> 12; matrix products, arithmetic and copies ran while one was open for 0% -> 0% of each run, Pallas kernels for 21% -> 22%
where the time goes in v5:
time: 102 us; the launch traced here: 101 us
  waiting for transfers between devices  46.5 us (46%)
  Pallas kernels  28.7 us (28%)
  starting transfers between devices  25.7 us (25%)
    ppermute x27, waiting for transfers between devices, swap(): return lax.ppermute(x, 'elem', [(i, i ^ stride) for i in range(count)])  40.4 us
    ppermute x27, starting transfers between devices, swap(): return lax.ppermute(x, 'elem', [(i, i ^ stride) for i in range(count)])  25.6 us
    pallas_call x5, Pallas kernels, front(): pl.pallas_call(functools.partial(front_kernel, bins_chip, ahead is not No...  16 us
    ppermute x1, waiting for transfers between devices, local(): edge = lax.ppermute(out, 'elem', pairs)  6.17 us
    pallas_call x1, Pallas kernels, tail(): pl.pallas_call(tail_kernel, in_specs=[pl.BlockSpec(memory_space=pltpu.SME...  5.24 us
    pallas_call x3, Pallas kernels, other_half(): pl.pallas_call(slice_kernel, grid_spec=pltpu.PrefetchScalarGridSpec(num_s...  4.31 us
  transfers between devices with their start and end apart: 28, of which 12 were waited for; matrix products, arithmetic and copies ran while one was open for 0% of the time, Pallas kernels for 22%

profile of v5, /device:TPU:0, one launch (start us, length us, event | category | flops | bytes accessed | tf_op | source)
XLA Modules:
  0.0 101.3 jit_solution(15099979962648888540)
XLA Ops:
  0.0 1.5 %slice.3 = bf16[8,256,384]{2,1,0:T(8,128)(2,1)S(1)} custom-call(s32[1]{0:T(128)} %bitcast.me_ref, bf16[8,256,3072]{2,1,0:T(8,128)(2,1)} %bitcast.2), custom_call_target="tpu_custom_call" | custom-call | flops 1000 | bytes 1000 | tf_op jit(solution)/shard_map/slice/pallas_call | solution.py:367
  1.5 0.5 collective-permute-start
  2.0 1.3 %slice.4 = bf16[8,256,256]{2,1,0:T(8,128)(2,1)S(1)} custom-call(s32[1]{0:T(128)} %bitcast.me_ref, bf16[8,256,3072]{2,1,0:T(8,128)(2,1)} %bitcast.3), custom_call_target="tpu_custom_call" | custom-call | flops 1000 | bytes 1000 | tf_op jit(solution)/shard_map/slice/pallas_call | solution.py:367
  3.3 0.0 copy-start
  3.3 0.0 copy-start.1
  3.3 1.6 %slice.5 = bf16[8,256,384]{2,1,0:T(8,128)(2,1)S(1)} custom-call(s32[1]{0:T(128)} %bitcast.me_ref, bf16[8,256,3072]{2,1,0:T(8,128)(2,1)} %bitcast.4), custom_call_target="tpu_custom_call" | custom-call | flops 1000 | bytes 1000 | tf_op jit(solution)/shard_map/slice/pallas_call | solution.py:367
  4.9 0.1 collective-permute-start.1
  5.1 3.6 %front.5 = (bf16[1024,384]{1,0:T(8,128)(2,1)S(1)}, f32[1024,384]{1,0:T(8,128)S(1)}, bf16[8,256,256]{2,1,0:T(8,128)(2,1)S(1)}) custom-call(s32[1]{0:T(128)} %bitcast.me_ref, s32[256,2]{1,0:T(8,128)S(1)} %copy-done.3, bf16[256,256]{1,0:T(8,128)(2,1)S(1)} %copy-done, bf16[2,128,16]{2,1,0:T(8,128)(2,1)S(1)} %copy-done.1, bf16[8,2,128]{2,1,0:T(2,128)(2,1)S(1)} %copy-done.6, ...), custom_call_target="tpu_custom_call" | custom-call | flops 1000 | bytes 1000 | tf_op jit(solution)/shard_map/front/pallas_call | solution.py:160
  8.6 0.5 collective-permute-start.2
  9.2 0.1 collective-permute-start.5
  9.2 3.0 %collective-permute-start.3 = (bf16[1024,384]{1,0:T(8,128)(2,1)S(1)}, bf16[1024,384]{1,0:T(8,128)(2,1)S(1)}, u32[]{:S(2)}, u32[]{:S(2)}) collective-permute-start(bf16[1024,384]{1,0:T(8,128)(2,1)S(1)} %get-tuple-element.59), channel_id=1, source_target_pairs={{0,2},{1,3},{2,0},{3,1},{4,6},{5,7},{6,4},{7,5},{8,10},{9,11},{10,... | collective-permute-start | bytes 2359304 | tf_op jit(solution)/shard_map/ppermute | solution.py:388
  12.2 4.1 %front.6 = (bf16[1024,384]{1,0:T(8,128)(2,1)}, f32[1024,384]{1,0:T(8,128)S(1)}) custom-call(s32[1]{0:T(128)} %bitcast.me_ref, s32[256,2]{1,0:T(8,128)S(1)} %copy-done.3, bf16[256,256]{1,0:T(8,128)(2,1)S(1)} %copy-done, bf16[2,128,16]{2,1,0:T(8,128)(2,1)S(1)} %copy-done.1, bf16[8,2,128]{2,1,0:T(2,128)(2,1)S(1)} %copy-done.6, bf16[8,256,3072]{2,1,0:T(8,128)(2,1)} %bitcast.7, ...), custom_call_target="tpu_custom_call" | custom-call | flops 1000 | bytes 1000 | tf_op jit(solution)/shard_map/front/pallas_call | solution.py:160
  16.3 3.0 %front.7 = (bf16[1024,256]{1,0:T(8,128)(2,1)S(1)}, f32[1024,256]{1,0:T(8,128)S(1)}, bf16[8,256,256]{2,1,0:T(8,128)(2,1)S(1)}) custom-call(s32[1]{0:T(128)} %bitcast.me_ref, s32[256,2]{1,0:T(8,128)S(1)} %copy-done.5, bf16[256,256]{1,0:T(8,128)(2,1)S(1)} %copy-done, bf16[2,128,16]{2,1,0:T(8,128)(2,1)S(1)} %copy-done.1, bf16[8,2,128]{2,1,0:T(2,128)(2,1)S(1)} %copy-done.6, ...), custom_call_target="tpu_custom_call" | custom-call | flops 1000 | bytes 1000 | tf_op jit(solution)/shard_map/front/pallas_call | solution.py:160
  19.3 0.1 collective-permute-start.6
  19.4 1.6 %collective-permute-start.4 = (bf16[1024,256]{1,0:T(8,128)(2,1)S(1)}, bf16[1024,256]{1,0:T(8,128)(2,1)S(1)}, u32[]{:S(2)}, u32[]{:S(2)}) collective-permute-start(bf16[1024,256]{1,0:T(8,128)(2,1)S(1)} %get-tuple-element.67), channel_id=1, source_target_pairs={{0,4},{1,5},{2,6},{3,7},{4,0},{5,1},{6,2},{7,3},{8,12},{9,13},{10,... | collective-permute-start | bytes 1572872 | tf_op jit(solution)/shard_map/ppermute | solution.py:388
  21.0 0.5 collective-permute-start.9
  21.5 9.0 %collective-permute-done.3.refs_0_ = bf16[1024,384]{1,0:T(8,128)(2,1)S(1)} collective-permute-done((bf16[1024,384]{1,0:T(8,128)(2,1)S(1)}, bf16[1024,384]{1,0:T(8,128)(2,1)S(1)}, u32[]{:S(2)}, u32[]{:S(2)}) %collective-permute-start.3) | collective-permute-done | bytes 786464 | tf_op jit(solution)/shard_map/ppermute | solution.py:388
  30.5 0.1 share.10
  30.6 2.2 %collective-permute-start.8 = (bf16[512,384]{1,0:T(8,128)(2,1)S(1)}, bf16[512,384]{1,0:T(8,128)(2,1)S(1)}, u32[]{:S(2)}, u32[]{:S(2)}) collective-permute-start(bf16[512,384]{1,0:T(8,128)(2,1)S(1)} %share.10), channel_id=1, source_target_pairs={{0,4},{1,5},{2,6},{3,7},{4,0},{5,1},{6,2},{7,3},{8,12},{9,13},{10,... | collective-permute-start | bytes 1179656 | tf_op jit(solution)/shard_map/ppermute | solution.py:388
  32.8 1.4 %collective-permute-done.4.refs_0_ = bf16[1024,256]{1,0:T(8,128)(2,1)S(1)} collective-permute-done((bf16[1024,256]{1,0:T(8,128)(2,1)S(1)}, bf16[1024,256]{1,0:T(8,128)(2,1)S(1)}, u32[]{:S(2)}, u32[]{:S(2)}) %collective-permute-start.4) | collective-permute-done | bytes 524320 | tf_op jit(solution)/shard_map/ppermute | solution.py:388
  34.2 2.6 %collective-permute-start.7 = (bf16[512,256]{1,0:T(8,128)(2,1)S(1)}, bf16[512,256]{1,0:T(8,128)(2,1)S(1)}, u32[]{:S(2)}, u32[]{:S(2)}) collective-permute-start(bf16[512,256]{1,0:T(8,128)(2,1)S(1)} %share.11), channel_id=1, source_target_pairs={{0,8},{1,9},{2,10},{3,11},{4,12},{5,13},{6,14},{7,15},{8,0},{9,1},... | collective-permute-start | bytes 786440 | tf_op jit(solution)/shard_map/ppermute | solution.py:388
  36.9 2.7 %front.8 = (bf16[1152,256]{1,0:T(8,128)(2,1)S(1)}, f32[1152,256]{1,0:T(8,128)S(1)}) custom-call(s32[1]{0:T(128)} %bitcast.me_ref, s32[288,2]{1,0:T(8,128)S(1)} %copy-done.2, bf16[256,256]{1,0:T(8,128)(2,1)S(1)} %copy-done, bf16[2,128,16]{2,1,0:T(8,128)(2,1)S(1)} %copy-done.1, bf16[8,2,128]{2,1,0:T(2,128)(2,1)S(1)} %copy-done.6, ...), custom_call_target="tpu_custom_call" | custom-call | flops 1000 | bytes 1000 | tf_op jit(solution)/shard_map/front/pallas_call | solution.py:160
  39.5 0.6 collective-permute-start.11
  40.1 2.7 %front.9 = (bf16[576,256]{1,0:T(8,128)(2,1)S(1)}, bf16[576,256]{1,0:T(8,128)(2,1)S(1)}, f32[1152,256]{1,0:T(8,128)S(1)}) custom-call(s32[1]{0:T(128)} %bitcast.me_ref, s32[288,2]{1,0:T(8,128)S(1)} %copy-done.2, bf16[256,256]{1,0:T(8,128)(2,1)S(1)} %copy-done, bf16[2,128,16]{2,1,0:T(8,128)(2,1)S(1)} %copy-done.1, bf16[8,2,128]{2,1,0:T(2,128)(2,1)S(1)} %copy-done.6, ...), custom_call_target="tpu_custom_call" | custom-call | flops 1000 | bytes 1000 | tf_op jit(solution)/shard_map/front/pallas_call | solution.py:160
  42.8 4.1 %collective-permute-done.7.refs_1_ = bf16[512,256]{1,0:T(8,128)(2,1)S(1)} collective-permute-done((bf16[512,256]{1,0:T(8,128)(2,1)S(1)}, bf16[512,256]{1,0:T(8,128)(2,1)S(1)}, u32[]{:S(2)}, u32[]{:S(2)}) %collective-permute-start.7) | collective-permute-done | bytes 262176 | tf_op jit(solution)/shard_map/ppermute | solution.py:388
  46.9 0.8 collective-permute-done.8.refs_1_
  47.8 0.1 share.13
  47.8 0.1 share.14
  47.9 2.7 %collective-permute-start.10 = (bf16[512,384]{1,0:T(8,128)(2,1)S(1)}, bf16[512,384]{1,0:T(8,128)(2,1)S(1)}, u32[]{:S(2)}, u32[]{:S(2)}) collective-permute-start(bf16[512,384]{1,0:T(8,128)(2,1)S(1)} %share.14), channel_id=1, source_target_pairs={{0,4},{1,5},{2,6},{3,7},{4,0},{5,1},{6,2},{7,3},{8,12},{9,13},{10,... | collective-permute-start | bytes 1179656 | tf_op jit(solution)/shard_map/ppermute | solution.py:388
  50.6 0.5 collective-permute-start.13
  51.2 2.6 %collective-permute-start.12 = (bf16[256,384]{1,0:T(8,128)(2,1)S(1)}, bf16[256,384]{1,0:T(8,128)(2,1)S(1)}, u32[]{:S(2)}, u32[]{:S(2)}) collective-permute-start(bf16[256,384]{1,0:T(8,128)(2,1)S(1)} %share.13), channel_id=1, source_target_pairs={{0,8},{1,9},{2,10},{3,11},{4,12},{5,13},{6,14},{7,15},{8,0},{9,1},... | collective-permute-start | bytes 589832 | tf_op jit(solution)/shard_map/ppermute | solution.py:388
  53.7 6.3 %collective-permute-done.11.refs_0_ = bf16[1152,256]{1,0:T(8,128)(2,1)S(1)} collective-permute-done((bf16[1152,256]{1,0:T(8,128)(2,1)S(1)}, bf16[1152,256]{1,0:T(8,128)(2,1)S(1)}, u32[]{:S(2)}, u32[]{:S(2)}) %collective-permute-start.11) | collective-permute-done | bytes 589856 | tf_op jit(solution)/shard_map/ppermute | solution.py:388
  60.0 0.1 share.15
  60.1 2.2 %collective-permute-start.20 = (bf16[576,256]{1,0:T(8,128)(2,1)S(1)}, bf16[576,256]{1,0:T(8,128)(2,1)S(1)}, u32[]{:S(2)}, u32[]{:S(2)}) collective-permute-start(bf16[576,256]{1,0:T(8,128)(2,1)S(1)} %share.15), channel_id=1, source_target_pairs={{0,4},{1,5},{2,6},{3,7},{4,0},{5,1},{6,2},{7,3},{8,12},{9,13},{10,... | collective-permute-start | bytes 884744 | tf_op jit(solution)/shard_map/ppermute | solution.py:388
  62.3 2.1 %collective-permute-done.10.refs_1_ = bf16[512,384]{1,0:T(8,128)(2,1)S(1)} collective-permute-done((bf16[512,384]{1,0:T(8,128)(2,1)S(1)}, bf16[512,384]{1,0:T(8,128)(2,1)S(1)}, u32[]{:S(2)}, u32[]{:S(2)}) %collective-permute-start.10) | collective-permute-done | bytes 393248 | tf_op jit(solution)/shard_map/ppermute | solution.py:388
  64.3 0.1 share.16
  64.4 0.6 collective-permute-start.15
  65.0 1.5 %collective-permute-start.14 = (bf16[256,256]{1,0:T(8,128)(2,1)S(1)}, bf16[256,256]{1,0:T(8,128)(2,1)S(1)}, u32[]{:S(2)}, u32[]{:S(2)}) collective-permute-start(bf16[256,256]{1,0:T(8,128)(2,1)S(1)} %share.12), channel_id=1, source_target_pairs={{0,2},{1,3},{2,0},{3,1},{4,6},{5,7},{6,4},{7,5},{8,10},{9,11},{10,... | collective-permute-start | bytes 393224 | tf_op jit(solution)/shard_map/ppermute | solution.py:388
  66.5 0.5 collective-permute-start.21
  67.0 0.2 finish.5
  67.2 0.1 collective-permute-start.17
  67.3 0.1 share.17
  67.3 4.1 %collective-permute-done.14.refs_2_ = bf16[256,256]{1,0:T(8,128)(2,1)S(1)} collective-permute-done((bf16[256,256]{1,0:T(8,128)(2,1)S(1)}, bf16[256,256]{1,0:T(8,128)(2,1)S(1)}, u32[]{:S(2)}, u32[]{:S(2)}) %collective-permute-start.14) | collective-permute-done | bytes 131104 | tf_op jit(solution)/shard_map/ppermute | solution.py:388
  71.4 0.1 finish.6
  71.5 3.4 %collective-permute-done.15.refs_2_ = bf16[256,384]{1,0:T(8,128)(2,1)S(1)} collective-permute-done((bf16[256,384]{1,0:T(8,128)(2,1)S(1)}, bf16[256,384]{1,0:T(8,128)(2,1)S(1)}, u32[]{:S(2)}, u32[]{:S(2)}) %collective-permute-start.15) | collective-permute-done | bytes 196640 | tf_op jit(solution)/shard_map/ppermute | solution.py:388
  75.0 0.2 finish.7
  75.1 0.1 collective-permute-start.16
  75.2 0.5 collective-permute-start.22
  75.7 0.2 collective-permute-start.18
  75.9 0.1 share.18
  75.9 1.8 %collective-permute-start.23 = (bf16[288,256]{1,0:T(8,128)(2,1)S(1)}, bf16[288,256]{1,0:T(8,128)(2,1)S(1)}, u32[]{:S(2)}, u32[]{:S(2)}) collective-permute-start(bf16[288,256]{1,0:T(8,128)(2,1)S(1)} %share.18), channel_id=1, source_target_pairs={{0,8},{1,9},{2,10},{3,11},{4,12},{5,13},{6,14},{7,15},{8,0},{9,1},... | collective-permute-start | bytes 442376 | tf_op jit(solution)/shard_map/ppermute | solution.py:388
  77.7 6.2 %collective-permute-done.22.refs_1_ = bf16[288,256]{1,0:T(8,128)(2,1)S(1)} collective-permute-done((bf16[288,256]{1,0:T(8,128)(2,1)S(1)}, bf16[288,256]{1,0:T(8,128)(2,1)S(1)}, u32[]{:S(2)}, u32[]{:S(2)}) %collective-permute-start.22) | collective-permute-done | bytes 147488 | tf_op jit(solution)/shard_map/ppermute | solution.py:388
  83.9 0.1 share.19
  84.0 0.5 collective-permute-start.25
  84.5 0.1 collective-permute-start.19
  84.6 1.7 %collective-permute-done.23.refs_2_ = bf16[288,256]{1,0:T(8,128)(2,1)S(1)} collective-permute-done((bf16[288,256]{1,0:T(8,128)(2,1)S(1)}, bf16[288,256]{1,0:T(8,128)(2,1)S(1)}, u32[]{:S(2)}, u32[]{:S(2)}) %collective-permute-start.23) | collective-permute-done | bytes 147488 | tf_op jit(solution)/shard_map/ppermute | solution.py:388
  86.2 0.1 finish.8
  86.3 0.1 collective-permute-start.26
  86.4 6.2 %collective-permute-done.19.edge_ref = f32[16,2048]{1,0:T(8,128)S(1)} collective-permute-done((f32[16,2048]{1,0:T(8,128)S(1)}, f32[16,2048]{1,0:T(8,128)S(1)}, u32[]{:S(2)}, u32[]{:S(2)}) %collective-permute-start.19) | collective-permute-done | bytes 131104 | tf_op jit(solution)/shard_map/ppermute | solution.py:528
  92.6 1.8 %gram.1 = (f32[384,160]{1,0:T(8,128)S(1)}, f32[2,160,1024]{2,1,0:T(8,128)S(1)}) custom-call(s32[1]{0:T(128)} %bitcast.me_ref, f32[16,2048]{1,0:T(8,128)S(1)} %collective-permute-done.19.edge_ref, s32[8,3072]{1,0:T(8,128)S(1)} %copy-done.4, f32[144,384]{1,0:T(8,128)S(1)} %get-tuple-element.91.refs_3_.refs_0_, ...), custom_call_target="tpu_custom_call" | custom-call | flops 1000 | bytes 1000 | tf_op jit(solution)/shard_map/gram/pallas_call | solution.py:228
  94.4 0.1 finish.9
  94.5 0.1 collective-permute-start.27
  94.6 1.4 %collective-permute-done.27.refs_3_ = f32[160,256]{1,0:T(8,128)S(1)} collective-permute-done((f32[160,256]{1,0:T(8,128)S(1)}, f32[160,256]{1,0:T(8,128)S(1)}, u32[]{:S(2)}, u32[]{:S(2)}) %collective-permute-start.27) | collective-permute-done | bytes 163872 | tf_op jit(solution)/shard_map/ppermute | solution.py:388
  96.0 5.2 %tail.1 = f32[8,2,3072]{2,1,0:T(2,128)} custom-call(s32[1]{0:T(128)} %bitcast.me_ref, f32[2,24]{1,0:T(2,128)S(1)} %copy-done.7, f32[384,160]{1,0:T(8,128)S(1)} %get-tuple-element.100.gram_ref, f32[2,160,1024]{2,1,0:T(8,128)S(1)} %get-tuple-element.101.window_ref, s32[8,3072]{1,0:T(8,128)S(1)} %copy-done.4, f32[160,256]{1,0:T(8,128)S(1)} %get-tuple-element.102.refs_0_, ...), custom_call_target="tpu_custom_call" | custom-call | flops 1000 | bytes 1000 | tf_op jit(solution)/shard_map/tail/pallas_call | solution.py:345
  (34 shorter events, 0.2 us)
Async XLA Ops:
  1.5 3.6 %collective-permute-start = (bf16[8,256,384]{2,1,0:T(8,128)(2,1)S(1)}, bf16[8,256,384]{2,1,0:T(8,128)(2,1)S(1)}, u32[]{:S(2)}, u32[]{:S(2)}) collective-permute-start(bf16[8,256,384]{2,1,0:T(8,128)(2,1)S(1)} %slice.3), channel_id=1, source_target_pairs={{0,1},{1,0},{2,3},{3,2},{4,5},{5,4},{6,7},{7,6},{8,9},{9,8},{10,11... | collective-permute-start | bytes 4718600 | tf_op jit(solution)/shard_map/ppermute | solution.py:388
  3.3 1.8 %copy-start = (bf16[256,256]{1,0:T(8,128)(2,1)S(1)}, bf16[256,256]{1,0:T(8,128)(2,1)}, u32[]{:S(2)}) copy-start(bf16[256,256]{1,0:T(8,128)(2,1)} %constant.15.clone.natural_ref) | copy-start | bytes 393220
  3.3 1.8 %copy-start.1 = (bf16[2,128,16]{2,1,0:T(8,128)(2,1)S(1)}, bf16[2,128,16]{2,1,0:T(8,128)(2,1)}, u32[]{:S(2)}) copy-start(bf16[2,128,16]{2,1,0:T(8,128)(2,1)} %constant.16.clone.picks_ref) | copy-start | bytes 24580
  3.3 1.7 %copy-start.3 = (s32[256,2]{1,0:T(8,128)S(1)}, s32[256,2]{1,0:T(8,128)}, u32[]{:S(2)}) copy-start(s32[256,2]{1,0:T(8,128)} %constant.14.clone.order_ref) | copy-start | bytes 6148
  3.3 1.7 %copy-start.6 = (bf16[8,2,128]{2,1,0:T(2,128)(2,1)S(1)}, bf16[8,2,128]{2,1,0:T(2,128)(2,1)}, u32[]{:S(2)}) copy-start(bf16[8,2,128]{2,1,0:T(2,128)(2,1)} %beam_ref.9) | copy-start | bytes 12292
  4.9 7.3 %collective-permute-start.1 = (bf16[8,256,384]{2,1,0:T(8,128)(2,1)S(1)}, bf16[8,256,384]{2,1,0:T(8,128)(2,1)S(1)}, u32[]{:S(2)}, u32[]{:S(2)}) collective-permute-start(bf16[8,256,384]{2,1,0:T(8,128)(2,1)S(1)} %slice.5), channel_id=1, source_target_pairs={{0,1},{1,0},{2,3},{3,2},{4,5},{5,4},{6,7},{7,6},{8,9},{9,8},{10,11... | collective-permute-start | bytes 4718600 | tf_op jit(solution)/shard_map/ppermute | solution.py:388
  8.6 7.6 %collective-permute-start.2 = (bf16[8,256,256]{2,1,0:T(8,128)(2,1)S(1)}, bf16[8,256,256]{2,1,0:T(8,128)(2,1)S(1)}, u32[]{:S(2)}, u32[]{:S(2)}) collective-permute-start(bf16[8,256,256]{2,1,0:T(8,128)(2,1)S(1)} %get-tuple-element.64), channel_id=1, source_target_pairs={{0,1},{1,0},{2,3},{3,2},{4,5},{5,4},{6,7},{7,6},{8,9},{9,8},{10,11... | collective-permute-start | bytes 3145736 | tf_op jit(solution)/shard_map/ppermute | solution.py:388
  9.2 27.7 %collective-permute-start.5 = (bf16[8,256,256]{2,1,0:T(8,128)(2,1)S(1)}, bf16[8,256,256]{2,1,0:T(8,128)(2,1)S(1)}, u32[]{:S(2)}, u32[]{:S(2)}) collective-permute-start(bf16[8,256,256]{2,1,0:T(8,128)(2,1)S(1)} %slice.4), channel_id=1, source_target_pairs={{0,1},{1,0},{2,3},{3,2},{4,5},{5,4},{6,7},{7,6},{8,9},{9,8},{10,11... | collective-permute-start | bytes 3145736 | tf_op jit(solution)/shard_map/ppermute | solution.py:388
  9.2 7.1 %copy-start.5 = (s32[256,2]{1,0:T(8,128)S(1)}, s32[256,2]{1,0:T(8,128)}, u32[]{:S(2)}) copy-start(s32[256,2]{1,0:T(8,128)} %constant.17.clone.order_ref) | copy-start | bytes 6148
  9.2 21.3 %collective-permute-start.3 = (bf16[1024,384]{1,0:T(8,128)(2,1)S(1)}, bf16[1024,384]{1,0:T(8,128)(2,1)S(1)}, u32[]{:S(2)}, u32[]{:S(2)}) collective-permute-start(bf16[1024,384]{1,0:T(8,128)(2,1)S(1)} %get-tuple-element.59), channel_id=1, source_target_pairs={{0,2},{1,3},{2,0},{3,1},{4,6},{5,7},{6,4},{7,5},{8,10},{9,11},{10,... | collective-permute-start | bytes 2359304 | tf_op jit(solution)/shard_map/ppermute | solution.py:388
  19.3 20.8 %collective-permute-start.6 = (bf16[8,256,256]{2,1,0:T(8,128)(2,1)S(1)}, bf16[8,256,256]{2,1,0:T(8,128)(2,1)S(1)}, u32[]{:S(2)}, u32[]{:S(2)}) collective-permute-start(bf16[8,256,256]{2,1,0:T(8,128)(2,1)S(1)} %get-tuple-element.73), channel_id=1, source_target_pairs={{0,1},{1,0},{2,3},{3,2},{4,5},{5,4},{6,7},{7,6},{8,9},{9,8},{10,11... | collective-permute-start | bytes 3145736 | tf_op jit(solution)/shard_map/ppermute | solution.py:388
  19.4 14.8 %collective-permute-start.4 = (bf16[1024,256]{1,0:T(8,128)(2,1)S(1)}, bf16[1024,256]{1,0:T(8,128)(2,1)S(1)}, u32[]{:S(2)}, u32[]{:S(2)}) collective-permute-start(bf16[1024,256]{1,0:T(8,128)(2,1)S(1)} %get-tuple-element.67), channel_id=1, source_target_pairs={{0,4},{1,5},{2,6},{3,7},{4,0},{5,1},{6,2},{7,3},{8,12},{9,13},{10,... | collective-permute-start | bytes 1572872 | tf_op jit(solution)/shard_map/ppermute | solution.py:388
  21.0 26.8 %collective-permute-start.9 = (bf16[1024,384]{1,0:T(8,128)(2,1)}, bf16[1024,384]{1,0:T(8,128)(2,1)S(1)}, u32[]{:S(2)}, u32[]{:S(2)}) collective-permute-start(bf16[1024,384]{1,0:T(8,128)(2,1)} %get-tuple-element.62), channel_id=1, source_target_pairs={{0,2},{1,3},{2,0},{3,1},{4,6},{5,7},{6,4},{7,5},{8,10},{9,11},{10,... | collective-permute-start | bytes 2359304 | tf_op jit(solution)/shard_map/ppermute | solution.py:388
  30.6 6.3 %copy-start.2 = (s32[288,2]{1,0:T(8,128)S(1)}, s32[288,2]{1,0:T(8,128)}, u32[]{:S(2)}) copy-start(s32[288,2]{1,0:T(8,128)} %constant.18.clone.order_ref) | copy-start | bytes 6916
  30.6 17.1 %collective-permute-start.8 = (bf16[512,384]{1,0:T(8,128)(2,1)S(1)}, bf16[512,384]{1,0:T(8,128)(2,1)S(1)}, u32[]{:S(2)}, u32[]{:S(2)}) collective-permute-start(bf16[512,384]{1,0:T(8,128)(2,1)S(1)} %share.10), channel_id=1, source_target_pairs={{0,4},{1,5},{2,6},{3,7},{4,0},{5,1},{6,2},{7,3},{8,12},{9,13},{10,... | collective-permute-start | bytes 1179656 | tf_op jit(solution)/shard_map/ppermute | solution.py:388
  34.2 12.7 %collective-permute-start.7 = (bf16[512,256]{1,0:T(8,128)(2,1)S(1)}, bf16[512,256]{1,0:T(8,128)(2,1)S(1)}, u32[]{:S(2)}, u32[]{:S(2)}) collective-permute-start(bf16[512,256]{1,0:T(8,128)(2,1)S(1)} %share.11), channel_id=1, source_target_pairs={{0,8},{1,9},{2,10},{3,11},{4,12},{5,13},{6,14},{7,15},{8,0},{9,1},... | collective-permute-start | bytes 786440 | tf_op jit(solution)/shard_map/ppermute | solution.py:388
  39.5 20.5 %collective-permute-start.11 = (bf16[1152,256]{1,0:T(8,128)(2,1)S(1)}, bf16[1152,256]{1,0:T(8,128)(2,1)S(1)}, u32[]{:S(2)}, u32[]{:S(2)}) collective-permute-start(bf16[1152,256]{1,0:T(8,128)(2,1)S(1)} %get-tuple-element.71), channel_id=1, source_target_pairs={{0,2},{1,3},{2,0},{3,1},{4,6},{5,7},{6,4},{7,5},{8,10},{9,11},{10,... | collective-permute-start | bytes 1769480 | tf_op jit(solution)/shard_map/ppermute | solution.py:388
  47.9 16.4 %collective-permute-start.10 = (bf16[512,384]{1,0:T(8,128)(2,1)S(1)}, bf16[512,384]{1,0:T(8,128)(2,1)S(1)}, u32[]{:S(2)}, u32[]{:S(2)}) collective-permute-start(bf16[512,384]{1,0:T(8,128)(2,1)S(1)} %share.14), channel_id=1, source_target_pairs={{0,4},{1,5},{2,6},{3,7},{4,0},{5,1},{6,2},{7,3},{8,12},{9,13},{10,... | collective-permute-start | bytes 1179656 | tf_op jit(solution)/shard_map/ppermute | solution.py:388
  50.6 16.6 %collective-permute-start.13 = (bf16[576,256]{1,0:T(8,128)(2,1)S(1)}, bf16[576,256]{1,0:T(8,128)(2,1)S(1)}, u32[]{:S(2)}, u32[]{:S(2)}) collective-permute-start(bf16[576,256]{1,0:T(8,128)(2,1)S(1)} %get-tuple-element.75), channel_id=1, source_target_pairs={{0,2},{1,3},{2,0},{3,1},{4,6},{5,7},{6,4},{7,5},{8,10},{9,11},{10,... | collective-permute-start | bytes 884744 | tf_op jit(solution)/shard_map/ppermute | solution.py:388
  51.2 15.4 %collective-permute-start.12 = (bf16[256,384]{1,0:T(8,128)(2,1)S(1)}, bf16[256,384]{1,0:T(8,128)(2,1)S(1)}, u32[]{:S(2)}, u32[]{:S(2)}) collective-permute-start(bf16[256,384]{1,0:T(8,128)(2,1)S(1)} %share.13), channel_id=1, source_target_pairs={{0,8},{1,9},{2,10},{3,11},{4,12},{5,13},{6,14},{7,15},{8,0},{9,1},... | collective-permute-start | bytes 589832 | tf_op jit(solution)/shard_map/ppermute | solution.py:388
  60.1 15.6 %collective-permute-start.20 = (bf16[576,256]{1,0:T(8,128)(2,1)S(1)}, bf16[576,256]{1,0:T(8,128)(2,1)S(1)}, u32[]{:S(2)}, u32[]{:S(2)}) collective-permute-start(bf16[576,256]{1,0:T(8,128)(2,1)S(1)} %share.15), channel_id=1, source_target_pairs={{0,4},{1,5},{2,6},{3,7},{4,0},{5,1},{6,2},{7,3},{8,12},{9,13},{10,... | collective-permute-start | bytes 884744 | tf_op jit(solution)/shard_map/ppermute | solution.py:388
  64.4 10.6 %collective-permute-start.15 = (bf16[256,384]{1,0:T(8,128)(2,1)S(1)}, bf16[256,384]{1,0:T(8,128)(2,1)S(1)}, u32[]{:S(2)}, u32[]{:S(2)}) collective-permute-start(bf16[256,384]{1,0:T(8,128)(2,1)S(1)} %share.16), channel_id=1, source_target_pairs={{0,8},{1,9},{2,10},{3,11},{4,12},{5,13},{6,14},{7,15},{8,0},{9,1},... | collective-permute-start | bytes 589832 | tf_op jit(solution)/shard_map/ppermute | solution.py:388
  65.0 6.4 %collective-permute-start.14 = (bf16[256,256]{1,0:T(8,128)(2,1)S(1)}, bf16[256,256]{1,0:T(8,128)(2,1)S(1)}, u32[]{:S(2)}, u32[]{:S(2)}) collective-permute-start(bf16[256,256]{1,0:T(8,128)(2,1)S(1)} %share.12), channel_id=1, source_target_pairs={{0,2},{1,3},{2,0},{3,1},{4,6},{5,7},{6,4},{7,5},{8,10},{9,11},{10,... | collective-permute-start | bytes 393224 | tf_op jit(solution)/shard_map/ppermute | solution.py:388
  66.5 9.4 %collective-permute-start.21 = (bf16[576,256]{1,0:T(8,128)(2,1)S(1)}, bf16[576,256]{1,0:T(8,128)(2,1)S(1)}, u32[]{:S(2)}, u32[]{:S(2)}) collective-permute-start(bf16[576,256]{1,0:T(8,128)(2,1)S(1)} %get-tuple-element.96), channel_id=1, source_target_pairs={{0,2},{1,3},{2,0},{3,1},{4,6},{5,7},{6,4},{7,5},{8,10},{9,11},{10,... | collective-permute-start | bytes 884744 | tf_op jit(solution)/shard_map/ppermute | solution.py:388
  67.2 17.2 %collective-permute-start.17 = (f32[144,384]{1,0:T(8,128)S(1)}, f32[144,384]{1,0:T(8,128)S(1)}, u32[]{:S(2)}, u32[]{:S(2)}) collective-permute-start(f32[144,384]{1,0:T(8,128)S(1)} %get-tuple-element.84), channel_id=1, source_target_pairs={{0,1},{1,0},{2,3},{3,2},{4,5},{5,4},{6,7},{7,6},{8,9},{9,8},{10,11... | collective-permute-start | bytes 663560 | tf_op jit(solution)/shard_map/ppermute | solution.py:388
  75.1 9.3 %collective-permute-start.16 = (f32[144,384]{1,0:T(8,128)S(1)}, f32[144,384]{1,0:T(8,128)S(1)}, u32[]{:S(2)}, u32[]{:S(2)}) collective-permute-start(f32[144,384]{1,0:T(8,128)S(1)} %get-tuple-element.90), channel_id=1, source_target_pairs={{0,1},{1,0},{2,3},{3,2},{4,5},{5,4},{6,7},{7,6},{8,9},{9,8},{10,11... | collective-permute-start | bytes 663560 | tf_op jit(solution)/shard_map/ppermute | solution.py:388
  75.2 8.7 %collective-permute-start.22 = (bf16[288,256]{1,0:T(8,128)(2,1)S(1)}, bf16[288,256]{1,0:T(8,128)(2,1)S(1)}, u32[]{:S(2)}, u32[]{:S(2)}) collective-permute-start(bf16[288,256]{1,0:T(8,128)(2,1)S(1)} %get-tuple-element.86), channel_id=1, source_target_pairs={{0,4},{1,5},{2,6},{3,7},{4,0},{5,1},{6,2},{7,3},{8,12},{9,13},{10,... | collective-permute-start | bytes 442376 | tf_op jit(solution)/shard_map/ppermute | solution.py:388
  75.7 8.3 %collective-permute-start.18 = (f32[144,256]{1,0:T(8,128)S(1)}, f32[144,256]{1,0:T(8,128)S(1)}, u32[]{:S(2)}, u32[]{:S(2)}) collective-permute-start(f32[144,256]{1,0:T(8,128)S(1)} %get-tuple-element.88), channel_id=1, source_target_pairs={{0,1},{1,0},{2,3},{3,2},{4,5},{5,4},{6,7},{7,6},{8,9},{9,8},{10,11... | collective-permute-start | bytes 442376 | tf_op jit(solution)/shard_map/ppermute | solution.py:388
  75.9 10.3 %collective-permute-start.23 = (bf16[288,256]{1,0:T(8,128)(2,1)S(1)}, bf16[288,256]{1,0:T(8,128)(2,1)S(1)}, u32[]{:S(2)}, u32[]{:S(2)}) collective-permute-start(bf16[288,256]{1,0:T(8,128)(2,1)S(1)} %share.18), channel_id=1, source_target_pairs={{0,8},{1,9},{2,10},{3,11},{4,12},{5,13},{6,14},{7,15},{8,0},{9,1},... | collective-permute-start | bytes 442376 | tf_op jit(solution)/shard_map/ppermute | solution.py:388
  83.9 10.5 %collective-permute-start.24 = (bf16[288,256]{1,0:T(8,128)(2,1)S(1)}, bf16[288,256]{1,0:T(8,128)(2,1)S(1)}, u32[]{:S(2)}, u32[]{:S(2)}) collective-permute-start(bf16[288,256]{1,0:T(8,128)(2,1)S(1)} %get-tuple-element.104), channel_id=1, source_target_pairs={{0,4},{1,5},{2,6},{3,7},{4,0},{5,1},{6,2},{7,3},{8,12},{9,13},{10,... | collective-permute-start | bytes 442376 | tf_op jit(solution)/shard_map/ppermute | solution.py:388
  84.0 10.5 %collective-permute-start.25 = (bf16[288,256]{1,0:T(8,128)(2,1)S(1)}, bf16[288,256]{1,0:T(8,128)(2,1)S(1)}, u32[]{:S(2)}, u32[]{:S(2)}) collective-permute-start(bf16[288,256]{1,0:T(8,128)(2,1)S(1)} %share.19), channel_id=1, source_target_pairs={{0,8},{1,9},{2,10},{3,11},{4,12},{5,13},{6,14},{7,15},{8,0},{9,1},... | collective-permute-start | bytes 442376 | tf_op jit(solution)/shard_map/ppermute | solution.py:388
  84.4 8.1 %copy-start.4 = (s32[8,3072]{1,0:T(8,128)S(1)}, s32[8,3072]{1,0:T(8,128)}, u32[]{:S(2)}) copy-start(s32[8,3072]{1,0:T(8,128)} %mask_ref.2) | copy-start | bytes 294916
  84.5 8.1 %collective-permute-start.19 = (f32[16,2048]{1,0:T(8,128)S(1)}, f32[16,2048]{1,0:T(8,128)S(1)}, u32[]{:S(2)}, u32[]{:S(2)}) collective-permute-start(f32[16,2048]{1,0:T(8,128)S(1)} %edges.1), channel_id=1, source_target_pairs={{2,1},{4,3},{6,5},{8,7},{10,9},{12,11},{14,13},{0,15},{1,2},{3,4},... | collective-permute-start | bytes 393224 | tf_op jit(solution)/shard_map/ppermute | solution.py:528
  86.3 9.7 %copy-start.7 = (f32[2,24]{1,0:T(2,128)S(1)}, f32[2,24]{1,0:T(2,128)}, u32[]{:S(2)}) copy-start(f32[2,24]{1,0:T(2,128)} %steer_ref.1) | copy-start | bytes 580
  86.3 8.3 %collective-permute-start.26 = (f32[160,256]{1,0:T(8,128)S(1)}, f32[160,256]{1,0:T(8,128)S(1)}, u32[]{:S(2)}, u32[]{:S(2)}) collective-permute-start(f32[160,256]{1,0:T(8,128)S(1)} %get-tuple-element.98), channel_id=1, source_target_pairs={{0,1},{1,0},{2,3},{3,2},{4,5},{5,4},{6,7},{7,6},{8,9},{9,8},{10,11... | collective-permute-start | bytes 491528 | tf_op jit(solution)/shard_map/ppermute | solution.py:388
  94.5 1.5 %collective-permute-start.27 = (f32[160,256]{1,0:T(8,128)S(1)}, f32[160,256]{1,0:T(8,128)S(1)}, u32[]{:S(2)}, u32[]{:S(2)}) collective-permute-start(f32[160,256]{1,0:T(8,128)S(1)} %get-tuple-element.106), channel_id=1, source_target_pairs={{0,1},{1,0},{2,3},{3,2},{4,5},{5,4},{6,7},{7,6},{8,9},{9,8},{10,11... | collective-permute-start | bytes 491528 | tf_op jit(solution)/shard_map/ppermute | solution.py:388

commit v6 on v5

--- a/solution.py
+++ b/solution.py
@@ -20,7 +20,7 @@
 STEPS = (
     (1, 0), (3, 0), (0, 0), (1, 1), (0, 1), (2, 1), (1, 2), (2, 2), (3, 1), (4, 1),
     (2, 3), (1, 3), (0, 2), (3, 2), (0, 11), (0, 3), (1, 4), (4, 2), (2, 4), (0, 4),
-    (3, 3), ("halo", 0), (4, 3), (3, 4), ("gram", 0), (4, 4),
+    ("halo", 0), ("gram", 0), (3, 3), (4, 3), (3, 4), ("edge", 0), (4, 4),
 )
 
 
@@ -198,13 +198,11 @@
     return lambda gates: pl.ds(pl.multiple_of((core ^ half) * (gates // 2) + start, 128), size)
 
 
-def gram_kernel(spans, me_ref, edge_ref, mask_ref, *refs):
+def gram_kernel(spans, rows, me_ref, mask_ref, *refs):
     parts, (gram_ref, window_ref) = refs[:-2], refs[-2:]
-    rows = edge_ref.shape[0]
     inner = parts[0].shape[0]
     core = me_ref[0] % 2
     gates = mask_ref.shape[1]
-    early = sum(size for _, size in spans)
     total = None
     for index, part in enumerate(parts):
         half, (start, size) = index // len(spans), spans[index % len(spans)]
@@ -212,23 +210,21 @@
         inner_at = pl.multiple_of((1 - core) * rows, rows)
         edge_at = pl.multiple_of(core * inner, rows)
         window_ref[half, pl.ds(inner_at, inner), lanes] = part[...]
-        edge = edge_ref[:, half * early + start : half * early + start + size]
-        window_ref[half, pl.ds(edge_at, rows), lanes] = edge
+        window_ref[half, pl.ds(edge_at, rows), lanes] = jnp.zeros((rows, size), F32)
         mask = mask_ref[:, half_lanes(core, half, start, size)(gates)]
         sums = gram_sums(window_ref[half, :, lanes], mask, rows)
         total = sums if total is None else total + sums
     gram_ref[...] = total
 
 
-def gram_of(me, spans, mine, theirs, edge, mask):
+def gram_of(me, spans, mine, theirs, mask, rows):
     bins_here = mask.shape[0]
-    rows = edge.shape[0]
     inner = mine[0].shape[0]
     early = sum(size for _, size in spans)
     return pl.pallas_call(
-        functools.partial(gram_kernel, spans),
+        functools.partial(gram_kernel, spans, rows),
         in_specs=[pl.BlockSpec(memory_space=pltpu.SMEM)]
-        + [pl.BlockSpec(memory_space=pltpu.VMEM)] * (2 + 2 * len(mine)),
+        + [pl.BlockSpec(memory_space=pltpu.VMEM)] * (1 + 2 * len(mine)),
         out_shape=[
             jax.ShapeDtypeStruct((bins_here * 3 * rows, inner + rows), F32),
             jax.ShapeDtypeStruct((2, inner + rows, early), F32),
@@ -236,10 +232,52 @@
         compiler_params=pltpu.CompilerParams(vmem_limit_bytes=VMEM),
         cost_estimate=pl.CostEstimate(flops=1000, bytes_accessed=1000, transcendentals=0),
         name="gram",
-    )(me, edge, mask, *mine, *theirs)
-
-
-def solve(gram, steer, bins_here, beams):
+    )(me, mask, *mine, *theirs)
+
+
+def split_dot(left, right, mask):
+    dims = (((1,), (1,)), ((), ()))
+    keep = mask.astype(BF16)
+    tops = [x.astype(BF16) for x in (left, right)]
+    rests = [(x - top.astype(F32)).astype(BF16) for x, top in zip((left, right), tops)]
+    total = lax.dot_general(tops[0] * keep, tops[1], dims, preferred_element_type=F32)
+    total += lax.dot_general(tops[0] * keep, rests[1], dims, preferred_element_type=F32)
+    return total + lax.dot_general(rests[0] * keep, tops[1], dims, preferred_element_type=F32)
+
+
+def edge_sums(core, edge, window, mask, rows):
+    last = window.shape[0] - 3 * rows
+    held = jnp.where(core == 0, window[: 3 * rows], window[last:])
+    held = jnp.concatenate(
+        [
+            jnp.where(core == 0, edge, held[:rows]),
+            held[rows : 2 * rows],
+            jnp.where(core == 0, held[2 * rows :], edge),
+        ],
+        axis=0,
+    )
+    mask = jnp.where(core == 0, mask[0:1], mask[mask.shape[0] - 1 :]).astype(F32)
+    columns = split_dot(held, edge, mask)
+    lane = lax.broadcasted_iota(jnp.int32, (rows, 3 * rows), 1)
+    first = core * 2 * rows
+    others = (lane < first) | (lane >= first + rows)
+    across = jnp.where(others, split_dot(edge, held, mask), 0.0)
+    blank = jnp.zeros((3 * rows, 2 * rows), F32)
+    columns = jnp.where(
+        core == 0,
+        jnp.concatenate([columns, blank], axis=1),
+        jnp.concatenate([blank, columns], axis=1),
+    )
+    blank = jnp.zeros((2 * rows, 3 * rows), F32)
+    across = jnp.where(
+        core == 0,
+        jnp.concatenate([across, blank], axis=0),
+        jnp.concatenate([blank, across], axis=0),
+    )
+    return columns + across
+
+
+def solve(gram, extra, core, steer, bins_here, beams):
     rows, order = 2 * beams, 3 * beams
     lane = lax.broadcasted_iota(jnp.int32, (1, 1, 128), 2)
     real_lane = lane // beams % 2 == 0
@@ -251,6 +289,10 @@
     pad = jnp.zeros((3 * rows, 128 - 3 * rows), F32)
     for d in range(bins_here):
         block = gram[3 * rows * d : 3 * rows * (d + 1), rows * d : rows * (d + 3)]
+        if d == 0:
+            block = block + jnp.where(core == 0, extra, 0.0)
+        if d == bins_here - 1:
+            block = block + jnp.where(core == 1, extra, 0.0)
         block = jnp.concatenate([block, pad], axis=1)
         pieces = [block[i : i + beams] for i in range(0, 3 * rows, beams)]
         from_re = jnp.concatenate(pieces[0::2], axis=0)
@@ -310,12 +352,17 @@
         out_ref[d, :, at] = jnp.concatenate([row_re, row_im], axis=0)
 
 
-def tail_kernel(me_ref, steer_ref, gram_ref, window_ref, mask_ref, *refs):
+def tail_kernel(me_ref, steer_ref, gram_ref, window_ref, edge_ref, mask_ref, *refs):
     parts, out_ref = refs[:-1], refs[-1]
     bins_here, gates = mask_ref.shape
     rows = window_ref.shape[1] // (bins_here + 2)
     beams = rows // 2
     core = me_ref[0] % 2
+    early = window_ref.shape[2]
+    edge = edge_ref[...]
+    early_mask = [mask_ref[:, half_lanes(core, half, 0, early)(gates)] for half in range(2)]
+    early_window = jnp.concatenate([window_ref[0], window_ref[1]], axis=1)
+    extra = edge_sums(core, edge, early_window, jnp.concatenate(early_mask, axis=1), rows)
     pieces = [(0, 0, window_ref.at[0]), (1, 0, window_ref.at[1])]
     gram = gram_ref[...]
     count = len(parts) // 2
@@ -327,7 +374,7 @@
             gram += gram_sums(ref[...], mask, rows)
             pieces.append((half, start, ref))
             start += size
-    weight_re, weight_im = solve(gram, steer_ref[...], bins_here, beams)
+    weight_re, weight_im = solve(gram, extra, core, steer_ref[...], bins_here, beams)
 
     def split(value):
         return [value[i : i + beams] for i in range(0, value.shape[0], beams)]
@@ -335,22 +382,28 @@
     for half, start, ref in pieces:
         for at in range(0, ref.shape[1], 128):
             lanes = half_lanes(core, half, start + at, 128)(gates)
-            blocks = split(ref[:, at : at + 128])
+            value = ref[:, at : at + 128]
+            blocks = split(value)
+            if start == 0:
+                part = edge[:, half * early + at : half * early + at + 128]
+                low, high = value[:rows], value[value.shape[0] - rows :]
+                blocks[:2] = split(jnp.where(core == 0, part, low))
+                blocks[-2:] = split(jnp.where(core == 0, high, part))
             filter_gates(out_ref, lanes, blocks, weight_re, weight_im, beams)
 
 
-def tail(me, steer, gram, window, mask, mine, theirs):
+def tail(me, steer, gram, window, edge, mask, mine, theirs):
     bins_here, gates = mask.shape
     parts = mine + theirs
     return pl.pallas_call(
         tail_kernel,
         in_specs=[pl.BlockSpec(memory_space=pltpu.SMEM)]
-        + [pl.BlockSpec(memory_space=pltpu.VMEM)] * (4 + len(parts)),
+        + [pl.BlockSpec(memory_space=pltpu.VMEM)] * (5 + len(parts)),
         out_shape=jax.ShapeDtypeStruct((bins_here, 2, gates), F32),
         compiler_params=pltpu.CompilerParams(vmem_limit_bytes=VMEM),
         cost_estimate=pl.CostEstimate(flops=1000, bytes_accessed=1000, transcendentals=0),
         name="tail",
-    )(me, steer, gram, window, mask, *parts)
+    )(me, steer, gram, window, edge, mask, *parts)
 
 
 def slice_kernel(me_ref, echo_ref, part_ref):
@@ -527,8 +580,11 @@
             pairs += [(i, (i + 1) % count) for i in range(1, count, 2)]
             edge = lax.ppermute(out, "elem", pairs)
         elif c == "gram":
-            gram, window = gram_of(at, early, near[:last], far[:last], edge, chain.enter(train_mask))
+            mask = chain.enter(train_mask)
+            gram, window = gram_of(at, early, near[:last], far[:last], mask, rows)
             chain.leave(gram)
+        elif c == "edge":
+            edge = chain.leave(chain.enter(edge))
         elif stage == 0:
             part = chain.leave(other_half(at, chain.enter(echo), *spans[c]))
             theirs[c] = swap(part, 1, count)
@@ -561,7 +617,7 @@
             near[c], send = finish(at, chain.enter(keeps[c]), [x[-1] for x in received[c]], held, step)
             chain.leave(send)
             far[c] = swap(send, 1, count)
-    return tail(at, steer, gram, window, train_mask, near[last:], far[last:])
+    return tail(at, steer, gram, window, edge, train_mask, near[last:], far[last:])
 
 
 def solution(mesh):

time: 102 us -> 100 us (0.980)
  waiting for transfers between devices: 46.5 us -> 40.4 us
  starting transfers between devices: 25.7 us -> 30.3 us
    ppermute x27, waiting for transfers between devices: 40.4 us -> 36.3 us  [swap(): return lax.ppermute(x, 'elem', [(i, i ^ stride) for i in range(count)])]
    ppermute x27, starting transfers between devices: 25.6 us -> 29 us  [swap(): return lax.ppermute(x, 'elem', [(i, i ^ stride) for i in range(count)])]
    ppermute x1, waiting for transfers between devices: 6.17 us -> 4.13 us  [local(): edge = lax.ppermute(out, 'elem', pairs)]
    ppermute x1, starting transfers between devices: 0.07 us -> 1.35 us  [local(): edge = lax.ppermute(out, 'elem', pairs)]
  transfers between devices with their start and end apart: 28 -> 28, of which waited for: 12 -> 15; matrix products, arithmetic and copies ran while one was open for 0% -> 0% of each run, Pallas kernels for 22% -> 22%
where the time goes in v6:
time: 100 us
  waiting for transfers between devices  40.4 us (40%)
  starting transfers between devices  30.3 us (30%)
  Pallas kernels  29 us (29%)
    ppermute x27, waiting for transfers between devices, swap(): return lax.ppermute(x, 'elem', [(i, i ^ stride) for i in range(count)])  36.3 us
    ppermute x27, starting transfers between devices, swap(): return lax.ppermute(x, 'elem', [(i, i ^ stride) for i in range(count)])  29 us
    pallas_call x5, Pallas kernels, front(): pl.pallas_call(functools.partial(front_kernel, bins_chip, ahead is not No...  16 us
    pallas_call x1, Pallas kernels, tail(): pl.pallas_call(tail_kernel, in_specs=[pl.BlockSpec(memory_space=pltpu.SME...  5.62 us
    pallas_call x3, Pallas kernels, other_half(): pl.pallas_call(slice_kernel, grid_spec=pltpu.PrefetchScalarGridSpec(num_s...  4.31 us
    ppermute x1, waiting for transfers between devices, local(): edge = lax.ppermute(out, 'elem', pairs)  4.13 us
  transfers between devices with their start and end apart: 28, of which 15 were waited for; matrix products, arithmetic and copies ran while one was open for 0% of the time, Pallas kernels for 22%

profile of v6, /device:TPU:0, one launch (start us, length us, event | category | flops | bytes accessed | tf_op | source)
XLA Modules:
  0.0 100.1 jit_solution(12946582453518438519)
XLA Ops:
  0.0 1.5 %slice.3 = bf16[8,256,384]{2,1,0:T(8,128)(2,1)S(1)} custom-call(s32[1]{0:T(128)} %bitcast.me_ref, bf16[8,256,3072]{2,1,0:T(8,128)(2,1)} %bitcast.2), custom_call_target="tpu_custom_call" | custom-call | flops 1000 | bytes 1000 | tf_op jit(solution)/shard_map/slice/pallas_call | solution.py:420
  1.5 0.5 collective-permute-start
  2.0 1.3 %slice.4 = bf16[8,256,256]{2,1,0:T(8,128)(2,1)S(1)} custom-call(s32[1]{0:T(128)} %bitcast.me_ref, bf16[8,256,3072]{2,1,0:T(8,128)(2,1)} %bitcast.3), custom_call_target="tpu_custom_call" | custom-call | flops 1000 | bytes 1000 | tf_op jit(solution)/shard_map/slice/pallas_call | solution.py:420
  3.3 1.6 %slice.5 = bf16[8,256,384]{2,1,0:T(8,128)(2,1)S(1)} custom-call(s32[1]{0:T(128)} %bitcast.me_ref, bf16[8,256,3072]{2,1,0:T(8,128)(2,1)} %bitcast.4), custom_call_target="tpu_custom_call" | custom-call | flops 1000 | bytes 1000 | tf_op jit(solution)/shard_map/slice/pallas_call | solution.py:420
  4.9 0.1 collective-permute-start.1
  5.1 3.6 %front.5 = (bf16[1024,384]{1,0:T(8,128)(2,1)S(1)}, f32[1024,384]{1,0:T(8,128)S(1)}, bf16[8,256,256]{2,1,0:T(8,128)(2,1)S(1)}) custom-call(s32[1]{0:T(128)} %bitcast.me_ref, s32[256,2]{1,0:T(8,128)S(1)} %copy-done.3, bf16[256,256]{1,0:T(8,128)(2,1)S(1)} %copy-done, bf16[2,128,16]{2,1,0:T(8,128)(2,1)S(1)} %copy-done.1, bf16[8,2,128]{2,1,0:T(2,128)(2,1)S(1)} %copy-done.6, ...), custom_call_target="tpu_custom_call" | custom-call | flops 1000 | bytes 1000 | tf_op jit(solution)/shard_map/front/pallas_call | solution.py:160
  8.6 0.5 collective-permute-start.2
  9.2 0.1 collective-permute-start.5
  9.2 3.0 %collective-permute-start.3 = (bf16[1024,384]{1,0:T(8,128)(2,1)S(1)}, bf16[1024,384]{1,0:T(8,128)(2,1)S(1)}, u32[]{:S(2)}, u32[]{:S(2)}) collective-permute-start(bf16[1024,384]{1,0:T(8,128)(2,1)S(1)} %get-tuple-element.60), channel_id=1, source_target_pairs={{0,2},{1,3},{2,0},{3,1},{4,6},{5,7},{6,4},{7,5},{8,10},{9,11},{10,... | collective-permute-start | bytes 2359304 | tf_op jit(solution)/shard_map/ppermute | solution.py:441
  12.2 4.1 %front.6 = (bf16[1024,384]{1,0:T(8,128)(2,1)}, f32[1024,384]{1,0:T(8,128)S(1)}) custom-call(s32[1]{0:T(128)} %bitcast.me_ref, s32[256,2]{1,0:T(8,128)S(1)} %copy-done.3, bf16[256,256]{1,0:T(8,128)(2,1)S(1)} %copy-done, bf16[2,128,16]{2,1,0:T(8,128)(2,1)S(1)} %copy-done.1, bf16[8,2,128]{2,1,0:T(2,128)(2,1)S(1)} %copy-done.6, bf16[8,256,3072]{2,1,0:T(8,128)(2,1)} %bitcast.7, ...), custom_call_target="tpu_custom_call" | custom-call | flops 1000 | bytes 1000 | tf_op jit(solution)/shard_map/front/pallas_call | solution.py:160
  16.3 3.0 %front.7 = (bf16[1024,256]{1,0:T(8,128)(2,1)S(1)}, f32[1024,256]{1,0:T(8,128)S(1)}, bf16[8,256,256]{2,1,0:T(8,128)(2,1)S(1)}) custom-call(s32[1]{0:T(128)} %bitcast.me_ref, s32[256,2]{1,0:T(8,128)S(1)} %copy-done.5, bf16[256,256]{1,0:T(8,128)(2,1)S(1)} %copy-done, bf16[2,128,16]{2,1,0:T(8,128)(2,1)S(1)} %copy-done.1, bf16[8,2,128]{2,1,0:T(2,128)(2,1)S(1)} %copy-done.6, ...), custom_call_target="tpu_custom_call" | custom-call | flops 1000 | bytes 1000 | tf_op jit(solution)/shard_map/front/pallas_call | solution.py:160
  19.3 0.1 collective-permute-start.6
  19.4 1.6 %collective-permute-start.4 = (bf16[1024,256]{1,0:T(8,128)(2,1)S(1)}, bf16[1024,256]{1,0:T(8,128)(2,1)S(1)}, u32[]{:S(2)}, u32[]{:S(2)}) collective-permute-start(bf16[1024,256]{1,0:T(8,128)(2,1)S(1)} %get-tuple-element.68), channel_id=1, source_target_pairs={{0,4},{1,5},{2,6},{3,7},{4,0},{5,1},{6,2},{7,3},{8,12},{9,13},{10,... | collective-permute-start | bytes 1572872 | tf_op jit(solution)/shard_map/ppermute | solution.py:441
  21.0 0.5 collective-permute-start.9
  21.5 9.0 %collective-permute-done.3.refs_0_ = bf16[1024,384]{1,0:T(8,128)(2,1)S(1)} collective-permute-done((bf16[1024,384]{1,0:T(8,128)(2,1)S(1)}, bf16[1024,384]{1,0:T(8,128)(2,1)S(1)}, u32[]{:S(2)}, u32[]{:S(2)}) %collective-permute-start.3) | collective-permute-done | bytes 786464 | tf_op jit(solution)/shard_map/ppermute | solution.py:441
  30.5 0.1 share.10
  30.6 2.2 %collective-permute-start.8 = (bf16[512,384]{1,0:T(8,128)(2,1)S(1)}, bf16[512,384]{1,0:T(8,128)(2,1)S(1)}, u32[]{:S(2)}, u32[]{:S(2)}) collective-permute-start(bf16[512,384]{1,0:T(8,128)(2,1)S(1)} %share.10), channel_id=1, source_target_pairs={{0,4},{1,5},{2,6},{3,7},{4,0},{5,1},{6,2},{7,3},{8,12},{9,13},{10,... | collective-permute-start | bytes 1179656 | tf_op jit(solution)/shard_map/ppermute | solution.py:441
  32.8 1.4 %collective-permute-done.4.refs_0_ = bf16[1024,256]{1,0:T(8,128)(2,1)S(1)} collective-permute-done((bf16[1024,256]{1,0:T(8,128)(2,1)S(1)}, bf16[1024,256]{1,0:T(8,128)(2,1)S(1)}, u32[]{:S(2)}, u32[]{:S(2)}) %collective-permute-start.4) | collective-permute-done | bytes 524320 | tf_op jit(solution)/shard_map/ppermute | solution.py:441
  34.2 2.6 %collective-permute-start.7 = (bf16[512,256]{1,0:T(8,128)(2,1)S(1)}, bf16[512,256]{1,0:T(8,128)(2,1)S(1)}, u32[]{:S(2)}, u32[]{:S(2)}) collective-permute-start(bf16[512,256]{1,0:T(8,128)(2,1)S(1)} %share.11), channel_id=1, source_target_pairs={{0,8},{1,9},{2,10},{3,11},{4,12},{5,13},{6,14},{7,15},{8,0},{9,1},... | collective-permute-start | bytes 786440 | tf_op jit(solution)/shard_map/ppermute | solution.py:441
  36.9 2.7 %front.8 = (bf16[1152,256]{1,0:T(8,128)(2,1)S(1)}, f32[1152,256]{1,0:T(8,128)S(1)}) custom-call(s32[1]{0:T(128)} %bitcast.me_ref, s32[288,2]{1,0:T(8,128)S(1)} %copy-done.2, bf16[256,256]{1,0:T(8,128)(2,1)S(1)} %copy-done, bf16[2,128,16]{2,1,0:T(8,128)(2,1)S(1)} %copy-done.1, bf16[8,2,128]{2,1,0:T(2,128)(2,1)S(1)} %copy-done.6, ...), custom_call_target="tpu_custom_call" | custom-call | flops 1000 | bytes 1000 | tf_op jit(solution)/shard_map/front/pallas_call | solution.py:160
  39.5 0.6 collective-permute-start.11
  40.1 2.7 %front.9 = (bf16[576,256]{1,0:T(8,128)(2,1)S(1)}, bf16[576,256]{1,0:T(8,128)(2,1)S(1)}, f32[1152,256]{1,0:T(8,128)S(1)}) custom-call(s32[1]{0:T(128)} %bitcast.me_ref, s32[288,2]{1,0:T(8,128)S(1)} %copy-done.2, bf16[256,256]{1,0:T(8,128)(2,1)S(1)} %copy-done, bf16[2,128,16]{2,1,0:T(8,128)(2,1)S(1)} %copy-done.1, bf16[8,2,128]{2,1,0:T(2,128)(2,1)S(1)} %copy-done.6, ...), custom_call_target="tpu_custom_call" | custom-call | flops 1000 | bytes 1000 | tf_op jit(solution)/shard_map/front/pallas_call | solution.py:160
  42.8 4.1 %collective-permute-done.7.refs_1_ = bf16[512,256]{1,0:T(8,128)(2,1)S(1)} collective-permute-done((bf16[512,256]{1,0:T(8,128)(2,1)S(1)}, bf16[512,256]{1,0:T(8,128)(2,1)S(1)}, u32[]{:S(2)}, u32[]{:S(2)}) %collective-permute-start.7) | collective-permute-done | bytes 262176 | tf_op jit(solution)/shard_map/ppermute | solution.py:441
  46.9 0.8 collective-permute-done.8.refs_1_
  47.8 0.1 share.13
  47.8 0.1 share.14
  47.9 2.7 %collective-permute-start.10 = (bf16[512,384]{1,0:T(8,128)(2,1)S(1)}, bf16[512,384]{1,0:T(8,128)(2,1)S(1)}, u32[]{:S(2)}, u32[]{:S(2)}) collective-permute-start(bf16[512,384]{1,0:T(8,128)(2,1)S(1)} %share.14), channel_id=1, source_target_pairs={{0,4},{1,5},{2,6},{3,7},{4,0},{5,1},{6,2},{7,3},{8,12},{9,13},{10,... | collective-permute-start | bytes 1179656 | tf_op jit(solution)/shard_map/ppermute | solution.py:441
  50.6 0.5 collective-permute-start.13
  51.2 2.6 %collective-permute-start.12 = (bf16[256,384]{1,0:T(8,128)(2,1)S(1)}, bf16[256,384]{1,0:T(8,128)(2,1)S(1)}, u32[]{:S(2)}, u32[]{:S(2)}) collective-permute-start(bf16[256,384]{1,0:T(8,128)(2,1)S(1)} %share.13), channel_id=1, source_target_pairs={{0,8},{1,9},{2,10},{3,11},{4,12},{5,13},{6,14},{7,15},{8,0},{9,1},... | collective-permute-start | bytes 589832 | tf_op jit(solution)/shard_map/ppermute | solution.py:441
  53.7 1.0 collective-permute-start.14
  54.7 5.3 %collective-permute-done.11.refs_0_ = bf16[1152,256]{1,0:T(8,128)(2,1)S(1)} collective-permute-done((bf16[1152,256]{1,0:T(8,128)(2,1)S(1)}, bf16[1152,256]{1,0:T(8,128)(2,1)S(1)}, u32[]{:S(2)}, u32[]{:S(2)}) %collective-permute-start.11) | collective-permute-done | bytes 589856 | tf_op jit(solution)/shard_map/ppermute | solution.py:441
  60.0 0.1 share.15
  60.1 3.0 %collective-permute-done.10.refs_1_ = bf16[512,384]{1,0:T(8,128)(2,1)S(1)} collective-permute-done((bf16[512,384]{1,0:T(8,128)(2,1)S(1)}, bf16[512,384]{1,0:T(8,128)(2,1)S(1)}, u32[]{:S(2)}, u32[]{:S(2)}) %collective-permute-start.10) | collective-permute-done | bytes 393248 | tf_op jit(solution)/shard_map/ppermute | solution.py:441
  63.1 0.1 share.16
  63.2 0.3 collective-permute-start.15
  63.5 2.5 %collective-permute-start.20 = (bf16[576,256]{1,0:T(8,128)(2,1)S(1)}, bf16[576,256]{1,0:T(8,128)(2,1)S(1)}, u32[]{:S(2)}, u32[]{:S(2)}) collective-permute-start(bf16[576,256]{1,0:T(8,128)(2,1)S(1)} %share.15), channel_id=1, source_target_pairs={{0,4},{1,5},{2,6},{3,7},{4,0},{5,1},{6,2},{7,3},{8,12},{9,13},{10,... | collective-permute-start | bytes 884744 | tf_op jit(solution)/shard_map/ppermute | solution.py:441
  66.0 0.2 finish.5
  66.1 0.2 collective-permute-done.13.refs_0_
  66.3 0.1 share.17
  66.4 2.2 %collective-permute-done.14.refs_2_ = bf16[256,256]{1,0:T(8,128)(2,1)S(1)} collective-permute-done((bf16[256,256]{1,0:T(8,128)(2,1)S(1)}, bf16[256,256]{1,0:T(8,128)(2,1)S(1)}, u32[]{:S(2)}, u32[]{:S(2)}) %collective-permute-start.14) | collective-permute-done | bytes 131104 | tf_op jit(solution)/shard_map/ppermute | solution.py:441
  68.6 0.1 finish.6
  68.7 0.1 collective-permute-start.18
  68.8 1.8 %collective-permute-start.21 = (bf16[576,256]{1,0:T(8,128)(2,1)S(1)}, bf16[576,256]{1,0:T(8,128)(2,1)S(1)}, u32[]{:S(2)}, u32[]{:S(2)}) collective-permute-start(bf16[576,256]{1,0:T(8,128)(2,1)S(1)} %get-tuple-element.100), channel_id=1, source_target_pairs={{0,2},{1,3},{2,0},{3,1},{4,6},{5,7},{6,4},{7,5},{8,10},{9,11},{10,... | collective-permute-start | bytes 884744 | tf_op jit(solution)/shard_map/ppermute | solution.py:441
  70.6 0.2 collective-permute-start.17
  70.8 1.9 %collective-permute-done.15.refs_2_ = bf16[256,384]{1,0:T(8,128)(2,1)S(1)} collective-permute-done((bf16[256,384]{1,0:T(8,128)(2,1)S(1)}, bf16[256,384]{1,0:T(8,128)(2,1)S(1)}, u32[]{:S(2)}, u32[]{:S(2)}) %collective-permute-start.15) | collective-permute-done | bytes 196640 | tf_op jit(solution)/shard_map/ppermute | solution.py:441
  72.7 0.2 finish.7
  72.8 0.1 collective-permute-start.16
  72.9 0.1 collective-permute-start.22
  73.0 1.4 %collective-permute-done.16.refs_3_.refs_0_ = f32[144,384]{1,0:T(8,128)S(1)} collective-permute-done((f32[144,384]{1,0:T(8,128)S(1)}, f32[144,384]{1,0:T(8,128)S(1)}, u32[]{:S(2)}, u32[]{:S(2)}) %collective-permute-start.16) | collective-permute-done | bytes 221216 | tf_op jit(solution)/shard_map/ppermute | solution.py:441
  74.4 1.8 %gram.1 = (f32[384,160]{1,0:T(8,128)S(1)}, f32[2,160,1024]{2,1,0:T(8,128)S(1)}) custom-call(s32[1]{0:T(128)} %bitcast.me_ref, s32[8,3072]{1,0:T(8,128)S(1)} %copy-done.4, f32[144,384]{1,0:T(8,128)S(1)} %get-tuple-element.93.refs_0_.refs_3_, f32[144,384]{1,0:T(8,128)S(1)} %get-tuple-element.94.refs_1_.refs_4_, ...), custom_call_target="tpu_custom_call" | custom-call | flops 1000 | bytes 1000 | tf_op jit(solution)/shard_map/gram/pallas_call | solution.py:224
  76.3 1.7 %collective-permute-start.23 = (bf16[288,256]{1,0:T(8,128)(2,1)S(1)}, bf16[288,256]{1,0:T(8,128)(2,1)S(1)}, u32[]{:S(2)}, u32[]{:S(2)}) collective-permute-start(bf16[288,256]{1,0:T(8,128)(2,1)S(1)} %share.18), channel_id=1, source_target_pairs={{0,8},{1,9},{2,10},{3,11},{4,12},{5,13},{6,14},{7,15},{8,0},{9,1},... | collective-permute-start | bytes 442376 | tf_op jit(solution)/shard_map/ppermute | solution.py:441
  78.0 1.4 %collective-permute-start.24 = (bf16[288,256]{1,0:T(8,128)(2,1)S(1)}, bf16[288,256]{1,0:T(8,128)(2,1)S(1)}, u32[]{:S(2)}, u32[]{:S(2)}) collective-permute-start(bf16[288,256]{1,0:T(8,128)(2,1)S(1)} %get-tuple-element.106), channel_id=1, source_target_pairs={{0,4},{1,5},{2,6},{3,7},{4,0},{5,1},{6,2},{7,3},{8,12},{9,13},{10,... | collective-permute-start | bytes 442376 | tf_op jit(solution)/shard_map/ppermute | solution.py:441
  79.4 1.7 %collective-permute-start.25 = (bf16[288,256]{1,0:T(8,128)(2,1)S(1)}, bf16[288,256]{1,0:T(8,128)(2,1)S(1)}, u32[]{:S(2)}, u32[]{:S(2)}) collective-permute-start(bf16[288,256]{1,0:T(8,128)(2,1)S(1)} %share.19), channel_id=1, source_target_pairs={{0,8},{1,9},{2,10},{3,11},{4,12},{5,13},{6,14},{7,15},{8,0},{9,1},... | collective-permute-start | bytes 442376 | tf_op jit(solution)/shard_map/ppermute | solution.py:441
  81.2 1.4 %collective-permute-start.19 = (f32[16,2048]{1,0:T(8,128)S(1)}, f32[16,2048]{1,0:T(8,128)S(1)}, u32[]{:S(2)}, u32[]{:S(2)}) collective-permute-start(f32[16,2048]{1,0:T(8,128)S(1)} %edges.1), channel_id=1, source_target_pairs={{2,1},{4,3},{6,5},{8,7},{10,9},{12,11},{14,13},{0,15},{1,2},{3,4},... | collective-permute-start | bytes 393224 | tf_op jit(solution)/shard_map/ppermute | solution.py:581
  82.5 4.8 %collective-permute-done.23.refs_2_ = bf16[288,256]{1,0:T(8,128)(2,1)S(1)} collective-permute-done((bf16[288,256]{1,0:T(8,128)(2,1)S(1)}, bf16[288,256]{1,0:T(8,128)(2,1)S(1)}, u32[]{:S(2)}, u32[]{:S(2)}) %collective-permute-start.23) | collective-permute-done | bytes 147488 | tf_op jit(solution)/shard_map/ppermute | solution.py:441
  87.4 0.1 finish.8
  87.5 4.1 %collective-permute-done.19.edge_ref = f32[16,2048]{1,0:T(8,128)S(1)} collective-permute-done((f32[16,2048]{1,0:T(8,128)S(1)}, f32[16,2048]{1,0:T(8,128)S(1)}, u32[]{:S(2)}, u32[]{:S(2)}) %collective-permute-start.19) | collective-permute-done | bytes 131104 | tf_op jit(solution)/shard_map/ppermute | solution.py:581
  91.6 1.1 %collective-permute-done.25.refs_2_ = bf16[288,256]{1,0:T(8,128)(2,1)S(1)} collective-permute-done((bf16[288,256]{1,0:T(8,128)(2,1)S(1)}, bf16[288,256]{1,0:T(8,128)(2,1)S(1)}, u32[]{:S(2)}, u32[]{:S(2)}) %collective-permute-start.25) | collective-permute-done | bytes 147488 | tf_op jit(solution)/shard_map/ppermute | solution.py:441
  92.7 0.1 finish.9
  92.8 0.1 collective-permute-start.27
  92.9 0.5 collective-permute-start.26
  93.4 0.9 collective-permute-done.27.refs_3_
  94.2 0.2 collective-permute-done.26.refs_2_
  94.5 5.6 %tail.1 = f32[8,2,3072]{2,1,0:T(2,128)} custom-call(s32[1]{0:T(128)} %bitcast.me_ref, f32[2,24]{1,0:T(2,128)S(1)} %copy-done.7, f32[384,160]{1,0:T(8,128)S(1)} %get-tuple-element.96.gram_ref, f32[2,160,1024]{2,1,0:T(8,128)S(1)} %get-tuple-element.97.window_ref, f32[16,2048]{1,0:T(8,128)S(1)} %collective-permute-done.19.edge_ref, s32[8,3072]{1,0:T(8,128)S(1)} %copy-done.4, ...), custom_call_target="tpu_custom_call" | custom-call | flops 1000 | bytes 1000 | tf_op jit(solution)/shard_map/tail/pallas_call | solution.py:398
  (34 shorter events, 0.3 us)
Async XLA Ops:
  1.5 3.6 %collective-permute-start = (bf16[8,256,384]{2,1,0:T(8,128)(2,1)S(1)}, bf16[8,256,384]{2,1,0:T(8,128)(2,1)S(1)}, u32[]{:S(2)}, u32[]{:S(2)}) collective-permute-start(bf16[8,256,384]{2,1,0:T(8,128)(2,1)S(1)} %slice.3), channel_id=1, source_target_pairs={{0,1},{1,0},{2,3},{3,2},{4,5},{5,4},{6,7},{7,6},{8,9},{9,8},{10,11... | collective-permute-start | bytes 4718600 | tf_op jit(solution)/shard_map/ppermute | solution.py:441
  3.3 1.8 %copy-start = (bf16[256,256]{1,0:T(8,128)(2,1)S(1)}, bf16[256,256]{1,0:T(8,128)(2,1)}, u32[]{:S(2)}) copy-start(bf16[256,256]{1,0:T(8,128)(2,1)} %constant.15.clone.natural_ref) | copy-start | bytes 393220
  3.3 1.8 %copy-start.1 = (bf16[2,128,16]{2,1,0:T(8,128)(2,1)S(1)}, bf16[2,128,16]{2,1,0:T(8,128)(2,1)}, u32[]{:S(2)}) copy-start(bf16[2,128,16]{2,1,0:T(8,128)(2,1)} %constant.16.clone.picks_ref) | copy-start | bytes 24580
  3.3 1.7 %copy-start.3 = (s32[256,2]{1,0:T(8,128)S(1)}, s32[256,2]{1,0:T(8,128)}, u32[]{:S(2)}) copy-start(s32[256,2]{1,0:T(8,128)} %constant.14.clone.order_ref) | copy-start | bytes 6148
  3.3 1.7 %copy-start.6 = (bf16[8,2,128]{2,1,0:T(2,128)(2,1)S(1)}, bf16[8,2,128]{2,1,0:T(2,128)(2,1)}, u32[]{:S(2)}) copy-start(bf16[8,2,128]{2,1,0:T(2,128)(2,1)} %beam_ref.9) | copy-start | bytes 12292
  4.9 7.3 %collective-permute-start.1 = (bf16[8,256,384]{2,1,0:T(8,128)(2,1)S(1)}, bf16[8,256,384]{2,1,0:T(8,128)(2,1)S(1)}, u32[]{:S(2)}, u32[]{:S(2)}) collective-permute-start(bf16[8,256,384]{2,1,0:T(8,128)(2,1)S(1)} %slice.5), channel_id=1, source_target_pairs={{0,1},{1,0},{2,3},{3,2},{4,5},{5,4},{6,7},{7,6},{8,9},{9,8},{10,11... | collective-permute-start | bytes 4718600 | tf_op jit(solution)/shard_map/ppermute | solution.py:441
  8.6 7.6 %collective-permute-start.2 = (bf16[8,256,256]{2,1,0:T(8,128)(2,1)S(1)}, bf16[8,256,256]{2,1,0:T(8,128)(2,1)S(1)}, u32[]{:S(2)}, u32[]{:S(2)}) collective-permute-start(bf16[8,256,256]{2,1,0:T(8,128)(2,1)S(1)} %get-tuple-element.65), channel_id=1, source_target_pairs={{0,1},{1,0},{2,3},{3,2},{4,5},{5,4},{6,7},{7,6},{8,9},{9,8},{10,11... | collective-permute-start | bytes 3145736 | tf_op jit(solution)/shard_map/ppermute | solution.py:441
  9.2 27.7 %collective-permute-start.5 = (bf16[8,256,256]{2,1,0:T(8,128)(2,1)S(1)}, bf16[8,256,256]{2,1,0:T(8,128)(2,1)S(1)}, u32[]{:S(2)}, u32[]{:S(2)}) collective-permute-start(bf16[8,256,256]{2,1,0:T(8,128)(2,1)S(1)} %slice.4), channel_id=1, source_target_pairs={{0,1},{1,0},{2,3},{3,2},{4,5},{5,4},{6,7},{7,6},{8,9},{9,8},{10,11... | collective-permute-start | bytes 3145736 | tf_op jit(solution)/shard_map/ppermute | solution.py:441
  9.2 7.1 %copy-start.5 = (s32[256,2]{1,0:T(8,128)S(1)}, s32[256,2]{1,0:T(8,128)}, u32[]{:S(2)}) copy-start(s32[256,2]{1,0:T(8,128)} %constant.17.clone.order_ref) | copy-start | bytes 6148
  9.2 21.3 %collective-permute-start.3 = (bf16[1024,384]{1,0:T(8,128)(2,1)S(1)}, bf16[1024,384]{1,0:T(8,128)(2,1)S(1)}, u32[]{:S(2)}, u32[]{:S(2)}) collective-permute-start(bf16[1024,384]{1,0:T(8,128)(2,1)S(1)} %get-tuple-element.60), channel_id=1, source_target_pairs={{0,2},{1,3},{2,0},{3,1},{4,6},{5,7},{6,4},{7,5},{8,10},{9,11},{10,... | collective-permute-start | bytes 2359304 | tf_op jit(solution)/shard_map/ppermute | solution.py:441
  19.3 20.8 %collective-permute-start.6 = (bf16[8,256,256]{2,1,0:T(8,128)(2,1)S(1)}, bf16[8,256,256]{2,1,0:T(8,128)(2,1)S(1)}, u32[]{:S(2)}, u32[]{:S(2)}) collective-permute-start(bf16[8,256,256]{2,1,0:T(8,128)(2,1)S(1)} %get-tuple-element.74), channel_id=1, source_target_pairs={{0,1},{1,0},{2,3},{3,2},{4,5},{5,4},{6,7},{7,6},{8,9},{9,8},{10,11... | collective-permute-start | bytes 3145736 | tf_op jit(solution)/shard_map/ppermute | solution.py:441
  19.4 14.8 %collective-permute-start.4 = (bf16[1024,256]{1,0:T(8,128)(2,1)S(1)}, bf16[1024,256]{1,0:T(8,128)(2,1)S(1)}, u32[]{:S(2)}, u32[]{:S(2)}) collective-permute-start(bf16[1024,256]{1,0:T(8,128)(2,1)S(1)} %get-tuple-element.68), channel_id=1, source_target_pairs={{0,4},{1,5},{2,6},{3,7},{4,0},{5,1},{6,2},{7,3},{8,12},{9,13},{10,... | collective-permute-start | bytes 1572872 | tf_op jit(solution)/shard_map/ppermute | solution.py:441
  21.0 26.8 %collective-permute-start.9 = (bf16[1024,384]{1,0:T(8,128)(2,1)}, bf16[1024,384]{1,0:T(8,128)(2,1)S(1)}, u32[]{:S(2)}, u32[]{:S(2)}) collective-permute-start(bf16[1024,384]{1,0:T(8,128)(2,1)} %get-tuple-element.63), channel_id=1, source_target_pairs={{0,2},{1,3},{2,0},{3,1},{4,6},{5,7},{6,4},{7,5},{8,10},{9,11},{10,... | collective-permute-start | bytes 2359304 | tf_op jit(solution)/shard_map/ppermute | solution.py:441
  30.6 6.3 %copy-start.2 = (s32[288,2]{1,0:T(8,128)S(1)}, s32[288,2]{1,0:T(8,128)}, u32[]{:S(2)}) copy-start(s32[288,2]{1,0:T(8,128)} %constant.18.clone.order_ref) | copy-start | bytes 6916
  30.6 17.1 %collective-permute-start.8 = (bf16[512,384]{1,0:T(8,128)(2,1)S(1)}, bf16[512,384]{1,0:T(8,128)(2,1)S(1)}, u32[]{:S(2)}, u32[]{:S(2)}) collective-permute-start(bf16[512,384]{1,0:T(8,128)(2,1)S(1)} %share.10), channel_id=1, source_target_pairs={{0,4},{1,5},{2,6},{3,7},{4,0},{5,1},{6,2},{7,3},{8,12},{9,13},{10,... | collective-permute-start | bytes 1179656 | tf_op jit(solution)/shard_map/ppermute | solution.py:441
  34.2 12.7 %collective-permute-start.7 = (bf16[512,256]{1,0:T(8,128)(2,1)S(1)}, bf16[512,256]{1,0:T(8,128)(2,1)S(1)}, u32[]{:S(2)}, u32[]{:S(2)}) collective-permute-start(bf16[512,256]{1,0:T(8,128)(2,1)S(1)} %share.11), channel_id=1, source_target_pairs={{0,8},{1,9},{2,10},{3,11},{4,12},{5,13},{6,14},{7,15},{8,0},{9,1},... | collective-permute-start | bytes 786440 | tf_op jit(solution)/shard_map/ppermute | solution.py:441
  39.5 20.5 %collective-permute-start.11 = (bf16[1152,256]{1,0:T(8,128)(2,1)S(1)}, bf16[1152,256]{1,0:T(8,128)(2,1)S(1)}, u32[]{:S(2)}, u32[]{:S(2)}) collective-permute-start(bf16[1152,256]{1,0:T(8,128)(2,1)S(1)} %get-tuple-element.72), channel_id=1, source_target_pairs={{0,2},{1,3},{2,0},{3,1},{4,6},{5,7},{6,4},{7,5},{8,10},{9,11},{10,... | collective-permute-start | bytes 1769480 | tf_op jit(solution)/shard_map/ppermute | solution.py:441
  47.9 15.2 %collective-permute-start.10 = (bf16[512,384]{1,0:T(8,128)(2,1)S(1)}, bf16[512,384]{1,0:T(8,128)(2,1)S(1)}, u32[]{:S(2)}, u32[]{:S(2)}) collective-permute-start(bf16[512,384]{1,0:T(8,128)(2,1)S(1)} %share.14), channel_id=1, source_target_pairs={{0,4},{1,5},{2,6},{3,7},{4,0},{5,1},{6,2},{7,3},{8,12},{9,13},{10,... | collective-permute-start | bytes 1179656 | tf_op jit(solution)/shard_map/ppermute | solution.py:441
  50.6 15.7 %collective-permute-start.13 = (bf16[576,256]{1,0:T(8,128)(2,1)S(1)}, bf16[576,256]{1,0:T(8,128)(2,1)S(1)}, u32[]{:S(2)}, u32[]{:S(2)}) collective-permute-start(bf16[576,256]{1,0:T(8,128)(2,1)S(1)} %get-tuple-element.76), channel_id=1, source_target_pairs={{0,2},{1,3},{2,0},{3,1},{4,6},{5,7},{6,4},{7,5},{8,10},{9,11},{10,... | collective-permute-start | bytes 884744 | tf_op jit(solution)/shard_map/ppermute | solution.py:441
  51.2 14.8 %collective-permute-start.12 = (bf16[256,384]{1,0:T(8,128)(2,1)S(1)}, bf16[256,384]{1,0:T(8,128)(2,1)S(1)}, u32[]{:S(2)}, u32[]{:S(2)}) collective-permute-start(bf16[256,384]{1,0:T(8,128)(2,1)S(1)} %share.13), channel_id=1, source_target_pairs={{0,8},{1,9},{2,10},{3,11},{4,12},{5,13},{6,14},{7,15},{8,0},{9,1},... | collective-permute-start | bytes 589832 | tf_op jit(solution)/shard_map/ppermute | solution.py:441
  53.7 14.9 %collective-permute-start.14 = (bf16[256,256]{1,0:T(8,128)(2,1)S(1)}, bf16[256,256]{1,0:T(8,128)(2,1)S(1)}, u32[]{:S(2)}, u32[]{:S(2)}) collective-permute-start(bf16[256,256]{1,0:T(8,128)(2,1)S(1)} %share.12), channel_id=1, source_target_pairs={{0,2},{1,3},{2,0},{3,1},{4,6},{5,7},{6,4},{7,5},{8,10},{9,11},{10,... | collective-permute-start | bytes 393224 | tf_op jit(solution)/shard_map/ppermute | solution.py:441
  63.2 9.5 %collective-permute-start.15 = (bf16[256,384]{1,0:T(8,128)(2,1)S(1)}, bf16[256,384]{1,0:T(8,128)(2,1)S(1)}, u32[]{:S(2)}, u32[]{:S(2)}) collective-permute-start(bf16[256,384]{1,0:T(8,128)(2,1)S(1)} %share.16), channel_id=1, source_target_pairs={{0,8},{1,9},{2,10},{3,11},{4,12},{5,13},{6,14},{7,15},{8,0},{9,1},... | collective-permute-start | bytes 589832 | tf_op jit(solution)/shard_map/ppermute | solution.py:441
  63.5 12.7 %collective-permute-start.20 = (bf16[576,256]{1,0:T(8,128)(2,1)S(1)}, bf16[576,256]{1,0:T(8,128)(2,1)S(1)}, u32[]{:S(2)}, u32[]{:S(2)}) collective-permute-start(bf16[576,256]{1,0:T(8,128)(2,1)S(1)} %share.15), channel_id=1, source_target_pairs={{0,4},{1,5},{2,6},{3,7},{4,0},{5,1},{6,2},{7,3},{8,12},{9,13},{10,... | collective-permute-start | bytes 884744 | tf_op jit(solution)/shard_map/ppermute | solution.py:441
  68.7 5.7 %copy-start.4 = (s32[8,3072]{1,0:T(8,128)S(1)}, s32[8,3072]{1,0:T(8,128)}, u32[]{:S(2)}) copy-start(s32[8,3072]{1,0:T(8,128)} %mask_ref.2) | copy-start | bytes 294916
  68.7 4.2 %collective-permute-start.18 = (f32[144,256]{1,0:T(8,128)S(1)}, f32[144,256]{1,0:T(8,128)S(1)}, u32[]{:S(2)}, u32[]{:S(2)}) collective-permute-start(f32[144,256]{1,0:T(8,128)S(1)} %get-tuple-element.89), channel_id=1, source_target_pairs={{0,1},{1,0},{2,3},{3,2},{4,5},{5,4},{6,7},{7,6},{8,9},{9,8},{10,11... | collective-permute-start | bytes 442376 | tf_op jit(solution)/shard_map/ppermute | solution.py:441
  68.8 10.6 %collective-permute-start.21 = (bf16[576,256]{1,0:T(8,128)(2,1)S(1)}, bf16[576,256]{1,0:T(8,128)(2,1)S(1)}, u32[]{:S(2)}, u32[]{:S(2)}) collective-permute-start(bf16[576,256]{1,0:T(8,128)(2,1)S(1)} %get-tuple-element.100), channel_id=1, source_target_pairs={{0,2},{1,3},{2,0},{3,1},{4,6},{5,7},{6,4},{7,5},{8,10},{9,11},{10,... | collective-permute-start | bytes 884744 | tf_op jit(solution)/shard_map/ppermute | solution.py:441
  70.6 2.4 %collective-permute-start.17 = (f32[144,384]{1,0:T(8,128)S(1)}, f32[144,384]{1,0:T(8,128)S(1)}, u32[]{:S(2)}, u32[]{:S(2)}) collective-permute-start(f32[144,384]{1,0:T(8,128)S(1)} %get-tuple-element.85), channel_id=1, source_target_pairs={{0,1},{1,0},{2,3},{3,2},{4,5},{5,4},{6,7},{7,6},{8,9},{9,8},{10,11... | collective-permute-start | bytes 663560 | tf_op jit(solution)/shard_map/ppermute | solution.py:441
  72.8 1.5 %collective-permute-start.16 = (f32[144,384]{1,0:T(8,128)S(1)}, f32[144,384]{1,0:T(8,128)S(1)}, u32[]{:S(2)}, u32[]{:S(2)}) collective-permute-start(f32[144,384]{1,0:T(8,128)S(1)} %get-tuple-element.91), channel_id=1, source_target_pairs={{0,1},{1,0},{2,3},{3,2},{4,5},{5,4},{6,7},{7,6},{8,9},{9,8},{10,11... | collective-permute-start | bytes 663560 | tf_op jit(solution)/shard_map/ppermute | solution.py:441
  72.9 6.4 %collective-permute-start.22 = (bf16[288,256]{1,0:T(8,128)(2,1)S(1)}, bf16[288,256]{1,0:T(8,128)(2,1)S(1)}, u32[]{:S(2)}, u32[]{:S(2)}) collective-permute-start(bf16[288,256]{1,0:T(8,128)(2,1)S(1)} %get-tuple-element.87), channel_id=1, source_target_pairs={{0,4},{1,5},{2,6},{3,7},{4,0},{5,1},{6,2},{7,3},{8,12},{9,13},{10,... | collective-permute-start | bytes 442376 | tf_op jit(solution)/shard_map/ppermute | solution.py:441
  76.3 11.1 %collective-permute-start.23 = (bf16[288,256]{1,0:T(8,128)(2,1)S(1)}, bf16[288,256]{1,0:T(8,128)(2,1)S(1)}, u32[]{:S(2)}, u32[]{:S(2)}) collective-permute-start(bf16[288,256]{1,0:T(8,128)(2,1)S(1)} %share.18), channel_id=1, source_target_pairs={{0,8},{1,9},{2,10},{3,11},{4,12},{5,13},{6,14},{7,15},{8,0},{9,1},... | collective-permute-start | bytes 442376 | tf_op jit(solution)/shard_map/ppermute | solution.py:441
  78.0 13.6 %collective-permute-start.24 = (bf16[288,256]{1,0:T(8,128)(2,1)S(1)}, bf16[288,256]{1,0:T(8,128)(2,1)S(1)}, u32[]{:S(2)}, u32[]{:S(2)}) collective-permute-start(bf16[288,256]{1,0:T(8,128)(2,1)S(1)} %get-tuple-element.106), channel_id=1, source_target_pairs={{0,4},{1,5},{2,6},{3,7},{4,0},{5,1},{6,2},{7,3},{8,12},{9,13},{10,... | collective-permute-start | bytes 442376 | tf_op jit(solution)/shard_map/ppermute | solution.py:441
  79.4 13.3 %collective-permute-start.25 = (bf16[288,256]{1,0:T(8,128)(2,1)S(1)}, bf16[288,256]{1,0:T(8,128)(2,1)S(1)}, u32[]{:S(2)}, u32[]{:S(2)}) collective-permute-start(bf16[288,256]{1,0:T(8,128)(2,1)S(1)} %share.19), channel_id=1, source_target_pairs={{0,8},{1,9},{2,10},{3,11},{4,12},{5,13},{6,14},{7,15},{8,0},{9,1},... | collective-permute-start | bytes 442376 | tf_op jit(solution)/shard_map/ppermute | solution.py:441
  81.2 13.3 %copy-start.7 = (f32[2,24]{1,0:T(2,128)S(1)}, f32[2,24]{1,0:T(2,128)}, u32[]{:S(2)}) copy-start(f32[2,24]{1,0:T(2,128)} %steer_ref.1) | copy-start | bytes 580
  81.2 10.4 %collective-permute-start.19 = (f32[16,2048]{1,0:T(8,128)S(1)}, f32[16,2048]{1,0:T(8,128)S(1)}, u32[]{:S(2)}, u32[]{:S(2)}) collective-permute-start(f32[16,2048]{1,0:T(8,128)S(1)} %edges.1), channel_id=1, source_target_pairs={{2,1},{4,3},{6,5},{8,7},{10,9},{12,11},{14,13},{0,15},{1,2},{3,4},... | collective-permute-start | bytes 393224 | tf_op jit(solution)/shard_map/ppermute | solution.py:581
  92.8 1.5 %collective-permute-start.27 = (f32[160,256]{1,0:T(8,128)S(1)}, f32[160,256]{1,0:T(8,128)S(1)}, u32[]{:S(2)}, u32[]{:S(2)}) collective-permute-start(f32[160,256]{1,0:T(8,128)S(1)} %get-tuple-element.108), channel_id=1, source_target_pairs={{0,1},{1,0},{2,3},{3,2},{4,5},{5,4},{6,7},{7,6},{8,9},{9,8},{10,11... | collective-permute-start | bytes 491528 | tf_op jit(solution)/shard_map/ppermute | solution.py:441
  92.9 1.6 %collective-permute-start.26 = (f32[160,256]{1,0:T(8,128)S(1)}, f32[160,256]{1,0:T(8,128)S(1)}, u32[]{:S(2)}, u32[]{:S(2)}) collective-permute-start(f32[160,256]{1,0:T(8,128)S(1)} %get-tuple-element.102), channel_id=1, source_target_pairs={{0,1},{1,0},{2,3},{3,2},{4,5},{5,4},{6,7},{7,6},{8,9},{9,8},{10,11... | collective-permute-start | bytes 491528 | tf_op jit(solution)/shard_map/ppermute | solution.py:441

commit v7 on v6

--- a/solution.py
+++ b/solution.py
@@ -74,58 +74,66 @@
         refs[2 + parts][...] = refs[0][...]
         refs = refs[1 : 2 + parts] + refs[3 + parts :]
     sends, keep_ref, table_ref, weights_ref, spectra_ref = refs[:parts], *refs[parts:]
-    elem_dev = mine_ref.shape[0]
+    each = mine_ref.shape[0]
+    elem_dev = 2 * each
     groups = spectra_ref.shape[0]
     width = mine_ref.shape[-1]
     rows_in = natural_ref.shape[0]
-    me = me_ref[0]
-    order = order_ref[...]
-    source = jnp.bitwise_xor(order[:, 0:1], me // 2) * (2 * bins_chip) + order[:, 1:2]
-    source = lax.rem(source + rows_in, rows_in)
-    lane = lax.broadcasted_iota(jnp.int32, (order.shape[0], rows_in), 1)
-    picked = jnp.where(source == lane, 1.0, 0.0).astype(BF16)
-    table_ref[...] = dot(picked, natural_ref[...]).astype(BF16)
-    given = beam_ref[...].astype(F32)
-    given = jnp.concatenate([given[:, 0], given[:, 1]], axis=0).astype(BF16)
-    elements = given.shape[1]
-    columns = weights_ref.shape[1]
-    row = lax.broadcasted_iota(jnp.int32, (elements, columns), 0)
-    column = lax.broadcasted_iota(jnp.int32, (elements, columns), 1)
-    held = column // (2 * GROUP)
-    first = jnp.where(held < elem_dev, me, jnp.bitwise_xor(me, 1)) * elem_dev
-    here = row == first + held % elem_dev
-    total = jnp.zeros(weights_ref.shape, F32)
-    for part in range(2):
-        spread = jnp.where(here & (column % 2 == part), 1.0, 0.0).astype(BF16)
-        total += dot(dot(picks_ref[part], given).astype(BF16), spread)
-    row = lax.broadcasted_iota(jnp.int32, weights_ref.shape, 0)
-    column = lax.broadcasted_iota(jnp.int32, weights_ref.shape, 1)
-    same = row // (weights_ref.shape[0] // GROUP) == column % (2 * GROUP) // 2
-    weights_ref[...] = jnp.where(same, total, 0.0).astype(BF16)
+    step = pl.program_id(0)
+
+    @pl.when(step == 0)
+    def _():
+        me = me_ref[0]
+        order = order_ref[...]
+        source = jnp.bitwise_xor(order[:, 0:1], me // 2) * (2 * bins_chip) + order[:, 1:2]
+        source = lax.rem(source + rows_in, rows_in)
+        lane = lax.broadcasted_iota(jnp.int32, (order.shape[0], rows_in), 1)
+        picked = jnp.where(source == lane, 1.0, 0.0).astype(BF16)
+        table_ref[...] = dot(picked, natural_ref[...]).astype(BF16)
+        given = beam_ref[...].astype(F32)
+        given = jnp.concatenate([given[:, 0], given[:, 1]], axis=0).astype(BF16)
+        elements = given.shape[1]
+        columns = weights_ref.shape[1]
+        row = lax.broadcasted_iota(jnp.int32, (elements, columns), 0)
+        column = lax.broadcasted_iota(jnp.int32, (elements, columns), 1)
+        held = column // (2 * GROUP)
+        first = jnp.where(held < elem_dev, me, jnp.bitwise_xor(me, 1)) * elem_dev
+        here = row == first + held % elem_dev
+        total = jnp.zeros(weights_ref.shape, F32)
+        for part in range(2):
+            spread = jnp.where(here & (column % 2 == part), 1.0, 0.0).astype(BF16)
+            total += dot(dot(picks_ref[part], given).astype(BF16), spread)
+        row = lax.broadcasted_iota(jnp.int32, weights_ref.shape, 0)
+        column = lax.broadcasted_iota(jnp.int32, weights_ref.shape, 1)
+        same = row // (weights_ref.shape[0] // GROUP) == column % (2 * GROUP) // 2
+        weights_ref[...] = jnp.where(same, total, 0.0).astype(BF16)
 
     table = table_ref[...]
-    echoes = [mine_ref[e] for e in range(elem_dev)] + [theirs_ref[e] for e in range(elem_dev)]
-    for e in range(0, 2 * elem_dev, 2):
-        spectra = dot(table, jnp.concatenate(echoes[e : e + 2], axis=1)).astype(BF16)
-        for i in range(2):
-            part = spectra[:, i * width : (i + 1) * width]
-            spectra_ref[:, e + i] = part.reshape(groups, 2 * GROUP, width)
-    weights = weights_ref[...]
-    rows = weights.shape[0]
-    tall = sends[0].shape[0]
-    for pair in range(0, groups, 2):
-        spectra = [spectra_ref[g].reshape(-1, width) for g in (pair, pair + 1)]
-        both = dot(weights, jnp.concatenate(spectra, axis=1))
-        for g in (pair, pair + 1):
-            sums = both[:, (g - pair) * width : (g - pair + 1) * width]
-            if g < groups // 2:
-                keep_ref[g * rows : (g + 1) * rows] = sums
-                continue
-            sums = sums.astype(BF16)
-            for low in range(0, rows, 16):
-                at = (g - groups // 2) * rows + low
-                out_ref = sends[parts - 1 - at // tall]
-                out_ref[at % tall : at % tall + 16] = sums[low : low + 16]
+    for held, echo_ref in ((0, mine_ref), (elem_dev, theirs_ref)):
+        for j in range(0, each, 2):
+            spectra = dot(table, jnp.concatenate([echo_ref[j], echo_ref[j + 1]], axis=1)).astype(BF16)
+            for i in range(2):
+                part = spectra[:, i * width : (i + 1) * width]
+                spectra_ref[:, held + step * each + j + i] = part.reshape(groups, 2 * GROUP, width)
+
+    @pl.when(step == 1)
+    def _():
+        weights = weights_ref[...]
+        rows = weights.shape[0]
+        tall = sends[0].shape[0]
+        for pair in range(0, groups, 2):
+            spectra = [spectra_ref[g].reshape(-1, width) for g in (pair, pair + 1)]
+            both = dot(weights, jnp.concatenate(spectra, axis=1))
+            for g in (pair, pair + 1):
+                sums = both[:, (g - pair) * width : (g - pair + 1) * width]
+                if g < groups // 2:
+                    keep_ref[g * rows : (g + 1) * rows] = sums
+                    continue
+                sums = sums.astype(BF16)
+                for low in range(0, rows, 16):
+                    at = (g - groups // 2) * rows + low
+                    out_ref = sends[parts - 1 - at // tall]
+                    out_ref[at % tall : at % tall + 16] = sums[low : low + 16]
 
 
 def front(me, strides, extra, bins_chip, beam_weights, echo, theirs, span, ahead, parts):
@@ -141,29 +149,36 @@
     block_rows, block_columns = GROUP * 2 * beams, elem_dev * 4 * GROUP
     whole = lambda shape: pl.BlockSpec(shape, lambda i, me: (0,) * len(shape))
 
+    each = elem_dev // 2
+
     def gates(which, start, size):
         lane = lambda me: ((me[0] + which) % 2) * (gate_count // 2) + start
         return pl.BlockSpec(
-            (pl.Element(elem_dev), pl.Element(rows_in), pl.Element(size)),
-            lambda i, me: (0, 0, pl.multiple_of(lane(me), 128)),
+            (pl.Element(each), pl.Element(rows_in), pl.Element(size)),
+            lambda i, me: (i * each, 0, pl.multiple_of(lane(me), 128)),
         )
 
     in_specs = [whole(x.shape) for x in (order, natural, picks, beam_weights)]
-    in_specs += [gates(0, start, size), whole(theirs.shape)]
+    in_specs += [
+        gates(0, start, size),
+        pl.BlockSpec((each, rows_in, size), lambda i, me: (i, 0, 0)),
+    ]
     out_shape = [jax.ShapeDtypeStruct((half // parts, size), BF16)] * parts
     out_shape += [jax.ShapeDtypeStruct((half, size), F32)]
+    out_specs = [whole(x.shape) for x in out_shape]
     operands = [me, jnp.asarray(order), jnp.asarray(natural), jnp.asarray(picks), beam_weights, echo, theirs]
     if ahead:
         in_specs.append(gates(1, *ahead))
         operands.append(echo)
         out_shape.append(jax.ShapeDtypeStruct((elem_dev, rows_in, ahead[1]), BF16))
+        out_specs.append(pl.BlockSpec((each, rows_in, ahead[1]), lambda i, me: (i, 0, 0)))
     return pl.pallas_call(
         functools.partial(front_kernel, bins_chip, ahead is not None, parts),
         grid_spec=pltpu.PrefetchScalarGridSpec(
             num_scalar_prefetch=1,
-            grid=(1,),
+            grid=(2,),
             in_specs=in_specs,
-            out_specs=[whole(x.shape) for x in out_shape],
+            out_specs=out_specs,
             scratch_shapes=[
                 pltpu.VMEM((table_rows, rows_in), BF16),
                 pltpu.VMEM((block_rows, block_columns), BF16),

time: 100 us -> 101 us (1.010)
  transfers between devices with their start and end apart: 28 -> 28, of which waited for: 15 -> 14; matrix products, arithmetic and copies ran while one was open for 0% -> 0% of each run, Pallas kernels for 22% -> 23%
where the time goes in v7:
time: 101 us; the launch traced here: 100 us
  waiting for transfers between devices  40.4 us (40%)
  starting transfers between devices  29.8 us (30%)
  Pallas kernels  29.7 us (29%)
    ppermute x27, waiting for transfers between devices, swap(): return lax.ppermute(x, 'elem', [(i, i ^ stride) for i in range(count)])  36.7 us
    ppermute x27, starting transfers between devices, swap(): return lax.ppermute(x, 'elem', [(i, i ^ stride) for i in range(count)])  28.5 us
    pallas_call x5, Pallas kernels, front(): pl.pallas_call(functools.partial(front_kernel, bins_chip, ahead is not No...  16.8 us
    pallas_call x1, Pallas kernels, tail(): pl.pallas_call(tail_kernel, in_specs=[pl.BlockSpec(memory_space=pltpu.SME...  5.45 us
    pallas_call x3, Pallas kernels, other_half(): pl.pallas_call(slice_kernel, grid_spec=pltpu.PrefetchScalarGridSpec(num_s...  4.31 us
    ppermute x1, waiting for transfers between devices, local(): edge = lax.ppermute(out, 'elem', pairs)  3.77 us
  transfers between devices with their start and end apart: 28, of which 14 were waited for; matrix products, arithmetic and copies ran while one was open for 0% of the time, Pallas kernels for 23%

profile of v7, /device:TPU:0, one launch (start us, length us, event | category | flops | bytes accessed | tf_op | source)
XLA Modules:
  0.0 100.3 jit_solution(17294777082856131081)
XLA Ops:
  0.0 1.5 %slice.3 = bf16[8,256,384]{2,1,0:T(8,128)(2,1)S(1)} custom-call(s32[1]{0:T(128)} %bitcast.me_ref, bf16[8,256,3072]{2,1,0:T(8,128)(2,1)} %bitcast.2), custom_call_target="tpu_custom_call" | custom-call | flops 1000 | bytes 1000 | tf_op jit(solution)/shard_map/slice/pallas_call | solution.py:435
  1.5 0.5 collective-permute-start
  2.0 1.3 %slice.4 = bf16[8,256,256]{2,1,0:T(8,128)(2,1)S(1)} custom-call(s32[1]{0:T(128)} %bitcast.me_ref, bf16[8,256,3072]{2,1,0:T(8,128)(2,1)} %bitcast.3), custom_call_target="tpu_custom_call" | custom-call | flops 1000 | bytes 1000 | tf_op jit(solution)/shard_map/slice/pallas_call | solution.py:435
  3.3 1.6 %slice.5 = bf16[8,256,384]{2,1,0:T(8,128)(2,1)S(1)} custom-call(s32[1]{0:T(128)} %bitcast.me_ref, bf16[8,256,3072]{2,1,0:T(8,128)(2,1)} %bitcast.4), custom_call_target="tpu_custom_call" | custom-call | flops 1000 | bytes 1000 | tf_op jit(solution)/shard_map/slice/pallas_call | solution.py:435
  4.9 0.1 collective-permute-start.1
  5.1 3.6 %front.5 = (bf16[1024,384]{1,0:T(8,128)(2,1)S(1)}, f32[1024,384]{1,0:T(8,128)S(1)}, bf16[8,256,256]{2,1,0:T(8,128)(2,1)S(1)}) custom-call(s32[1]{0:T(128)} %bitcast.me_ref, s32[256,2]{1,0:T(8,128)S(1)} %copy-done.3, bf16[256,256]{1,0:T(8,128)(2,1)S(1)} %copy-done, bf16[2,128,16]{2,1,0:T(8,128)(2,1)S(1)} %copy-done.1, bf16[8,2,128]{2,1,0:T(2,128)(2,1)S(1)} %copy-done.6, ...), custom_call_target="tpu_custom_call" | custom-call | flops 1000 | bytes 1000 | tf_op jit(solution)/shard_map/front/pallas_call | solution.py:175
  8.6 0.5 collective-permute-start.2
  9.2 0.1 collective-permute-start.5
  9.2 2.9 %collective-permute-start.3 = (bf16[1024,384]{1,0:T(8,128)(2,1)S(1)}, bf16[1024,384]{1,0:T(8,128)(2,1)S(1)}, u32[]{:S(2)}, u32[]{:S(2)}) collective-permute-start(bf16[1024,384]{1,0:T(8,128)(2,1)S(1)} %get-tuple-element.60), channel_id=1, source_target_pairs={{0,2},{1,3},{2,0},{3,1},{4,6},{5,7},{6,4},{7,5},{8,10},{9,11},{10,... | collective-permute-start | bytes 2359304 | tf_op jit(solution)/shard_map/ppermute | solution.py:456
  12.2 4.2 %front.6 = (bf16[1024,384]{1,0:T(8,128)(2,1)}, f32[1024,384]{1,0:T(8,128)S(1)}) custom-call(s32[1]{0:T(128)} %bitcast.me_ref, s32[256,2]{1,0:T(8,128)S(1)} %copy-done.3, bf16[256,256]{1,0:T(8,128)(2,1)S(1)} %copy-done, bf16[2,128,16]{2,1,0:T(8,128)(2,1)S(1)} %copy-done.1, bf16[8,2,128]{2,1,0:T(2,128)(2,1)S(1)} %copy-done.6, bf16[8,256,3072]{2,1,0:T(8,128)(2,1)} %bitcast.7, ...), custom_call_target="tpu_custom_call" | custom-call | flops 1000 | bytes 1000 | tf_op jit(solution)/shard_map/front/pallas_call | solution.py:175
  16.4 3.1 %front.7 = (bf16[1024,256]{1,0:T(8,128)(2,1)S(1)}, f32[1024,256]{1,0:T(8,128)S(1)}, bf16[8,256,256]{2,1,0:T(8,128)(2,1)S(1)}) custom-call(s32[1]{0:T(128)} %bitcast.me_ref, s32[256,2]{1,0:T(8,128)S(1)} %copy-done.5, bf16[256,256]{1,0:T(8,128)(2,1)S(1)} %copy-done, bf16[2,128,16]{2,1,0:T(8,128)(2,1)S(1)} %copy-done.1, bf16[8,2,128]{2,1,0:T(2,128)(2,1)S(1)} %copy-done.6, ...), custom_call_target="tpu_custom_call" | custom-call | flops 1000 | bytes 1000 | tf_op jit(solution)/shard_map/front/pallas_call | solution.py:175
  19.5 0.1 collective-permute-start.6
  19.5 1.6 %collective-permute-start.4 = (bf16[1024,256]{1,0:T(8,128)(2,1)S(1)}, bf16[1024,256]{1,0:T(8,128)(2,1)S(1)}, u32[]{:S(2)}, u32[]{:S(2)}) collective-permute-start(bf16[1024,256]{1,0:T(8,128)(2,1)S(1)} %get-tuple-element.68), channel_id=1, source_target_pairs={{0,4},{1,5},{2,6},{3,7},{4,0},{5,1},{6,2},{7,3},{8,12},{9,13},{10,... | collective-permute-start | bytes 1572872 | tf_op jit(solution)/shard_map/ppermute | solution.py:456
  21.2 0.5 collective-permute-start.9
  21.7 8.8 %collective-permute-done.3.refs_0_ = bf16[1024,384]{1,0:T(8,128)(2,1)S(1)} collective-permute-done((bf16[1024,384]{1,0:T(8,128)(2,1)S(1)}, bf16[1024,384]{1,0:T(8,128)(2,1)S(1)}, u32[]{:S(2)}, u32[]{:S(2)}) %collective-permute-start.3) | collective-permute-done | bytes 786464 | tf_op jit(solution)/shard_map/ppermute | solution.py:456
  30.5 0.1 share.10
  30.6 2.2 %collective-permute-start.8 = (bf16[512,384]{1,0:T(8,128)(2,1)S(1)}, bf16[512,384]{1,0:T(8,128)(2,1)S(1)}, u32[]{:S(2)}, u32[]{:S(2)}) collective-permute-start(bf16[512,384]{1,0:T(8,128)(2,1)S(1)} %share.10), channel_id=1, source_target_pairs={{0,4},{1,5},{2,6},{3,7},{4,0},{5,1},{6,2},{7,3},{8,12},{9,13},{10,... | collective-permute-start | bytes 1179656 | tf_op jit(solution)/shard_map/ppermute | solution.py:456
  32.8 1.5 %collective-permute-done.4.refs_0_ = bf16[1024,256]{1,0:T(8,128)(2,1)S(1)} collective-permute-done((bf16[1024,256]{1,0:T(8,128)(2,1)S(1)}, bf16[1024,256]{1,0:T(8,128)(2,1)S(1)}, u32[]{:S(2)}, u32[]{:S(2)}) %collective-permute-start.4) | collective-permute-done | bytes 524320 | tf_op jit(solution)/shard_map/ppermute | solution.py:456
  34.4 2.6 %collective-permute-start.7 = (bf16[512,256]{1,0:T(8,128)(2,1)S(1)}, bf16[512,256]{1,0:T(8,128)(2,1)S(1)}, u32[]{:S(2)}, u32[]{:S(2)}) collective-permute-start(bf16[512,256]{1,0:T(8,128)(2,1)S(1)} %share.11), channel_id=1, source_target_pairs={{0,8},{1,9},{2,10},{3,11},{4,12},{5,13},{6,14},{7,15},{8,0},{9,1},... | collective-permute-start | bytes 786440 | tf_op jit(solution)/shard_map/ppermute | solution.py:456
  37.0 2.9 %front.8 = (bf16[1152,256]{1,0:T(8,128)(2,1)S(1)}, f32[1152,256]{1,0:T(8,128)S(1)}) custom-call(s32[1]{0:T(128)} %bitcast.me_ref, s32[288,2]{1,0:T(8,128)S(1)} %copy-done.2, bf16[256,256]{1,0:T(8,128)(2,1)S(1)} %copy-done, bf16[2,128,16]{2,1,0:T(8,128)(2,1)S(1)} %copy-done.1, bf16[8,2,128]{2,1,0:T(2,128)(2,1)S(1)} %copy-done.6, ...), custom_call_target="tpu_custom_call" | custom-call | flops 1000 | bytes 1000 | tf_op jit(solution)/shard_map/front/pallas_call | solution.py:175
  39.9 0.6 collective-permute-start.11
  40.5 3.1 %front.9 = (bf16[576,256]{1,0:T(8,128)(2,1)S(1)}, bf16[576,256]{1,0:T(8,128)(2,1)S(1)}, f32[1152,256]{1,0:T(8,128)S(1)}) custom-call(s32[1]{0:T(128)} %bitcast.me_ref, s32[288,2]{1,0:T(8,128)S(1)} %copy-done.2, bf16[256,256]{1,0:T(8,128)(2,1)S(1)} %copy-done, bf16[2,128,16]{2,1,0:T(8,128)(2,1)S(1)} %copy-done.1, bf16[8,2,128]{2,1,0:T(2,128)(2,1)S(1)} %copy-done.6, ...), custom_call_target="tpu_custom_call" | custom-call | flops 1000 | bytes 1000 | tf_op jit(solution)/shard_map/front/pallas_call | solution.py:175
  43.6 3.4 %collective-permute-done.7.refs_1_ = bf16[512,256]{1,0:T(8,128)(2,1)S(1)} collective-permute-done((bf16[512,256]{1,0:T(8,128)(2,1)S(1)}, bf16[512,256]{1,0:T(8,128)(2,1)S(1)}, u32[]{:S(2)}, u32[]{:S(2)}) %collective-permute-start.7) | collective-permute-done | bytes 262176 | tf_op jit(solution)/shard_map/ppermute | solution.py:456
  47.1 0.8 collective-permute-done.8.refs_1_
  47.9 0.1 share.13
  48.0 0.1 share.14
  48.1 2.7 %collective-permute-start.10 = (bf16[512,384]{1,0:T(8,128)(2,1)S(1)}, bf16[512,384]{1,0:T(8,128)(2,1)S(1)}, u32[]{:S(2)}, u32[]{:S(2)}) collective-permute-start(bf16[512,384]{1,0:T(8,128)(2,1)S(1)} %share.14), channel_id=1, source_target_pairs={{0,4},{1,5},{2,6},{3,7},{4,0},{5,1},{6,2},{7,3},{8,12},{9,13},{10,... | collective-permute-start | bytes 1179656 | tf_op jit(solution)/shard_map/ppermute | solution.py:456
  50.8 0.5 collective-permute-start.13
  51.3 2.4 %collective-permute-start.12 = (bf16[256,384]{1,0:T(8,128)(2,1)S(1)}, bf16[256,384]{1,0:T(8,128)(2,1)S(1)}, u32[]{:S(2)}, u32[]{:S(2)}) collective-permute-start(bf16[256,384]{1,0:T(8,128)(2,1)S(1)} %share.13), channel_id=1, source_target_pairs={{0,8},{1,9},{2,10},{3,11},{4,12},{5,13},{6,14},{7,15},{8,0},{9,1},... | collective-permute-start | bytes 589832 | tf_op jit(solution)/shard_map/ppermute | solution.py:456
  53.7 1.2 %collective-permute-start.14 = (bf16[256,256]{1,0:T(8,128)(2,1)S(1)}, bf16[256,256]{1,0:T(8,128)(2,1)S(1)}, u32[]{:S(2)}, u32[]{:S(2)}) collective-permute-start(bf16[256,256]{1,0:T(8,128)(2,1)S(1)} %share.12), channel_id=1, source_target_pairs={{0,2},{1,3},{2,0},{3,1},{4,6},{5,7},{6,4},{7,5},{8,10},{9,11},{10,... | collective-permute-start | bytes 393224 | tf_op jit(solution)/shard_map/ppermute | solution.py:456
  54.9 5.1 %collective-permute-done.11.refs_0_ = bf16[1152,256]{1,0:T(8,128)(2,1)S(1)} collective-permute-done((bf16[1152,256]{1,0:T(8,128)(2,1)S(1)}, bf16[1152,256]{1,0:T(8,128)(2,1)S(1)}, u32[]{:S(2)}, u32[]{:S(2)}) %collective-permute-start.11) | collective-permute-done | bytes 589856 | tf_op jit(solution)/shard_map/ppermute | solution.py:456
  60.0 0.1 share.15
  60.1 3.3 %collective-permute-done.10.refs_1_ = bf16[512,384]{1,0:T(8,128)(2,1)S(1)} collective-permute-done((bf16[512,384]{1,0:T(8,128)(2,1)S(1)}, bf16[512,384]{1,0:T(8,128)(2,1)S(1)}, u32[]{:S(2)}, u32[]{:S(2)}) %collective-permute-start.10) | collective-permute-done | bytes 393248 | tf_op jit(solution)/shard_map/ppermute | solution.py:456
  63.4 0.1 share.16
  63.5 0.2 collective-permute-start.15
  63.7 2.5 %collective-permute-start.20 = (bf16[576,256]{1,0:T(8,128)(2,1)S(1)}, bf16[576,256]{1,0:T(8,128)(2,1)S(1)}, u32[]{:S(2)}, u32[]{:S(2)}) collective-permute-start(bf16[576,256]{1,0:T(8,128)(2,1)S(1)} %share.15), channel_id=1, source_target_pairs={{0,4},{1,5},{2,6},{3,7},{4,0},{5,1},{6,2},{7,3},{8,12},{9,13},{10,... | collective-permute-start | bytes 884744 | tf_op jit(solution)/shard_map/ppermute | solution.py:456
  66.2 0.2 finish.5
  66.4 0.1 share.17
  66.4 2.2 %collective-permute-done.14.refs_2_ = bf16[256,256]{1,0:T(8,128)(2,1)S(1)} collective-permute-done((bf16[256,256]{1,0:T(8,128)(2,1)S(1)}, bf16[256,256]{1,0:T(8,128)(2,1)S(1)}, u32[]{:S(2)}, u32[]{:S(2)}) %collective-permute-start.14) | collective-permute-done | bytes 131104 | tf_op jit(solution)/shard_map/ppermute | solution.py:456
  68.6 0.1 finish.6
  68.7 0.1 collective-permute-start.18
  68.8 1.8 %collective-permute-start.21 = (bf16[576,256]{1,0:T(8,128)(2,1)S(1)}, bf16[576,256]{1,0:T(8,128)(2,1)S(1)}, u32[]{:S(2)}, u32[]{:S(2)}) collective-permute-start(bf16[576,256]{1,0:T(8,128)(2,1)S(1)} %get-tuple-element.100), channel_id=1, source_target_pairs={{0,2},{1,3},{2,0},{3,1},{4,6},{5,7},{6,4},{7,5},{8,10},{9,11},{10,... | collective-permute-start | bytes 884744 | tf_op jit(solution)/shard_map/ppermute | solution.py:456
  70.6 0.2 collective-permute-start.17
  70.8 2.3 %collective-permute-done.15.refs_2_ = bf16[256,384]{1,0:T(8,128)(2,1)S(1)} collective-permute-done((bf16[256,384]{1,0:T(8,128)(2,1)S(1)}, bf16[256,384]{1,0:T(8,128)(2,1)S(1)}, u32[]{:S(2)}, u32[]{:S(2)}) %collective-permute-start.15) | collective-permute-done | bytes 196640 | tf_op jit(solution)/shard_map/ppermute | solution.py:456
  73.0 0.2 finish.7
  73.2 0.1 collective-permute-start.16
  73.3 0.1 collective-permute-start.22
  73.4 1.4 %collective-permute-done.16.refs_3_.refs_0_ = f32[144,384]{1,0:T(8,128)S(1)} collective-permute-done((f32[144,384]{1,0:T(8,128)S(1)}, f32[144,384]{1,0:T(8,128)S(1)}, u32[]{:S(2)}, u32[]{:S(2)}) %collective-permute-start.16) | collective-permute-done | bytes 221216 | tf_op jit(solution)/shard_map/ppermute | solution.py:456
  74.7 1.8 %gram.1 = (f32[384,160]{1,0:T(8,128)S(1)}, f32[2,160,1024]{2,1,0:T(8,128)S(1)}) custom-call(s32[1]{0:T(128)} %bitcast.me_ref, s32[8,3072]{1,0:T(8,128)S(1)} %copy-done.4, f32[144,384]{1,0:T(8,128)S(1)} %get-tuple-element.93.refs_0_.refs_3_, f32[144,384]{1,0:T(8,128)S(1)} %get-tuple-element.94.refs_1_.refs_4_, ...), custom_call_target="tpu_custom_call" | custom-call | flops 1000 | bytes 1000 | tf_op jit(solution)/shard_map/gram/pallas_call | solution.py:239
  76.6 0.1 share.18
  76.7 1.7 %collective-permute-start.23 = (bf16[288,256]{1,0:T(8,128)(2,1)S(1)}, bf16[288,256]{1,0:T(8,128)(2,1)S(1)}, u32[]{:S(2)}, u32[]{:S(2)}) collective-permute-start(bf16[288,256]{1,0:T(8,128)(2,1)S(1)} %share.18), channel_id=1, source_target_pairs={{0,8},{1,9},{2,10},{3,11},{4,12},{5,13},{6,14},{7,15},{8,0},{9,1},... | collective-permute-start | bytes 442376 | tf_op jit(solution)/shard_map/ppermute | solution.py:456
  78.4 1.4 %collective-permute-start.24 = (bf16[288,256]{1,0:T(8,128)(2,1)S(1)}, bf16[288,256]{1,0:T(8,128)(2,1)S(1)}, u32[]{:S(2)}, u32[]{:S(2)}) collective-permute-start(bf16[288,256]{1,0:T(8,128)(2,1)S(1)} %get-tuple-element.106), channel_id=1, source_target_pairs={{0,4},{1,5},{2,6},{3,7},{4,0},{5,1},{6,2},{7,3},{8,12},{9,13},{10,... | collective-permute-start | bytes 442376 | tf_op jit(solution)/shard_map/ppermute | solution.py:456
  79.8 1.3 %collective-permute-start.25 = (bf16[288,256]{1,0:T(8,128)(2,1)S(1)}, bf16[288,256]{1,0:T(8,128)(2,1)S(1)}, u32[]{:S(2)}, u32[]{:S(2)}) collective-permute-start(bf16[288,256]{1,0:T(8,128)(2,1)S(1)} %share.19), channel_id=1, source_target_pairs={{0,8},{1,9},{2,10},{3,11},{4,12},{5,13},{6,14},{7,15},{8,0},{9,1},... | collective-permute-start | bytes 442376 | tf_op jit(solution)/shard_map/ppermute | solution.py:456
  81.2 1.4 %collective-permute-start.19 = (f32[16,2048]{1,0:T(8,128)S(1)}, f32[16,2048]{1,0:T(8,128)S(1)}, u32[]{:S(2)}, u32[]{:S(2)}) collective-permute-start(f32[16,2048]{1,0:T(8,128)S(1)} %edges.1), channel_id=1, source_target_pairs={{2,1},{4,3},{6,5},{8,7},{10,9},{12,11},{14,13},{0,15},{1,2},{3,4},... | collective-permute-start | bytes 393224 | tf_op jit(solution)/shard_map/ppermute | solution.py:596
  82.5 5.2 %collective-permute-done.23.refs_2_ = bf16[288,256]{1,0:T(8,128)(2,1)S(1)} collective-permute-done((bf16[288,256]{1,0:T(8,128)(2,1)S(1)}, bf16[288,256]{1,0:T(8,128)(2,1)S(1)}, u32[]{:S(2)}, u32[]{:S(2)}) %collective-permute-start.23) | collective-permute-done | bytes 147488 | tf_op jit(solution)/shard_map/ppermute | solution.py:456
  87.7 0.1 finish.8
  87.8 3.8 %collective-permute-done.19.edge_ref = f32[16,2048]{1,0:T(8,128)S(1)} collective-permute-done((f32[16,2048]{1,0:T(8,128)S(1)}, f32[16,2048]{1,0:T(8,128)S(1)}, u32[]{:S(2)}, u32[]{:S(2)}) %collective-permute-start.19) | collective-permute-done | bytes 131104 | tf_op jit(solution)/shard_map/ppermute | solution.py:596
  91.6 1.4 %collective-permute-done.25.refs_2_ = bf16[288,256]{1,0:T(8,128)(2,1)S(1)} collective-permute-done((bf16[288,256]{1,0:T(8,128)(2,1)S(1)}, bf16[288,256]{1,0:T(8,128)(2,1)S(1)}, u32[]{:S(2)}, u32[]{:S(2)}) %collective-permute-start.25) | collective-permute-done | bytes 147488 | tf_op jit(solution)/shard_map/ppermute | solution.py:456
  93.0 0.1 finish.9
  93.1 0.1 collective-permute-start.27
  93.2 0.5 collective-permute-start.26
  93.7 0.9 collective-permute-done.27.refs_3_
  94.6 0.2 collective-permute-done.26.refs_2_
  94.8 5.4 %tail.1 = f32[8,2,3072]{2,1,0:T(2,128)} custom-call(s32[1]{0:T(128)} %bitcast.me_ref, f32[2,24]{1,0:T(2,128)S(1)} %copy-done.7, f32[384,160]{1,0:T(8,128)S(1)} %get-tuple-element.96.gram_ref, f32[2,160,1024]{2,1,0:T(8,128)S(1)} %get-tuple-element.97.window_ref, f32[16,2048]{1,0:T(8,128)S(1)} %collective-permute-done.19.edge_ref, s32[8,3072]{1,0:T(8,128)S(1)} %copy-done.4, ...), custom_call_target="tpu_custom_call" | custom-call | flops 1000 | bytes 1000 | tf_op jit(solution)/shard_map/tail/pallas_call | solution.py:413
  (34 shorter events, 0.2 us)
Async XLA Ops:
  1.5 3.6 %collective-permute-start = (bf16[8,256,384]{2,1,0:T(8,128)(2,1)S(1)}, bf16[8,256,384]{2,1,0:T(8,128)(2,1)S(1)}, u32[]{:S(2)}, u32[]{:S(2)}) collective-permute-start(bf16[8,256,384]{2,1,0:T(8,128)(2,1)S(1)} %slice.3), channel_id=1, source_target_pairs={{0,1},{1,0},{2,3},{3,2},{4,5},{5,4},{6,7},{7,6},{8,9},{9,8},{10,11... | collective-permute-start | bytes 4718600 | tf_op jit(solution)/shard_map/ppermute | solution.py:456
  3.3 1.8 %copy-start = (bf16[256,256]{1,0:T(8,128)(2,1)S(1)}, bf16[256,256]{1,0:T(8,128)(2,1)}, u32[]{:S(2)}) copy-start(bf16[256,256]{1,0:T(8,128)(2,1)} %constant.15.clone.natural_ref) | copy-start | bytes 393220
  3.3 1.8 %copy-start.1 = (bf16[2,128,16]{2,1,0:T(8,128)(2,1)S(1)}, bf16[2,128,16]{2,1,0:T(8,128)(2,1)}, u32[]{:S(2)}) copy-start(bf16[2,128,16]{2,1,0:T(8,128)(2,1)} %constant.16.clone.picks_ref) | copy-start | bytes 24580
  3.3 1.7 %copy-start.3 = (s32[256,2]{1,0:T(8,128)S(1)}, s32[256,2]{1,0:T(8,128)}, u32[]{:S(2)}) copy-start(s32[256,2]{1,0:T(8,128)} %constant.14.clone.order_ref) | copy-start | bytes 6148
  3.3 1.7 %copy-start.6 = (bf16[8,2,128]{2,1,0:T(2,128)(2,1)S(1)}, bf16[8,2,128]{2,1,0:T(2,128)(2,1)}, u32[]{:S(2)}) copy-start(bf16[8,2,128]{2,1,0:T(2,128)(2,1)} %beam_ref.9) | copy-start | bytes 12292
  4.9 7.3 %collective-permute-start.1 = (bf16[8,256,384]{2,1,0:T(8,128)(2,1)S(1)}, bf16[8,256,384]{2,1,0:T(8,128)(2,1)S(1)}, u32[]{:S(2)}, u32[]{:S(2)}) collective-permute-start(bf16[8,256,384]{2,1,0:T(8,128)(2,1)S(1)} %slice.5), channel_id=1, source_target_pairs={{0,1},{1,0},{2,3},{3,2},{4,5},{5,4},{6,7},{7,6},{8,9},{9,8},{10,11... | collective-permute-start | bytes 4718600 | tf_op jit(solution)/shard_map/ppermute | solution.py:456
  8.6 7.7 %collective-permute-start.2 = (bf16[8,256,256]{2,1,0:T(8,128)(2,1)S(1)}, bf16[8,256,256]{2,1,0:T(8,128)(2,1)S(1)}, u32[]{:S(2)}, u32[]{:S(2)}) collective-permute-start(bf16[8,256,256]{2,1,0:T(8,128)(2,1)S(1)} %get-tuple-element.65), channel_id=1, source_target_pairs={{0,1},{1,0},{2,3},{3,2},{4,5},{5,4},{6,7},{7,6},{8,9},{9,8},{10,11... | collective-permute-start | bytes 3145736 | tf_op jit(solution)/shard_map/ppermute | solution.py:456
  9.2 27.9 %collective-permute-start.5 = (bf16[8,256,256]{2,1,0:T(8,128)(2,1)S(1)}, bf16[8,256,256]{2,1,0:T(8,128)(2,1)S(1)}, u32[]{:S(2)}, u32[]{:S(2)}) collective-permute-start(bf16[8,256,256]{2,1,0:T(8,128)(2,1)S(1)} %slice.4), channel_id=1, source_target_pairs={{0,1},{1,0},{2,3},{3,2},{4,5},{5,4},{6,7},{7,6},{8,9},{9,8},{10,11... | collective-permute-start | bytes 3145736 | tf_op jit(solution)/shard_map/ppermute | solution.py:456
  9.2 7.1 %copy-start.5 = (s32[256,2]{1,0:T(8,128)S(1)}, s32[256,2]{1,0:T(8,128)}, u32[]{:S(2)}) copy-start(s32[256,2]{1,0:T(8,128)} %constant.17.clone.order_ref) | copy-start | bytes 6148
  9.2 21.3 %collective-permute-start.3 = (bf16[1024,384]{1,0:T(8,128)(2,1)S(1)}, bf16[1024,384]{1,0:T(8,128)(2,1)S(1)}, u32[]{:S(2)}, u32[]{:S(2)}) collective-permute-start(bf16[1024,384]{1,0:T(8,128)(2,1)S(1)} %get-tuple-element.60), channel_id=1, source_target_pairs={{0,2},{1,3},{2,0},{3,1},{4,6},{5,7},{6,4},{7,5},{8,10},{9,11},{10,... | collective-permute-start | bytes 2359304 | tf_op jit(solution)/shard_map/ppermute | solution.py:456
  19.5 21.1 %collective-permute-start.6 = (bf16[8,256,256]{2,1,0:T(8,128)(2,1)S(1)}, bf16[8,256,256]{2,1,0:T(8,128)(2,1)S(1)}, u32[]{:S(2)}, u32[]{:S(2)}) collective-permute-start(bf16[8,256,256]{2,1,0:T(8,128)(2,1)S(1)} %get-tuple-element.74), channel_id=1, source_target_pairs={{0,1},{1,0},{2,3},{3,2},{4,5},{5,4},{6,7},{7,6},{8,9},{9,8},{10,11... | collective-permute-start | bytes 3145736 | tf_op jit(solution)/shard_map/ppermute | solution.py:456
  19.5 14.8 %collective-permute-start.4 = (bf16[1024,256]{1,0:T(8,128)(2,1)S(1)}, bf16[1024,256]{1,0:T(8,128)(2,1)S(1)}, u32[]{:S(2)}, u32[]{:S(2)}) collective-permute-start(bf16[1024,256]{1,0:T(8,128)(2,1)S(1)} %get-tuple-element.68), channel_id=1, source_target_pairs={{0,4},{1,5},{2,6},{3,7},{4,0},{5,1},{6,2},{7,3},{8,12},{9,13},{10,... | collective-permute-start | bytes 1572872 | tf_op jit(solution)/shard_map/ppermute | solution.py:456
  21.2 26.8 %collective-permute-start.9 = (bf16[1024,384]{1,0:T(8,128)(2,1)}, bf16[1024,384]{1,0:T(8,128)(2,1)S(1)}, u32[]{:S(2)}, u32[]{:S(2)}) collective-permute-start(bf16[1024,384]{1,0:T(8,128)(2,1)} %get-tuple-element.63), channel_id=1, source_target_pairs={{0,2},{1,3},{2,0},{3,1},{4,6},{5,7},{6,4},{7,5},{8,10},{9,11},{10,... | collective-permute-start | bytes 2359304 | tf_op jit(solution)/shard_map/ppermute | solution.py:456
  30.6 6.4 %copy-start.2 = (s32[288,2]{1,0:T(8,128)S(1)}, s32[288,2]{1,0:T(8,128)}, u32[]{:S(2)}) copy-start(s32[288,2]{1,0:T(8,128)} %constant.18.clone.order_ref) | copy-start | bytes 6916
  30.6 17.3 %collective-permute-start.8 = (bf16[512,384]{1,0:T(8,128)(2,1)S(1)}, bf16[512,384]{1,0:T(8,128)(2,1)S(1)}, u32[]{:S(2)}, u32[]{:S(2)}) collective-permute-start(bf16[512,384]{1,0:T(8,128)(2,1)S(1)} %share.10), channel_id=1, source_target_pairs={{0,4},{1,5},{2,6},{3,7},{4,0},{5,1},{6,2},{7,3},{8,12},{9,13},{10,... | collective-permute-start | bytes 1179656 | tf_op jit(solution)/shard_map/ppermute | solution.py:456
  34.4 12.7 %collective-permute-start.7 = (bf16[512,256]{1,0:T(8,128)(2,1)S(1)}, bf16[512,256]{1,0:T(8,128)(2,1)S(1)}, u32[]{:S(2)}, u32[]{:S(2)}) collective-permute-start(bf16[512,256]{1,0:T(8,128)(2,1)S(1)} %share.11), channel_id=1, source_target_pairs={{0,8},{1,9},{2,10},{3,11},{4,12},{5,13},{6,14},{7,15},{8,0},{9,1},... | collective-permute-start | bytes 786440 | tf_op jit(solution)/shard_map/ppermute | solution.py:456
  39.9 20.1 %collective-permute-start.11 = (bf16[1152,256]{1,0:T(8,128)(2,1)S(1)}, bf16[1152,256]{1,0:T(8,128)(2,1)S(1)}, u32[]{:S(2)}, u32[]{:S(2)}) collective-permute-start(bf16[1152,256]{1,0:T(8,128)(2,1)S(1)} %get-tuple-element.72), channel_id=1, source_target_pairs={{0,2},{1,3},{2,0},{3,1},{4,6},{5,7},{6,4},{7,5},{8,10},{9,11},{10,... | collective-permute-start | bytes 1769480 | tf_op jit(solution)/shard_map/ppermute | solution.py:456
  48.1 15.3 %collective-permute-start.10 = (bf16[512,384]{1,0:T(8,128)(2,1)S(1)}, bf16[512,384]{1,0:T(8,128)(2,1)S(1)}, u32[]{:S(2)}, u32[]{:S(2)}) collective-permute-start(bf16[512,384]{1,0:T(8,128)(2,1)S(1)} %share.14), channel_id=1, source_target_pairs={{0,4},{1,5},{2,6},{3,7},{4,0},{5,1},{6,2},{7,3},{8,12},{9,13},{10,... | collective-permute-start | bytes 1179656 | tf_op jit(solution)/shard_map/ppermute | solution.py:456
  50.8 15.6 %collective-permute-start.13 = (bf16[576,256]{1,0:T(8,128)(2,1)S(1)}, bf16[576,256]{1,0:T(8,128)(2,1)S(1)}, u32[]{:S(2)}, u32[]{:S(2)}) collective-permute-start(bf16[576,256]{1,0:T(8,128)(2,1)S(1)} %get-tuple-element.76), channel_id=1, source_target_pairs={{0,2},{1,3},{2,0},{3,1},{4,6},{5,7},{6,4},{7,5},{8,10},{9,11},{10,... | collective-permute-start | bytes 884744 | tf_op jit(solution)/shard_map/ppermute | solution.py:456
  51.3 14.9 %collective-permute-start.12 = (bf16[256,384]{1,0:T(8,128)(2,1)S(1)}, bf16[256,384]{1,0:T(8,128)(2,1)S(1)}, u32[]{:S(2)}, u32[]{:S(2)}) collective-permute-start(bf16[256,384]{1,0:T(8,128)(2,1)S(1)} %share.13), channel_id=1, source_target_pairs={{0,8},{1,9},{2,10},{3,11},{4,12},{5,13},{6,14},{7,15},{8,0},{9,1},... | collective-permute-start | bytes 589832 | tf_op jit(solution)/shard_map/ppermute | solution.py:456
  53.7 14.8 %collective-permute-start.14 = (bf16[256,256]{1,0:T(8,128)(2,1)S(1)}, bf16[256,256]{1,0:T(8,128)(2,1)S(1)}, u32[]{:S(2)}, u32[]{:S(2)}) collective-permute-start(bf16[256,256]{1,0:T(8,128)(2,1)S(1)} %share.12), channel_id=1, source_target_pairs={{0,2},{1,3},{2,0},{3,1},{4,6},{5,7},{6,4},{7,5},{8,10},{9,11},{10,... | collective-permute-start | bytes 393224 | tf_op jit(solution)/shard_map/ppermute | solution.py:456
  63.5 9.5 %collective-permute-start.15 = (bf16[256,384]{1,0:T(8,128)(2,1)S(1)}, bf16[256,384]{1,0:T(8,128)(2,1)S(1)}, u32[]{:S(2)}, u32[]{:S(2)}) collective-permute-start(bf16[256,384]{1,0:T(8,128)(2,1)S(1)} %share.16), channel_id=1, source_target_pairs={{0,8},{1,9},{2,10},{3,11},{4,12},{5,13},{6,14},{7,15},{8,0},{9,1},... | collective-permute-start | bytes 589832 | tf_op jit(solution)/shard_map/ppermute | solution.py:456
  63.7 12.9 %collective-permute-start.20 = (bf16[576,256]{1,0:T(8,128)(2,1)S(1)}, bf16[576,256]{1,0:T(8,128)(2,1)S(1)}, u32[]{:S(2)}, u32[]{:S(2)}) collective-permute-start(bf16[576,256]{1,0:T(8,128)(2,1)S(1)} %share.15), channel_id=1, source_target_pairs={{0,4},{1,5},{2,6},{3,7},{4,0},{5,1},{6,2},{7,3},{8,12},{9,13},{10,... | collective-permute-start | bytes 884744 | tf_op jit(solution)/shard_map/ppermute | solution.py:456
  68.7 6.0 %copy-start.4 = (s32[8,3072]{1,0:T(8,128)S(1)}, s32[8,3072]{1,0:T(8,128)}, u32[]{:S(2)}) copy-start(s32[8,3072]{1,0:T(8,128)} %mask_ref.2) | copy-start | bytes 294916
  68.7 4.6 %collective-permute-start.18 = (f32[144,256]{1,0:T(8,128)S(1)}, f32[144,256]{1,0:T(8,128)S(1)}, u32[]{:S(2)}, u32[]{:S(2)}) collective-permute-start(f32[144,256]{1,0:T(8,128)S(1)} %get-tuple-element.89), channel_id=1, source_target_pairs={{0,1},{1,0},{2,3},{3,2},{4,5},{5,4},{6,7},{7,6},{8,9},{9,8},{10,11... | collective-permute-start | bytes 442376 | tf_op jit(solution)/shard_map/ppermute | solution.py:456
  68.8 11.0 %collective-permute-start.21 = (bf16[576,256]{1,0:T(8,128)(2,1)S(1)}, bf16[576,256]{1,0:T(8,128)(2,1)S(1)}, u32[]{:S(2)}, u32[]{:S(2)}) collective-permute-start(bf16[576,256]{1,0:T(8,128)(2,1)S(1)} %get-tuple-element.100), channel_id=1, source_target_pairs={{0,2},{1,3},{2,0},{3,1},{4,6},{5,7},{6,4},{7,5},{8,10},{9,11},{10,... | collective-permute-start | bytes 884744 | tf_op jit(solution)/shard_map/ppermute | solution.py:456
  70.6 2.8 %collective-permute-start.17 = (f32[144,384]{1,0:T(8,128)S(1)}, f32[144,384]{1,0:T(8,128)S(1)}, u32[]{:S(2)}, u32[]{:S(2)}) collective-permute-start(f32[144,384]{1,0:T(8,128)S(1)} %get-tuple-element.85), channel_id=1, source_target_pairs={{0,1},{1,0},{2,3},{3,2},{4,5},{5,4},{6,7},{7,6},{8,9},{9,8},{10,11... | collective-permute-start | bytes 663560 | tf_op jit(solution)/shard_map/ppermute | solution.py:456
  73.2 1.5 %collective-permute-start.16 = (f32[144,384]{1,0:T(8,128)S(1)}, f32[144,384]{1,0:T(8,128)S(1)}, u32[]{:S(2)}, u32[]{:S(2)}) collective-permute-start(f32[144,384]{1,0:T(8,128)S(1)} %get-tuple-element.91), channel_id=1, source_target_pairs={{0,1},{1,0},{2,3},{3,2},{4,5},{5,4},{6,7},{7,6},{8,9},{9,8},{10,11... | collective-permute-start | bytes 663560 | tf_op jit(solution)/shard_map/ppermute | solution.py:456
  73.3 6.5 %collective-permute-start.22 = (bf16[288,256]{1,0:T(8,128)(2,1)S(1)}, bf16[288,256]{1,0:T(8,128)(2,1)S(1)}, u32[]{:S(2)}, u32[]{:S(2)}) collective-permute-start(bf16[288,256]{1,0:T(8,128)(2,1)S(1)} %get-tuple-element.87), channel_id=1, source_target_pairs={{0,4},{1,5},{2,6},{3,7},{4,0},{5,1},{6,2},{7,3},{8,12},{9,13},{10,... | collective-permute-start | bytes 442376 | tf_op jit(solution)/shard_map/ppermute | solution.py:456
  76.7 11.1 %collective-permute-start.23 = (bf16[288,256]{1,0:T(8,128)(2,1)S(1)}, bf16[288,256]{1,0:T(8,128)(2,1)S(1)}, u32[]{:S(2)}, u32[]{:S(2)}) collective-permute-start(bf16[288,256]{1,0:T(8,128)(2,1)S(1)} %share.18), channel_id=1, source_target_pairs={{0,8},{1,9},{2,10},{3,11},{4,12},{5,13},{6,14},{7,15},{8,0},{9,1},... | collective-permute-start | bytes 442376 | tf_op jit(solution)/shard_map/ppermute | solution.py:456
  78.4 13.2 %collective-permute-start.24 = (bf16[288,256]{1,0:T(8,128)(2,1)S(1)}, bf16[288,256]{1,0:T(8,128)(2,1)S(1)}, u32[]{:S(2)}, u32[]{:S(2)}) collective-permute-start(bf16[288,256]{1,0:T(8,128)(2,1)S(1)} %get-tuple-element.106), channel_id=1, source_target_pairs={{0,4},{1,5},{2,6},{3,7},{4,0},{5,1},{6,2},{7,3},{8,12},{9,13},{10,... | collective-permute-start | bytes 442376 | tf_op jit(solution)/shard_map/ppermute | solution.py:456
  79.8 13.2 %collective-permute-start.25 = (bf16[288,256]{1,0:T(8,128)(2,1)S(1)}, bf16[288,256]{1,0:T(8,128)(2,1)S(1)}, u32[]{:S(2)}, u32[]{:S(2)}) collective-permute-start(bf16[288,256]{1,0:T(8,128)(2,1)S(1)} %share.19), channel_id=1, source_target_pairs={{0,8},{1,9},{2,10},{3,11},{4,12},{5,13},{6,14},{7,15},{8,0},{9,1},... | collective-permute-start | bytes 442376 | tf_op jit(solution)/shard_map/ppermute | solution.py:456
  81.2 13.7 %copy-start.7 = (f32[2,24]{1,0:T(2,128)S(1)}, f32[2,24]{1,0:T(2,128)}, u32[]{:S(2)}) copy-start(f32[2,24]{1,0:T(2,128)} %steer_ref.1) | copy-start | bytes 580
  81.2 10.4 %collective-permute-start.19 = (f32[16,2048]{1,0:T(8,128)S(1)}, f32[16,2048]{1,0:T(8,128)S(1)}, u32[]{:S(2)}, u32[]{:S(2)}) collective-permute-start(f32[16,2048]{1,0:T(8,128)S(1)} %edges.1), channel_id=1, source_target_pairs={{2,1},{4,3},{6,5},{8,7},{10,9},{12,11},{14,13},{0,15},{1,2},{3,4},... | collective-permute-start | bytes 393224 | tf_op jit(solution)/shard_map/ppermute | solution.py:596
  93.1 1.5 %collective-permute-start.27 = (f32[160,256]{1,0:T(8,128)S(1)}, f32[160,256]{1,0:T(8,128)S(1)}, u32[]{:S(2)}, u32[]{:S(2)}) collective-permute-start(f32[160,256]{1,0:T(8,128)S(1)} %get-tuple-element.108), channel_id=1, source_target_pairs={{0,1},{1,0},{2,3},{3,2},{4,5},{5,4},{6,7},{7,6},{8,9},{9,8},{10,11... | collective-permute-start | bytes 491528 | tf_op jit(solution)/shard_map/ppermute | solution.py:456
  93.2 1.6 %collective-permute-start.26 = (f32[160,256]{1,0:T(8,128)S(1)}, f32[160,256]{1,0:T(8,128)S(1)}, u32[]{:S(2)}, u32[]{:S(2)}) collective-permute-start(f32[160,256]{1,0:T(8,128)S(1)} %get-tuple-element.102), channel_id=1, source_target_pairs={{0,1},{1,0},{2,3},{3,2},{4,5},{5,4},{6,7},{7,6},{8,9},{9,8},{10,11... | collective-permute-start | bytes 491528 | tf_op jit(solution)/shard_map/ppermute | solution.py:456
